TPU v7x, 128 devices: a whole 4x4x4 slice. The times are simulated.
128 devices in a mesh: ty: 16 (over z, y), tx: 8 (over x, core).
Axes of the slice: x: 4, y: 4, z: 4, core: 2. Of those that a mesh axis runs over, the one named last changes fastest.
Arguments:
- specimen: float32 [2, 8192, 8192], P(None, 'ty', 'tx'), may hold values from -4 to 4
- probe: float32 [2, 4, 256, 256], replicated, may hold values from -4 to 4
- amplitude: float32 [1536, 256, 256], P(('ty', 'tx')), may hold values from 0.4 to 3
- offsets: int32 [1536, 2], P(('ty', 'tx')), may hold values from 0 to 7936, as said below
Outputs:
- object_grad: float32 [2, 8192, 8192], P(None, 'ty', 'tx')
- probe_grad: float32 [2, 4, 256, 256], replicated
Inputs may be any that keep to these rules, and one draw needn't show every extreme that they name: Row offsets are at most 7936 and column offsets at most 7936. A position's column offset lies in the tile column of the device that holds it (offset // 1024 equals that device's index along tx). Of the positions that one device holds, exactly 2 or none have their row offset in any one tile row (offset // 512); some tile rows are chosen by many devices.
All inputs are finite; a program needn't handle non-finite values.
Results may differ from a plain program's by a relative error of at most 0.007.
The roundings to bfloat16 on the way count: a program that leaves them out, or rounds other values in their place, can miss the bound.
Values may be sent and summed in bfloat16 or wider, within the bound.
A program may use at most 192 MiB of HBM per device.

v0:
```python
import math

import jax
import jax.numpy as jnp
from jax import lax
from jax.sharding import PartitionSpec as P

MOST = 2


def from_behind(value, axis, steps):
    count = lax.axis_size(axis)
    leading, last = (max(0, -steps), min(count, count - steps))
    return lax.ppermute(value, axis, [(source, source + steps) for source in range(leading, last)])


def make_tables(size):
    index = jnp.arange(size, dtype=jnp.int32)
    phase = index[:, None] * index[None, :] % size
    angle = phase.astype(jnp.float32) * (2.0 * math.pi / size)
    factor = 1.0 / math.sqrt(size)
    return (
        (jnp.cos(angle) * factor).astype(jnp.bfloat16),
        (-jnp.sin(angle) * factor).astype(jnp.bfloat16),
    )


def right_product(left_re, left_im, table_re, table_im):
    out_re = jnp.einsum(
        "msk,kn->msn", left_re, table_re, preferred_element_type=jnp.float32
    ) - jnp.einsum("msk,kn->msn", left_im, table_im, preferred_element_type=jnp.float32)
    out_im = jnp.einsum(
        "msk,kn->msn", left_re, table_im, preferred_element_type=jnp.float32
    ) + jnp.einsum("msk,kn->msn", left_im, table_re, preferred_element_type=jnp.float32)
    return (out_re, out_im)


def left_product(table_re, table_im, right_re, right_im):
    out_re = jnp.einsum(
        "sk,mkn->msn", table_re, right_re, preferred_element_type=jnp.float32
    ) - jnp.einsum("sk,mkn->msn", table_im, right_im, preferred_element_type=jnp.float32)
    out_im = jnp.einsum(
        "sk,mkn->msn", table_re, right_im, preferred_element_type=jnp.float32
    ) + jnp.einsum("sk,mkn->msn", table_im, right_re, preferred_element_type=jnp.float32)
    return (out_re, out_im)


def position_terms(patch, measured, probe, four_re, four_im):
    patch_re = patch[0].astype(jnp.float32)
    patch_im = patch[1].astype(jnp.float32)
    probe_re = probe[0]
    probe_im = probe[1]
    exit_re = (probe_re * patch_re - probe_im * patch_im).astype(jnp.bfloat16)
    exit_im = (probe_re * patch_im + probe_im * patch_re).astype(jnp.bfloat16)
    half_re, half_im = right_product(exit_re, exit_im, four_re, four_im)
    far_re, far_im = left_product(
        four_re, four_im, half_re.astype(jnp.bfloat16), half_im.astype(jnp.bfloat16)
    )
    intensity = jnp.sum(far_re * far_re + far_im * far_im, axis=0)
    factor = 1.0 - measured / jnp.sqrt(jnp.maximum(intensity, 0.25))
    resid_re = (far_re * factor).astype(jnp.bfloat16)
    resid_im = (far_im * factor).astype(jnp.bfloat16)
    conj_im = -four_im
    back_re, back_im = right_product(resid_re, resid_im, four_re, conj_im)
    back_re, back_im = left_product(
        four_re, conj_im, back_re.astype(jnp.bfloat16), back_im.astype(jnp.bfloat16)
    )
    grad_re = jnp.sum(probe_re * back_re + probe_im * back_im, axis=0)
    grad_im = jnp.sum(probe_re * back_im - probe_im * back_re, axis=0)
    grad = jnp.stack([grad_re, grad_im]).astype(jnp.bfloat16)
    term = jnp.stack(
        [patch_re * back_re + patch_im * back_im, patch_re * back_im - patch_im * back_re]
    )
    return (grad, term)


def plan_slots(offsets, tile_rows, column_base, rows_ty):
    row_pos = offsets[:, 0]
    col_pos = offsets[:, 1]
    tile_index = row_pos // tile_rows
    order = jnp.arange(offsets.shape[0], dtype=jnp.int32)
    earlier = (tile_index[:, None] == tile_index[None, :]) & (order[None, :] < order[:, None])
    rank = jnp.sum(earlier.astype(jnp.int32), axis=1)
    slots = tile_index * MOST + rank
    local = jnp.stack([row_pos - tile_index * tile_rows, col_pos - column_base], axis=1)
    wanted = jnp.full((rows_ty * MOST, 2), -1, jnp.int32).at[slots].set(local)
    return (slots, wanted.reshape(rows_ty, MOST, 2))


def cut_patches(extended, incoming, size):
    places = jnp.maximum(incoming.reshape(-1, 2), 0)

    def cut_one(place):
        return lax.dynamic_slice(extended, (0, place[0], place[1]), (2, size, size))

    pieces = jax.vmap(cut_one)(places)
    return pieces.reshape(incoming.shape[0], incoming.shape[1], 2, size, size)


def run_positions(returned, slots, amplitude, probe, four_re, four_im):
    size = probe.shape[-1]
    flat = returned.reshape(-1, 2, size, size)
    patches = flat[slots]

    def advance(total, item):
        patch, measured = item
        grad, term = position_terms(patch, measured, probe, four_re, four_im)
        return (total + term, grad)

    total = jnp.zeros(probe.shape, jnp.float32)
    total, grads = lax.scan(advance, total, (patches, amplitude))
    outgoing = jnp.zeros((flat.shape[0], 2, size, size), jnp.bfloat16).at[slots].set(grads)
    return (outgoing.reshape(returned.shape), total)


def deposit(grid, incoming, arrived, size):
    places = jnp.maximum(incoming.reshape(-1, 2), 0)
    pieces = arrived.reshape(-1, 2, size, size)

    def add_one(index, field):
        place = places[index]
        start = (0, place[0], place[1])
        current = lax.dynamic_slice(field, start, (2, size, size))
        return lax.dynamic_update_slice(field, current + pieces[index].astype(jnp.float32), start)

    return lax.fori_loop(0, places.shape[0], add_one, grid)


def on_device(specimen, probe, amplitude, offsets):
    size = probe.shape[-1]
    tile_rows = specimen.shape[1]
    tile_cols = specimen.shape[2]
    rows_ty = lax.axis_size("ty")
    half_object = specimen.astype(jnp.bfloat16)
    right = from_behind(half_object[:, :, :size], "tx", -1)
    widened = jnp.concatenate([half_object, right], axis=2)
    lower = from_behind(widened[:, :size, :], "ty", -1)
    extended = jnp.concatenate([widened, lower], axis=1)
    four_re, four_im = make_tables(size)
    column_base = lax.axis_index("tx") * tile_cols
    grid = jnp.zeros((2, tile_rows + size, tile_cols + size), jnp.float32)
    slots, wanted = plan_slots(offsets, tile_rows, column_base, rows_ty)
    incoming = lax.all_to_all(wanted, "ty", split_axis=0, concat_axis=0, tiled=True)
    returned = lax.all_to_all(
        cut_patches(extended, incoming, size), "ty", split_axis=0, concat_axis=0, tiled=True
    )
    outgoing, batch_total = run_positions(returned, slots, amplitude, probe, four_re, four_im)
    arrived = lax.all_to_all(outgoing, "ty", split_axis=0, concat_axis=0, tiled=True)
    grid = deposit(grid, incoming, arrived, size)
    moved_down = from_behind(grid[:, tile_rows:, :], "ty", 1)
    grid = grid[:, :tile_rows, :].at[:, :size, :].add(moved_down)
    moved_right = from_behind(grid[:, :, tile_cols:], "tx", 1)
    object_grad = grid[:, :, :tile_cols].at[:, :, :size].add(moved_right)
    scale_root = (
        math.sqrt(offsets.shape[0] * lax.axis_size("ty") * lax.axis_size("tx")) / probe.shape[1]
    )
    probe_grad = lax.psum(batch_total, ("ty", "tx")) / scale_root
    return (object_grad, probe_grad)


def solution(mesh):
    in_specs = (P(None, "ty", "tx"), P(), P(("ty", "tx"), None, None), P(("ty", "tx"), None))
    out_specs = (P(None, "ty", "tx"), P())
    return jax.shard_map(
        on_device, mesh=mesh, in_specs=in_specs, out_specs=out_specs, check_vma=False
    )
```

profile of v0, /device:TPU:1, one launch (start us, length us, event | category | flops | bytes accessed | tf_op | source)
XLA Modules:
  0.0 1411.6 jit_solution(8462509010204656287)
XLA Ops:
  13.1 8.4 collective-permute-done
  25.7 9.3 all-to-all-start
  35.1 17.8 %all-to-all-done = s32[16,2,2]{1,2,0:T(2,128)S(1)} async-done(((s32[16,2,2]{1,2,0:T(2,128)}), s32[16,2,2]{1,2,0:T(2,128)S(1)}, u32[]{:S(2)}, u32[]{:S(2)}) %all-to-all-start) | async-done | bytes 288 | tf_op jit(solution)/shard_map/all_to_all | solution.py:143
  60.6 122.0 %while.32 = (s32[]{:T(128)}, bf16[2,768,1280]{2,1,0:T(8,128)(2,1)}, s32[32,3]{0,1:T(4,128)S(1)}, bf16[32,2,256,256]{3,2,1,0:T(8,128)(2,1)}, s32[]{:T(128)}) while((s32[]{:T(128)}, bf16[2,768,1280]{2,1,0:T(8,128)(2,1)}, s32[32,3]{0,1:T(4,128)S(1)}, bf16[32,2,256,256]{3,2,1,0:T(8,128)(2,1)}, s32[]{:T(128)}) %tuple.108), condition=%wide.while_cond.2, body=%wide.while_body.2.sunk | while | flops 2 | bytes 525929 | solution.py:94
  182.6 6.3 all-to-all-start.1
  190.8 114.8 %all-to-all-done.1 = bf16[16,2,2,256,256]{4,3,2,1,0:T(8,128)(2,1)} async-done(((bf16[16,2,2,256,256]{4,3,2,1,0:T(8,128)(2,1)}), bf16[16,2,2,256,256]{4,3,2,1,0:T(8,128)(2,1)}, u32[]{:S(2)}, u32[]{:S(2)}) %all-to-all-start.1) | async-done | bytes 8388640 | tf_op jit(solution)/shard_map/all_to_all | solution.py:144
  305.6 6.0 gather_fusion
  311.6 370.6 %while.33 = (s32[]{:T(128)}, f32[2,4,256,256]{2,3,1,0:T(8,128)}, bf16[12,2,256,256]{3,2,1,0:T(8,128)(2,1)}, bf16[12,2,256,256]{3,2,1,0:T(8,128)(2,1)}, f32[2,4,2...) while((s32[]{:T(128)}, f32[2,4,256,256]{2,3,1,0:T(8,128)}, ...), condition=%wide.region_6.7_spmd.clone.clone, body=%wide.region_2.6_spmd.clone.clone.sunk | while | flops 2179465216 | bytes 74973928 | solution.py:111
  686.4 8.3 scatter_fusion
  700.3 120.2 %all-to-all-done.2 = bf16[16,2,2,256,256]{4,3,2,1,0:T(8,128)(2,1)} async-done(((bf16[16,2,2,256,256]{4,3,2,1,0:T(8,128)(2,1)}), bf16[16,2,2,256,256]{4,3,2,1,0:T(8,128)(2,1)}, u32[]{:S(2)}, u32[]{:S(2)}) %all-to-all-start.2) | async-done | bytes 8388640 | tf_op jit(solution)/shard_map/all_to_all | solution.py:148
  824.1 376.0 %while.31 = (s32[]{:T(128)}, f32[2,768,1280]{2,1,0:T(8,128)}, s32[32,2]{0,1:T(2,128)S(1)}, bf16[32,2,256,256]{3,2,1,0:T(8,128)(2,1)}, s32[]{:T(128)}, /*index=5*/s32[]{:T(128)}, s32[]{:T(128)}, s32[]{:T(128)}) while((s32[]{:T(128)}, f32[2,768,1280]{2,1,0:T(8,128)}, s32[32,2]{0,1:T(2,128)S(1)}, bf16[32,2,256,256]{3,2,1,0:T(8,128)(2,1)}, ...), condition=%wide.region_9.10_spmd, body=%wide.region_8.9_spmd.sunk | while | flops 262152 | bytes 2359501 | solution.py:126
  829.9 5.9 dynamic_update_slice.17
  841.7 5.9 dynamic_update_slice.17
  865.2 5.9 dynamic_update_slice.17
  876.9 5.9 dynamic_update_slice.17
  900.4 5.9 dynamic_update_slice.17
  912.2 5.9 dynamic_update_slice.17
  935.7 5.9 dynamic_update_slice.17
  959.2 5.9 dynamic_update_slice.17
  970.9 5.9 dynamic_update_slice.17
  994.4 5.9 dynamic_update_slice.17
  1211.2 50.1 %collective-permute-done.2 = f32[2,256,1280]{2,1,0:T(8,128)} collective-permute-done((f32[2,256,1280]{2,1,0:T(8,128)}, f32[2,256,1280]{2,1,0:T(8,128)}, u32[]{:S(2)}, u32[]{:S(2)}) %collective-permute-start.2) | collective-permute-done | bytes 2621472 | tf_op jit(solution)/shard_map/ppermute | solution.py:14
  1266.5 24.7 %collective-permute-start.3 = (f32[2,512,256]{2,1,0:T(8,128)S(1)}, f32[2,512,256]{2,1,0:T(8,128)S(1)}, u32[]{:S(2)}, u32[]{:S(2)}) collective-permute-start(f32[2,512,256]{2,1,0:T(8,128)S(1)} %slice.154), channel_id=1, source_target_pairs={{0,1},{1,2},{2,3},{3,4},{4,5},{5,6},{6,7},{8,9},{9,10},{10,11},{11... | collective-permute-start | bytes 3145736 | tf_op jit(solution)/shard_map/ppermute | solution.py:14
  1291.2 104.5 %all-reduce.2.cloned.1.call-done = f32[2,4,256,256]{3,2,1,0:T(8,128)} async-done(((f32[2,4,256,256]{3,2,1,0:T(8,128)}), f32[2,4,256,256]{3,2,1,0:T(8,128)}) %all-reduce.2.cloned.1.call-update) | async-done | bytes 2097168 | tf_op jit(solution)/shard_map/psum | solution.py:157
  (696 shorter events, 746.0 us)
Async XLA Ops:
  9.7 14.3 %copy-start.7 = (s32[12,2]{0,1:T(2,128)S(1)}, s32[12,2]{0,1:T(2,128)}, u32[]{:S(2)}) copy-start(s32[12,2]{0,1:T(2,128)} %param.15) | copy-start | bytes 292
  9.8 11.8 collective-permute-start
  22.7 30.5 %collective-permute-start.1 = (bf16[2,256,1280]{2,1,0:T(8,128)(2,1)}, bf16[2,256,1280]{2,1,0:T(8,128)(2,1)}, u32[]{:S(2)}, u32[]{:S(2)}) collective-permute-start(bf16[2,256,1280]{2,1,0:T(8,128)(2,1)} %pad_maximum_fusion.2), channel_id=1, source_target_pairs={{8,0},{16,8},{24,16},{32,24},{40,32},{48,40},{56,48},{64,56},{72,6... | collective-permute-start | bytes 3932168 | tf_op jit(solution)/shard_map/ppermute | solution.py:14
  25.7 27.1 %all-to-all-start = ((s32[16,2,2]{1,2,0:T(2,128)}), s32[16,2,2]{1,2,0:T(2,128)S(1)}, u32[]{:S(2)}, u32[]{:S(2)}) async-start(s32[16,2,2]{1,2,0:T(2,128)} %copy.139), calls=%async_computation | async-start | bytes 32768 | tf_op jit(solution)/shard_map/all_to_all | solution.py:143
  182.6 123.1 %all-to-all-start.1 = ((bf16[16,2,2,256,256]{4,3,2,1,0:T(8,128)(2,1)}), bf16[16,2,2,256,256]{4,3,2,1,0:T(8,128)(2,1)}, u32[]{:S(2)}, u32[]{:S(2)}) async-start(bf16[16,2,2,256,256]{4,3,2,1,0:T(8,128)(2,1)} %bitcast.236), calls=%async_computation.1 | async-start | bytes 16777216 | tf_op jit(solution)/shard_map/all_to_all | solution.py:144
  329.9 3.8 copy-start.1
  329.9 3.8 copy-start.4
  391.0 3.8 copy-start.1
  391.1 3.8 copy-start.4
  452.9 3.8 copy-start.1
  452.9 3.8 copy-start.4
  483.9 3.8 copy-start.1
  483.9 3.8 copy-start.4
  545.7 3.8 copy-start.1
  545.7 3.8 copy-start.4
  576.7 3.8 copy-start.1
  576.7 3.8 copy-start.4
  638.6 3.8 copy-start.1
  638.6 3.8 copy-start.4
  694.8 125.8 %all-to-all-start.2 = ((bf16[16,2,2,256,256]{4,3,2,1,0:T(8,128)(2,1)}), bf16[16,2,2,256,256]{4,3,2,1,0:T(8,128)(2,1)}, u32[]{:S(2)}, u32[]{:S(2)}) async-start(bf16[16,2,2,256,256]{4,3,2,1,0:T(8,128)(2,1)} %bitcast.235), calls=%async_computation.2 | async-start | bytes 16777216 | tf_op jit(solution)/shard_map/all_to_all | solution.py:148
  700.3 695.4 %all-reduce.2.cloned.1.call-start = ((), (), s32[]{:S(2)}) async-start(), calls=%async_computation.3 | async-start | bytes 4194304 | tf_op jit(solution)/shard_map/psum | solution.py:157
  1200.1 6.3 copy-start.2
  1203.7 57.6 %collective-permute-start.2 = (f32[2,256,1280]{2,1,0:T(8,128)}, f32[2,256,1280]{2,1,0:T(8,128)}, u32[]{:S(2)}, u32[]{:S(2)}) collective-permute-start(f32[2,256,1280]{2,1,0:T(8,128)} %slice.122), channel_id=1, source_target_pairs={{0,8},{8,16},{16,24},{24,32},{32,40},{40,48},{48,56},{56,64},{64,7... | collective-permute-start | bytes 7864328 | tf_op jit(solution)/shard_map/ppermute | solution.py:14
  1266.5 134.8 %collective-permute-start.3 = (f32[2,512,256]{2,1,0:T(8,128)S(1)}, f32[2,512,256]{2,1,0:T(8,128)S(1)}, u32[]{:S(2)}, u32[]{:S(2)}) collective-permute-start(f32[2,512,256]{2,1,0:T(8,128)S(1)} %slice.154), channel_id=1, source_target_pairs={{0,1},{1,2},{2,3},{3,4},{4,5},{5,6},{6,7},{8,9},{9,10},{10,11},{11... | collective-permute-start | bytes 3145736 | tf_op jit(solution)/shard_map/ppermute | solution.py:14
  (36 other events, 113.1 us)
Sparse Core Ops, SparseCore 0:
  1208.4 187.1 all-reduce.1
where the time goes:
time: 1420 us; the launch traced here: 1410 us
  local copies, waits for them, and re-layouts  440 us (31%)
  waiting for transfers between devices  416 us (29%)
  matrix products  261 us (18%)
  loops' own time  122 us (9%)
  other arithmetic  106 us (7%)
  starting transfers between devices  53.2 us (4%)
  between operations  14.3 us (1%)
    dynamic_update_slice x32, local copies, waits for them, and re-layouts, add_one(): lax.dynamic_update_slice(field, current + pieces[index].astype(jnp.float3...  190 us
    gather x96, local copies, waits for them, and re-layouts  122 us
    all_to_all x1, waiting for transfers between devices, on_device(): lax.all_to_all(outgoing, 'ty', split_axis=0, concat_axis=0, tiled=True)  120 us
    another operation x1, loops' own time, deposit(): return lax.fori_loop(0, places.shape[0], add_one, grid)  119 us
    all_to_all x1, waiting for transfers between devices, on_device(): lax.all_to_all(cut_patches(extended, incoming, size), 'ty', split_axis=0,...  115 us
    psum x1, waiting for transfers between devices, on_device(): probe_grad = lax.psum(batch_total, ('ty', 'tx')) / scale_root  104 us
    ppermute x4, waiting for transfers between devices, from_behind(): lax.ppermute(value, axis, [(source, source + steps) for source in range(l...  58.6 us
    dot_general x24, matrix products, left_product(): jnp.einsum('sk,mkn->msn', table_im, right_im, preferred_element_type=jnp....  48.5 us
  transfers between devices with their start and end apart: 8, of which 6 were waited for; matrix products, arithmetic and copies ran while one was open for 1% of the time, Pallas kernels for 0%

commit v1 on v0

v1 whole, which is shorter than its diff:
```python
import jax
import jax.numpy as jnp
import ml_dtypes
import numpy as np
from jax import lax
from jax.experimental import pallas as pl
from jax.experimental.pallas import tpu as pltpu
from jax.sharding import PartitionSpec as P

bf = jnp.bfloat16
f32 = jnp.float32
N = 256
H = 128
TILE_R = 512
TILE_C = 1024
POS = 12
VMEM_LIMIT = 60 * 2**20


def make_tables():
    k = np.arange(N)
    ang = ((k[:, None] * k[None, :]) % N).astype(np.float64) * (2 * np.pi / N)
    re = (np.cos(ang) / 16).astype(np.float32).astype(ml_dtypes.bfloat16).astype(np.float32)
    im = (-np.sin(ang) / 16).astype(np.float32).astype(ml_dtypes.bfloat16).astype(np.float32)
    order = np.arange(128).reshape(8, 16).T.reshape(-1)
    def mix(a, b):
        return np.stack([a.reshape(16, 8, -1), b.reshape(16, 8, -1)], 1).reshape(256, -1)
    out = []
    for par in (0, 1):
        r, i = re[:H, par::2], im[:H, par::2]
        out.append(np.block([[r, i], [-i, r]]))
    for par in (0, 1):
        r, i = re[par::2][:, order], im[par::2][:, order]
        out.append(mix(np.block([r, -i]), np.block([i, r])))
    for par in (0, 1):
        r, i = re[par::2, :H], -im[par::2, :H]
        out.append(np.block([[r, i], [-i, r]]))
    for par in (0, 1):
        r, i = re[order][:, par::2], -im[order][:, par::2]
        out.append(mix(np.block([r, -i]), np.block([i, r])))
    return np.stack(out).astype(ml_dtypes.bfloat16)

def arrange(x):
    lead = x.shape[:-2]
    return jnp.swapaxes(jnp.moveaxis(x.reshape(*lead, 2, 8, 16, x.shape[-1]), -2, -4), -3, -3).reshape(*lead, 256, x.shape[-1])

def restore(x):
    lead = x.shape[:-2]
    return jnp.moveaxis(x.reshape(*lead, 16, 2, 8, x.shape[-1]), -4, -2).reshape(*lead, 256, x.shape[-1])

def dot(a, b):
    return jnp.dot(a, b, preferred_element_type=f32)

def halves(x):
    x = x.reshape(16, 2, 8, x.shape[-1])
    return x[:, 0].reshape(128, x.shape[-1]), x[:, 1].reshape(128, x.shape[-1])

def p1(m, probe, pat, A):
    for c in range(2):
        ch = slice(c * H, c * H + H)
    pr, pi = probe[0, m], probe[1, m]
    qr, qi = pat[0], pat[1]
    er = pr * qr - pi * qi
    ei = pr * qi + pi * qr
    A[m, 0, :, :H] = (er[:, :H] + er[:, H:]).astype(bf)
    A[m, 0, :, H:] = (ei[:, :H] + ei[:, H:]).astype(bf)
    A[m, 1, :, :H] = (er[:, :H] - er[:, H:]).astype(bf)
    A[m, 1, :, H:] = (ei[:, :H] - ei[:, H:]).astype(bf)

def p2(m, tab, A, B):
    for p in (0, 1):
        t, b = halves(dot(A[m, p], tab[p]))
        s = (t + b).astype(bf)
        d = (t - b).astype(bf)
        ls = slice(p * H, p * H + H)
        B[m, 0, :H, ls] = s[:, :H]
        B[m, 0, H:, ls] = s[:, H:]
        B[m, 1, :H, ls] = d[:, :H]
        B[m, 1, H:, ls] = d[:, H:]

def p3(m, tab, B, far, inten):
    for p in (0, 1):
        r, i = halves(dot(tab[2 + p], B[m, p]))
        far[m, p, 0] = r
        far[m, p, 1] = i
        t = r * r + i * i
        if m == 0:
            inten[p] = t
        else:
            inten[p] += t

def p4(amp, inten):
    for p in (0, 1):
        a = amp[p * H:(p + 1) * H].astype(f32)
        inten[p] = 1.0 - a * lax.rsqrt(jnp.maximum(inten[p], 0.25))

def p5(m, far, fac, C):
    for p in (0, 1):
        f = fac[p]
        rr = (far[m, p, 0] * f).astype(bf)
        ri = (far[m, p, 1] * f).astype(bf)
        rs = slice(p * H, p * H + H)
        C[m, 0, rs, :H] = rr[:, :H]
        C[m, 0, rs, H:] = ri[:, :H]
        C[m, 1, rs, :H] = rr[:, H:]
        C[m, 1, rs, H:] = ri[:, H:]

def p6(m, tab, C, G):
    e = dot(C[m, 0], tab[4])
    o = dot(C[m, 1], tab[5])
    s = (e + o).astype(bf)
    d = (e - o).astype(bf)
    for p in (0, 1):
        rs = slice(p * H, p * H + H)
        G[m, p, :H, :H] = s[rs, :H]
        G[m, p, :H, H:] = d[rs, :H]
        G[m, p, H:, :H] = s[rs, H:]
        G[m, p, H:, H:] = d[rs, H:]

def p7(m, tab, G, probe, pat, grad, total):
    e = dot(tab[6], G[m, 0])
    o = dot(tab[7], G[m, 1])
    er, ei = halves(e)
    r_, i_ = halves(o)
    def both(a, b):
        return jnp.stack([a.reshape(16, 8, 256), b.reshape(16, 8, 256)], 1).reshape(256, 256)
    br = both(er + r_, er - r_)
    bi = both(ei + i_, ei - i_)
    pr, pi = probe[0, m], probe[1, m]
    qr, qi = pat[0], pat[1]
    gr = pr * br + pi * bi
    gi = pr * bi - pi * br
    if m == 0:
        grad[0] = gr
        grad[1] = gi
    else:
        grad[0] += gr
        grad[1] += gi
    total[0, m] += qr * br + qi * bi
    total[1, m] += qr * bi - qi * br

def position(probe, pat, amp, tab, A, B, far, C, G, total, grad, inten):
    M = 4
    for t in range(M + 2):
        if t - 2 >= 0: p3(t - 2, tab, B, far, inten)
        if 0 <= t - 1 < M: p2(t - 1, tab, A, B)
        if t < M: p1(t, probe, pat, A)
    p4(amp, inten)
    for t in range(M + 2):
        if t - 2 >= 0: p7(t - 2, tab, G, probe, pat, grad, total)
        if 0 <= t - 1 < M: p6(t - 1, tab, C, G)
        if t < M: p5(t, far, inten, C)

def fetch(ext, pat, r, c):
    ct = c // 128
    sh = c % 128
    lane = lax.broadcasted_iota(jnp.int32, (128, 128), 1)
    keep = lane < 128 - sh
    for k in (0, 1):
        for h in (0, 1):
            x = []
            for t in range(3):
                v = jnp.concatenate([ext[k, ct + t, pl.ds(r + 128 * h + i, 8, stride=16)] for i in range(16)], axis=0)
                x.append(pltpu.roll(v, 128 - sh, axis=1))
            for t in (0, 1):
                y = jnp.where(keep, x[t], x[t + 1])
                for i in range(16):
                    pat[k, 16 * i + 8 * h:16 * i + 8 * h + 8, t * H:t * H + H] = y[8 * i:8 * i + 8]

def deposit(grid, grad, r, c):
    ct = c // 128
    sh = c % 128
    lane = lax.broadcasted_iota(jnp.int32, (256, 128), 1)
    keep = lane >= sh
    for k in (0, 1):
        x = grad[k].astype(bf).astype(f32)
        a = pltpu.roll(x[:, :H], sh, axis=1)
        b = pltpu.roll(x[:, H:], sh, axis=1)
        z = jnp.zeros_like(a)
        for t, y in enumerate((jnp.where(keep, a, z), jnp.where(keep, b, a), jnp.where(keep, z, b))):
            for i in range(16):
                for h in (0, 1):
                    ds = pl.ds(r + 128 * h + i, 8, stride=16)
                    grid[k, ct + t, ds] = grid[k, ct + t, ds] + y[16 * i + 8 * h:16 * i + 8 * h + 8]


def parity_matrix():
    order = np.concatenate([np.arange(0, N, 2), np.arange(1, N, 2)])
    return np.eye(N)[order].astype(ml_dtypes.bfloat16)


def slot_of(off, i):
    tile = off[2 * i] // TILE_R
    rank = jnp.int32(0)
    for j in range(POS):
        same = (off[2 * j] // TILE_R == tile) & (j < i)
        rank = rank + same.astype(jnp.int32)
    return tile, rank


def prep_kernel(off, amp, perm, out):
    a = amp[0].astype(bf)
    a = dot(perm[...], a).astype(bf)
    out[0, 0] = lax.dot_general(a, perm[...], (((1,), (1,)), ((), ())), preferred_element_type=f32).astype(bf)


def prepare(off, amplitude, sources):
    def place(i, off):
        tile, rank = slot_of(off, i)
        return (tile, rank, 0, 0)

    return pl.pallas_call(
        prep_kernel,
        out_shape=jax.ShapeDtypeStruct((sources, 2, N, N), bf),
        grid_spec=pltpu.PrefetchScalarGridSpec(
            num_scalar_prefetch=1,
            grid=(POS,),
            in_specs=[pl.BlockSpec((1, N, N), lambda i, o: (i, 0, 0)), pl.BlockSpec((N, N), lambda i, o: (0, 0))],
            out_specs=pl.BlockSpec((1, 1, N, N), place),
        ),
    )(off, amplitude, parity_matrix())


def find(off, source, tile):
    rows, cols = [jnp.int32(-1)] * 2, [jnp.int32(0)] * 2
    seen = jnp.int32(0)
    for i in range(POS):
        base = (source * POS + i) * 2
        r, c = off[base], off[base + 1]
        mine = r // TILE_R == tile
        for q in range(2):
            take = mine & (seen == q)
            rows[q] = jnp.where(take, r % TILE_R, rows[q])
            cols[q] = jnp.where(take, c % TILE_C, cols[q])
        seen = seen + mine.astype(jnp.int32)
    return rows, cols


def tile_kernel(off, spec, right, lower, corner, probe, amp, tab, main_o, down_o, right_o, corner_o, total, ext, grid, pat, A, B, far, C, G, grad, inten):
    s = pl.program_id(0)
    @pl.when(s == 0)
    def _():
        for c in (0, 1):
            for t in range(10):
                ls = slice(t * H, t * H + H)
                l2 = slice(t * H - 1024, t * H - 1024 + H)
                ext[c, t, :512] = (spec[c, :, ls] if t < 8 else right[c, :, l2]).astype(bf).astype(f32)
                ext[c, t, 512:] = (lower[c, :, ls] if t < 8 else corner[c, :, l2]).astype(f32)
        grid[...] = jnp.zeros_like(grid)
        total[...] = jnp.zeros_like(total)
    rows, cols = find(off, s, lax.axis_index("ty"))
    for q in range(2):
        @pl.when(rows[q] >= 0)
        def _():
            r = rows[q]
            c = cols[q]
            fetch(ext, pat, r, c)
            position(probe, pat, amp.at[0, q], tab, A, B, far, C, G, total, grad, inten)
            deposit(grid, grad, r, c)
    @pl.when(s == pl.num_programs(0) - 1)
    def _():
        for c in (0, 1):
            for t in range(10):
                ls = slice(t * H, t * H + H)
                l2 = slice(t * H - 1024, t * H - 1024 + H)
                if t < 8:
                    main_o[c, :, ls] = grid[c, t, :512]
                    down_o[c, :, ls] = grid[c, t, 512:].astype(bf)
                else:
                    right_o[c, :, l2] = grid[c, t, :512].astype(bf)
                    corner_o[c, :, l2] = grid[c, t, 512:].astype(bf)

def compute(off, spec, right, lower, corner, probe, amp, tab):
    probe = arrange(probe)
    full = lambda *shape: pl.BlockSpec(shape, lambda i, o: (0,) * len(shape), pipeline_mode=pl.Buffered(1))
    main, down, rt, cn, total = pl.pallas_call(
        tile_kernel,
        out_shape=[jax.ShapeDtypeStruct((2, 512, 1024), f32), jax.ShapeDtypeStruct((2, 256, 1024), bf),
                   jax.ShapeDtypeStruct((2, 512, 256), bf), jax.ShapeDtypeStruct((2, 256, 256), bf),
                   jax.ShapeDtypeStruct((2, 4, 256, 256), f32)],
        grid_spec=pltpu.PrefetchScalarGridSpec(
            num_scalar_prefetch=1, grid=(amp.shape[0],),
            in_specs=[full(2, 512, 1024), full(2, 512, 256), full(2, 256, 1024), full(2, 256, 256),
                      full(2, 4, 256, 256), pl.BlockSpec((1, 2, 256, 256), lambda i, o: (i, 0, 0, 0)), full(8, 256, 256)],
            out_specs=[full(2, 512, 1024), full(2, 256, 1024), full(2, 512, 256), full(2, 256, 256), full(2, 4, 256, 256)],
            scratch_shapes=[pltpu.VMEM((2, 10, 768, 128), f32), pltpu.VMEM((2, 10, 768, 128), f32), pltpu.VMEM((2, 256, 256), f32),
                            pltpu.VMEM((4, 2, 256, 256), bf), pltpu.VMEM((4, 2, 256, 256), bf), pltpu.VMEM((4, 2, 2, 128, 256), f32),
                            pltpu.VMEM((4, 2, 256, 256), bf), pltpu.VMEM((4, 2, 256, 256), bf), pltpu.VMEM((2, 256, 256), f32),
                            pltpu.VMEM((2, 128, 256), f32)]),
        compiler_params=pltpu.CompilerParams(vmem_limit_bytes=VMEM_LIMIT),
    )(off, spec, right, lower, corner, probe, amp, tab)
    return main, down, rt, cn, restore(total)


def shift(value, d_ty, d_tx, n_ty, n_tx):
    pairs = []
    for y in range(n_ty):
        for x in range(n_tx):
            if 0 <= y + d_ty < n_ty and 0 <= x + d_tx < n_tx:
                pairs.append((y * n_tx + x, (y + d_ty) * n_tx + x + d_tx))
    return lax.ppermute(value, ("ty", "tx"), pairs)


def on_device(specimen, probe, amplitude, offsets):
    n_ty, n_tx = lax.axis_size("ty"), lax.axis_size("tx")
    positions = offsets.shape[0] * n_ty * n_tx
    right = shift(specimen[:, :, :N].astype(bf), 0, -1, n_ty, n_tx)
    lower = shift(specimen[:, :N, :].astype(bf), -1, 0, n_ty, n_tx)
    corner = shift(specimen[:, :N, :N].astype(bf), -1, -1, n_ty, n_tx)
    everyone = lax.all_gather(offsets.reshape(-1), "ty", tiled=True)
    slots = prepare(offsets.reshape(-1), amplitude, n_ty)
    arrived = lax.all_to_all(slots, "ty", split_axis=0, concat_axis=0, tiled=True)
    main, down, rt, cn, total = compute(everyone, specimen, right, lower, corner, probe, arrived, make_tables())
    down = shift(down, 1, 0, n_ty, n_tx).astype(f32)
    rt = shift(rt, 0, 1, n_ty, n_tx).astype(f32)
    cn = shift(cn, 1, 1, n_ty, n_tx).astype(f32)
    main = main.at[:, :N, :].add(down).at[:, :, :N].add(rt).at[:, :N, :N].add(cn)
    probe_grad = lax.psum(total, ("ty", "tx")) * (probe.shape[1] / np.sqrt(positions))
    return (main, probe_grad.astype(f32))


def solution(mesh):
    in_specs = (P(None, "ty", "tx"), P(), P(("ty", "tx"), None, None), P(("ty", "tx"), None))
    out_specs = (P(None, "ty", "tx"), P())
    return jax.shard_map(on_device, mesh=mesh, in_specs=in_specs, out_specs=out_specs, check_vma=False)
```

time: 1420 us -> 438 us (0.31)
  local copies, waits for them, and re-layouts: 440 us -> 13.2 us
  waiting for transfers between devices: 416 us -> 142 us
  matrix products: 261 us -> 0 us
  loops' own time: 122 us -> 0 us
  other arithmetic: 106 us -> 6.77 us
  starting transfers between devices: 53.2 us -> 151 us
  blocking collectives: 0 us -> 81.2 us
  Pallas kernels: 0 us -> 28.2 us
    dot_general x192 -> x0, matrix products: 261 us -> none  [the longest x24 48.5 us: left_product(): jnp.einsum('sk,mkn->msn', table_im, right_im, preferred_element_type=jnp....]
    all_to_all x3 -> x1, waiting for transfers between devices: 253 us -> 0.01 us  [on_device(): lax.all_to_all(slots, 'ty', split_axis=0, concat_axis=0, tiled=True)]
    dynamic_update_slice x56 -> x0, local copies, waits for them, and re-layouts: 220 us -> none  [the longest x32 190 us: add_one(): lax.dynamic_update_slice(field, current + pieces[index].astype(jnp.float3...]
    gather x97 -> x0, local copies, waits for them, and re-layouts: 128 us -> none
    another operation x3 -> x0, loops' own time: 122 us -> none  [the longest x1 119 us: deposit(): return lax.fori_loop(0, places.shape[0], add_one, grid)]
    ppermute x4 -> x6, starting transfers between devices: 32.1 us -> 142 us  [shift(): return lax.ppermute(value, ('ty', 'tx'), pairs)]
    add x44 -> x0, other arithmetic: 86.8 us -> none  [the longest x32 45.4 us: add_one(): current + pieces[index].astype(jnp.float32)]
    unnamed x0 -> x1, blocking collectives: none -> 81.2 us
  transfers between devices with their start and end apart: 8 -> 8, of which waited for: 6 -> 1; matrix products, arithmetic and copies ran while one was open for 1% -> 2% of each run, Pallas kernels for 0% -> 0%
where the time goes in v1:
time: 438 us; the launch traced here: 437 us
  starting transfers between devices  151 us (34%)
  waiting for transfers between devices  142 us (32%)
  blocking collectives  81.2 us (19%)
  Pallas kernels  28.2 us (6%)
  between operations  14.8 us (3%)
  local copies, waits for them, and re-layouts  13.2 us (3%)
  other arithmetic  6.77 us (2%)
    psum x1, waiting for transfers between devices, on_device(): lax.psum(total, ('ty', 'tx')) * (probe.shape[1] / np.sqrt(positions))  142 us
    ppermute x6, starting transfers between devices, shift(): return lax.ppermute(value, ('ty', 'tx'), pairs)  142 us
    unnamed x1, blocking collectives  81.2 us
    pallas_call x1, Pallas kernels, compute(): pl.pallas_call(tile_kernel, out_shape=[jax.ShapeDtypeStruct((2, 512, 1024...  17.2 us
    pallas_call x1, Pallas kernels, prepare(): pl.pallas_call(prep_kernel, out_shape=jax.ShapeDtypeStruct((sources, 2, N...  11 us
  transfers between devices with their start and end apart: 8, of which 1 were waited for; matrix products, arithmetic and copies ran while one was open for 2% of the time, Pallas kernels for 0%

profile of v1, /device:TPU:1, one launch (start us, length us, event | category | flops | bytes accessed | tf_op | source)
XLA Modules:
  0.0 437.0 jit_solution(8896749244616689077)
XLA Ops:
  7.2 0.8 copy.11
  7.9 0.7 reshape.120.off
  8.6 11.0 %shard_map.77 = bf16[16,2,256,256]{3,2,1,0:T(8,128)(2,1)} custom-call(s32[24]{0:T(128)} %reshape.120.off, f32[12,256,256]{2,1,0:T(8,128)} %amp.1, bf16[256,256]{1,0:T(8,128)(2,1)} %constant.87.clone.perm), custom_call_target="tpu_custom_call" | custom-call | tf_op jit(solution)/shard_map/pallas_call | solution.py:212
  19.6 8.6 %all-to-all-start = ((bf16[16,2,256,256]{3,2,1,0:T(8,128)(2,1)}), bf16[16,2,256,256]{3,2,1,0:T(8,128)(2,1)}, u32[]{:S(2)}, u32[]{:S(2)}) async-start(bf16[16,2,256,256]{3,2,1,0:T(8,128)(2,1)} %shard_map.77), calls=%async_computation | async-start | bytes 8388608 | tf_op jit(solution)/shard_map/all_to_all | solution.py:312
  28.3 2.5 convert.5
  30.9 1.4 collective-permute-start.1
  32.4 2.9 collective-permute-start
  35.3 0.7 slice.97
  36.1 1.3 collective-permute-start.2
  37.4 2.5 copy.12
  39.9 0.6 dynamic-slice.24
  41.3 81.2 %all-reduce.off = s32[384]{0:T(512)} all-reduce(s32[384]{0:T(512)S(1)} %dynamic-update-slice.9), channel_id=1, replica_groups=mesh['ty'=16,'tx'=8] {'ty'}, use_global_device_ids=true, to_apply=%add | all-reduce | flops 384 | bytes 3072
  122.6 0.7 copy-done.5
  123.4 0.4 copy-done.3
  123.8 17.2 %shard_map.78 = (f32[2,512,1024]{2,1,0:T(8,128)}, bf16[2,256,1024]{2,1,0:T(8,128)(2,1)}, bf16[2,512,256]{2,1,0:T(8,128)(2,1)}, bf16[2,256,256]{2,1,0:T(8,128)(2,1)}, f32[2,4,256,256]{3,2,1,0:T(8,128)}) custom-call(s32[384]{0:T(512)} %all-reduce.off, f32[2,512,1024]{2,1,0:T(8,128)} %spec.1, bf16[2,512,256]{2,1,0:T(8,128)(2,1)} %copy-done.4, ...), custom_call_target="tpu_custom_call" | custom-call | tf_op jit(solution)/shard_map/pallas_call | solution.py:276
  141.0 4.2 copy.13
  145.2 32.8 %collective-permute-start.3 = (bf16[2,256,1024]{2,1,0:T(8,128)(2,1)S(1)}, bf16[2,256,1024]{2,1,0:T(8,128)(2,1)S(1)}, u32[]{:S(2)}, u32[]{:S(2)}) collective-permute-start(bf16[2,256,1024]{2,1,0:T(8,128)(2,1)S(1)} %copy-done.7), channel_id=1, source_target_pairs={{0,8},{1,9},{2,10},{3,11},{4,12},{5,13},{6,14},{7,15},{8,16},{9,17... | collective-permute-start | bytes 3145736 | tf_op jit(solution)/shard_map/ppermute | solution.py:301
  178.1 101.7 %collective-permute-start.5 = (bf16[2,256,256]{2,1,0:T(8,128)(2,1)}, bf16[2,256,256]{2,1,0:T(8,128)(2,1)S(1)}, u32[]{:S(2)}, u32[]{:S(2)}) collective-permute-start(bf16[2,256,256]{2,1,0:T(8,128)(2,1)} %get-tuple-element.46), channel_id=1, source_target_pairs={{0,9},{1,10},{2,11},{3,12},{4,13},{5,14},{6,15},{8,17},{9,18},{10,... | collective-permute-start | bytes 786440 | tf_op jit(solution)/shard_map/ppermute | solution.py:301
  279.8 1.9 collective-permute-start.4
  281.7 142.1 %all-reduce.3.cloned.1.call-done = f32[2,4,256,256]{3,2,1,0:T(8,128)} async-done(((f32[2,4,256,256]{3,2,1,0:T(8,128)}), f32[2,4,256,256]{3,2,1,0:T(8,128)}) %all-reduce.3.cloned.1.call-update) | async-done | bytes 2097168 | tf_op jit(solution)/shard_map/psum | solution.py:318
  423.9 3.2 broadcast_multiply_fusion
  427.1 0.6 add_dynamic-update-slice_fusion
  427.7 0.4 constant_dynamic-update-slice_fusion
  428.2 2.0 copy-done.1
  (31 shorter events, 0.7 us)
Async XLA Ops:
  19.6 103.0 %all-to-all-start = ((bf16[16,2,256,256]{3,2,1,0:T(8,128)(2,1)}), bf16[16,2,256,256]{3,2,1,0:T(8,128)(2,1)}, u32[]{:S(2)}, u32[]{:S(2)}) async-start(bf16[16,2,256,256]{3,2,1,0:T(8,128)(2,1)} %shard_map.77), calls=%async_computation | async-start | bytes 8388608 | tf_op jit(solution)/shard_map/all_to_all | solution.py:312
  28.2 395.6 %all-reduce.3.cloned.1.call-start = ((), (), s32[]{:S(2)}) async-start(), calls=%async_computation.1 | async-start | bytes 4194304 | tf_op jit(solution)/shard_map/psum | solution.py:318
  30.8 6.5 %copy-start.2 = (f32[2,4,256,256]{3,2,1,0:T(8,128)S(1)}, f32[2,4,256,256]{3,2,1,0:T(8,128)}, u32[]{:S(2)}) copy-start(f32[2,4,256,256]{3,2,1,0:T(8,128)} %param.13) | copy-start | bytes 6291460
  30.9 9.0 %copy-start.9 = (u32[128]{0:T(128)S(1)}, u32[128]{0:T(128)}, u32[]{:S(2)}) copy-start(u32[128]{0:T(128)} %constant.93) | copy-start | bytes 1540
  30.9 10.1 %copy-start.6 = (s32[24]{0:T(128)S(1)}, s32[24]{0:T(128)}, u32[]{:S(2)}) copy-start(s32[24]{0:T(128)} %reshape.120.off) | copy-start | bytes 292
  30.9 91.6 %collective-permute-start.1 = (bf16[2,256,1024]{2,1,0:T(8,128)(2,1)S(1)}, bf16[2,256,1024]{2,1,0:T(8,128)(2,1)S(1)}, u32[]{:S(2)}, u32[]{:S(2)}) collective-permute-start(bf16[2,256,1024]{2,1,0:T(8,128)(2,1)S(1)} %slice.96), channel_id=1, source_target_pairs={{8,0},{9,1},{10,2},{11,3},{12,4},{13,5},{14,6},{15,7},{16,8},{17,9... | collective-permute-start | bytes 3145736 | tf_op jit(solution)/shard_map/ppermute | solution.py:301
  32.4 90.1 %collective-permute-start = (bf16[2,512,256]{2,1,0:T(8,128)(2,1)S(1)}, bf16[2,512,256]{2,1,0:T(8,128)(2,1)S(1)}, u32[]{:S(2)}, u32[]{:S(2)}) collective-permute-start(bf16[2,512,256]{2,1,0:T(8,128)(2,1)S(1)} %slice.95), channel_id=1, source_target_pairs={{1,0},{2,1},{3,2},{4,3},{5,4},{6,5},{7,6},{9,8},{10,9},{11,10},{12... | collective-permute-start | bytes 1572872 | tf_op jit(solution)/shard_map/ppermute | solution.py:301
  36.1 86.5 %collective-permute-start.2 = (bf16[2,256,256]{2,1,0:T(8,128)(2,1)}, bf16[2,256,256]{2,1,0:T(8,128)(2,1)S(1)}, u32[]{:S(2)}, u32[]{:S(2)}) collective-permute-start(bf16[2,256,256]{2,1,0:T(8,128)(2,1)} %slice.97), channel_id=1, source_target_pairs={{9,0},{10,1},{11,2},{12,3},{13,4},{14,5},{15,6},{17,8},{18,9},{19,... | collective-permute-start | bytes 786440 | tf_op jit(solution)/shard_map/ppermute | solution.py:301
  122.5 0.7 copy-start.5
  122.5 0.9 copy-start.4
  122.5 1.3 copy-start.3
  141.0 4.3 copy-start.7
  141.0 138.8 %copy-start.8 = (bf16[2,512,256]{2,1,0:T(8,128)(2,1)S(1)}, bf16[2,512,256]{2,1,0:T(8,128)(2,1)}, u32[]{:S(2)}) copy-start(bf16[2,512,256]{2,1,0:T(8,128)(2,1)} %get-tuple-element.45) | copy-start | bytes 1572868
  145.2 281.9 %collective-permute-start.3 = (bf16[2,256,1024]{2,1,0:T(8,128)(2,1)S(1)}, bf16[2,256,1024]{2,1,0:T(8,128)(2,1)S(1)}, u32[]{:S(2)}, u32[]{:S(2)}) collective-permute-start(bf16[2,256,1024]{2,1,0:T(8,128)(2,1)S(1)} %copy-done.7), channel_id=1, source_target_pairs={{0,8},{1,9},{2,10},{3,11},{4,12},{5,13},{6,14},{7,15},{8,16},{9,17... | collective-permute-start | bytes 3145736 | tf_op jit(solution)/shard_map/ppermute | solution.py:301
  178.1 250.0 %collective-permute-start.5 = (bf16[2,256,256]{2,1,0:T(8,128)(2,1)}, bf16[2,256,256]{2,1,0:T(8,128)(2,1)S(1)}, u32[]{:S(2)}, u32[]{:S(2)}) collective-permute-start(bf16[2,256,256]{2,1,0:T(8,128)(2,1)} %get-tuple-element.46), channel_id=1, source_target_pairs={{0,9},{1,10},{2,11},{3,12},{4,13},{5,14},{6,15},{8,17},{9,18},{10,... | collective-permute-start | bytes 786440 | tf_op jit(solution)/shard_map/ppermute | solution.py:301
  279.8 147.9 %collective-permute-start.4 = (bf16[2,512,256]{2,1,0:T(8,128)(2,1)S(1)}, bf16[2,512,256]{2,1,0:T(8,128)(2,1)S(1)}, u32[]{:S(2)}, u32[]{:S(2)}) collective-permute-start(bf16[2,512,256]{2,1,0:T(8,128)(2,1)S(1)} %copy-done.8), channel_id=1, source_target_pairs={{0,1},{1,2},{2,3},{3,4},{4,5},{5,6},{6,7},{8,9},{9,10},{10,11},{11... | collective-permute-start | bytes 1572872 | tf_op jit(solution)/shard_map/ppermute | solution.py:301
  423.9 3.3 copy-start
  428.2 2.0 copy-start.1
Sparse Core Ops, SparseCore 0:
  145.3 278.4 all-reduce.2

commit v2 on v1

v2 whole, which is shorter than its diff:
```python
import functools

import jax
import jax.numpy as jnp
import ml_dtypes
import numpy as np
from jax import lax
from jax.experimental import pallas as pl
from jax.experimental.pallas import tpu as pltpu
from jax.sharding import PartitionSpec as P

bf = jnp.bfloat16
f32 = jnp.float32
N = 256
H = 128
TILE_R = 512
TILE_C = 1024
POS = 12
VMEM_LIMIT = 60 * 2**20
MESH = pl.DeviceIdType.MESH
S = 2
B = 16 // S

def row0(i):
    return i // S * 8 * S + i % S

def make_tables():
    k = np.arange(N)
    ang = ((k[:, None] * k[None, :]) % N).astype(np.float64) * (2 * np.pi / N)
    re = (np.cos(ang) / 16).astype(np.float32).astype(ml_dtypes.bfloat16).astype(np.float32)
    im = (-np.sin(ang) / 16).astype(np.float32).astype(ml_dtypes.bfloat16).astype(np.float32)
    order = np.arange(128).reshape(B, 8, S).swapaxes(1, 2).reshape(-1)
    def mix(a, b):
        return np.stack([a.reshape(16, 8, -1), b.reshape(16, 8, -1)], 1).reshape(256, -1)
    out = []
    for par in (0, 1):
        r, i = re[:H, par::2], im[:H, par::2]
        out.append(np.block([[r, i], [-i, r]]))
    for par in (0, 1):
        r, i = re[par::2][:, order], im[par::2][:, order]
        out.append(mix(np.block([r, -i]), np.block([i, r])))
    for par in (0, 1):
        r, i = re[par::2, :H], -im[par::2, :H]
        out.append(np.block([[r, i], [-i, r]]))
    for par in (0, 1):
        r, i = re[order][:, par::2], -im[order][:, par::2]
        out.append(mix(np.block([r, -i]), np.block([i, r])))
    return np.stack(out).astype(ml_dtypes.bfloat16)

def arrange(x):
    lead = x.shape[:-2]
    x = x.reshape(*lead, 2, B, 8, S, x.shape[-1])
    k = len(lead)
    return jnp.transpose(x, (*range(k), k + 1, k + 3, k, k + 2, k + 4)).reshape(*lead, 256, x.shape[-1])

def restore(x):
    lead = x.shape[:-2]
    x = x.reshape(*lead, B, S, 2, 8, x.shape[-1])
    k = len(lead)
    return jnp.transpose(x, (*range(k), k + 2, k, k + 3, k + 1, k + 4)).reshape(*lead, 256, x.shape[-1])

def dot(a, b):
    return jnp.dot(a, b, preferred_element_type=f32)

def halves(x):
    x = x.reshape(16, 2, 8, x.shape[-1])
    return x[:, 0].reshape(128, x.shape[-1]), x[:, 1].reshape(128, x.shape[-1])


def parity_matrix():
    order = np.concatenate([np.arange(0, N, 2), np.arange(1, N, 2)])
    return np.eye(N)[order].astype(ml_dtypes.bfloat16)


def slot_of(off, i):
    tile = off[2 * i] // TILE_R
    rank = jnp.int32(0)
    for j in range(POS):
        same = (off[2 * j] // TILE_R == tile) & (j < i)
        rank = rank + same.astype(jnp.int32)
    return tile, rank


def prep_kernel(off, amp, perm, out):
    a = amp[0].astype(bf)
    a = dot(perm[...], a).astype(bf)
    out[0, 0] = lax.dot_general(a, perm[...], (((1,), (1,)), ((), ())), preferred_element_type=f32).astype(bf)


def prepare(off, amplitude, sources):
    def place(i, off):
        tile, rank = slot_of(off, i)
        return (tile, rank, 0, 0)

    return pl.pallas_call(
        prep_kernel,
        out_shape=jax.ShapeDtypeStruct((sources, 2, N, N), bf),
        grid_spec=pltpu.PrefetchScalarGridSpec(
            num_scalar_prefetch=1,
            grid=(POS,),
            in_specs=[pl.BlockSpec((1, N, N), lambda i, o: (i, 0, 0)), pl.BlockSpec((N, N), lambda i, o: (0, 0))],
            out_specs=pl.BlockSpec((1, 1, N, N), place),
        ),
    )(off, amplitude, parity_matrix())


def find(off, source, tile):
    rows, cols = [jnp.int32(-1)] * 2, [jnp.int32(0)] * 2
    seen = jnp.int32(0)
    for i in range(POS):
        base = (source * POS + i) * 2
        r, c = off[base], off[base + 1]
        mine = r // TILE_R == tile
        for q in range(2):
            take = mine & (seen == q)
            rows[q] = jnp.where(take, r % TILE_R, rows[q])
            cols[q] = jnp.where(take, c % TILE_C, cols[q])
        seen = seen + mine.astype(jnp.int32)
    return rows, cols


def p1(probe, pat, A):
    pr, pi = probe[0], probe[1]
    qr, qi = pat[0], pat[1]
    er = pr * qr - pi * qi
    ei = pr * qi + pi * qr
    A[0, :, :H] = (er[:, :H] + er[:, H:]).astype(bf)
    A[0, :, H:] = (ei[:, :H] + ei[:, H:]).astype(bf)
    A[1, :, :H] = (er[:, :H] - er[:, H:]).astype(bf)
    A[1, :, H:] = (ei[:, :H] - ei[:, H:]).astype(bf)


def p2(tab, A, Bb):
    for p in (0, 1):
        t, b = halves(dot(A[p], tab[p]))
        s = (t + b).astype(bf)
        d = (t - b).astype(bf)
        ls = slice(p * H, p * H + H)
        Bb[0, :H, ls] = s[:, :H]
        Bb[0, H:, ls] = s[:, H:]
        Bb[1, :H, ls] = d[:, :H]
        Bb[1, H:, ls] = d[:, H:]


def p3(first, tab, Bb, far, inten):
    for p in (0, 1):
        r, i = halves(dot(tab[2 + p], Bb[p]))
        far[p, 0] = r
        far[p, 1] = i
        t = r * r + i * i
        inten[p] = t if first else inten[p] + t


def p4(amp, inten, fac):
    for p in (0, 1):
        a = amp[p * H:(p + 1) * H].astype(f32)
        fac[p] = 1.0 - a * lax.rsqrt(jnp.maximum(inten[p], 0.25))


def p5(far, fac, C):
    for p in (0, 1):
        f = fac[p]
        rr = (far[p, 0] * f).astype(bf)
        ri = (far[p, 1] * f).astype(bf)
        rs = slice(p * H, p * H + H)
        C[0, rs, :H] = rr[:, :H]
        C[0, rs, H:] = ri[:, :H]
        C[1, rs, :H] = rr[:, H:]
        C[1, rs, H:] = ri[:, H:]


def p6(tab, C, G):
    e = dot(C[0], tab[4])
    o = dot(C[1], tab[5])
    s = (e + o).astype(bf)
    d = (e - o).astype(bf)
    for p in (0, 1):
        rs = slice(p * H, p * H + H)
        G[p, :H, :H] = s[rs, :H]
        G[p, :H, H:] = d[rs, :H]
        G[p, H:, :H] = s[rs, H:]
        G[p, H:, H:] = d[rs, H:]


def both(a, b):
    return jnp.stack([a.reshape(16, 8, 256), b.reshape(16, 8, 256)], 1).reshape(256, 256)


def p7(first, tab, G, probe, pat, grad, total, m):
    er, ei = halves(dot(tab[6], G[0]))
    r_, i_ = halves(dot(tab[7], G[1]))
    br = both(er + r_, er - r_)
    bi = both(ei + i_, ei - i_)
    pr, pi = probe[0], probe[1]
    qr, qi = pat[0], pat[1]
    gr = pr * br + pi * bi
    gi = pr * bi - pi * br
    grad[0] = gr if first else grad[0] + gr
    grad[1] = gi if first else grad[1] + gi
    total[0, m] += qr * br + qi * bi
    total[1, m] += qr * bi - qi * br


def fetch(ext, pat, r, c):
    ct = c // 128
    sh = c % 128
    lane = lax.broadcasted_iota(jnp.int32, (128, 128), 1)
    keep = lane < 128 - sh
    for k in (0, 1):
        for h in (0, 1):
            x = []
            for t in range(3):
                v = jnp.concatenate([ext[k, ct + t, pl.ds(r + 128 * h + row0(i), 8, stride=S)] for i in range(16)], axis=0)
                x.append(pltpu.roll(v, 128 - sh, axis=1))
            for t in (0, 1):
                y = jnp.where(keep, x[t], x[t + 1])
                for i in range(16):
                    pat[k, 16 * i + 8 * h:16 * i + 8 * h + 8, t * H:t * H + H] = y[8 * i:8 * i + 8]

def deposit(grid, grad, r, c):
    ct = c // 128
    sh = c % 128
    lane = lax.broadcasted_iota(jnp.int32, (256, 128), 1)
    keep = lane >= sh
    for k in (0, 1):
        x = grad[k].astype(bf).astype(f32)
        a = pltpu.roll(x[:, :H], sh, axis=1)
        b = pltpu.roll(x[:, H:], sh, axis=1)
        z = jnp.zeros_like(a)
        for t, y in enumerate((jnp.where(keep, a, z), jnp.where(keep, b, a), jnp.where(keep, z, b))):
            for i in range(16):
                for h in (0, 1):
                    ds = pl.ds(r + 128 * h + row0(i), 8, stride=S)
                    grid[k, ct + t, ds] = grid[k, ct + t, ds] + y[16 * i + 8 * h:16 * i + 8 * h + 8]


def forward_kernel(off, spec, right, lower, corner, probe, tab, far, pat, inten, ext, A, Bb):
    s = pl.program_id(0)

    @pl.when(s == 0)
    def _():
        for c in (0, 1):
            for t in range(10):
                ls = slice(t * H, t * H + H)
                l2 = slice(t * H - 1024, t * H - 1024 + H)
                ext[c, t, :512] = (spec[c, :, ls] if t < 8 else right[c, :, l2]).astype(bf).astype(f32)
                ext[c, t, 512:] = (lower[c, :, ls] if t < 8 else corner[c, :, l2]).astype(f32)

    rows, cols = find(off, s, lax.axis_index("ty"))

    @pl.when(rows[0] >= 0)
    def _():
        items = [(q, m) for q in range(2) for m in range(4)]
        for t in range(len(items) + 2):
            if 0 <= t - 1 < len(items):
                q, m = items[t - 1]
                p2(tab, A.at[q, m], Bb.at[q, m])
            if 0 <= t - 2 < len(items):
                q, m = items[t - 2]
                p3(m == 0, tab, Bb.at[q, m], far.at[0, q, m], inten.at[0, q])
            if t < len(items):
                q, m = items[t]
                if m == 0:
                    fetch(ext, pat.at[0, q], rows[q], cols[q])
                p1(probe.at[:, m], pat.at[0, q], A.at[q, m])


def backward_kernel(off, probe, tab, amp, far, pat, inten, main_o, down_o, right_o, corner_o, total, grid, fac, C, G, grad):
    s = pl.program_id(0)

    @pl.when(s == 0)
    def _():
        grid[...] = jnp.zeros_like(grid)
        total[...] = jnp.zeros_like(total)

    rows, cols = find(off, s, lax.axis_index("ty"))

    @pl.when(rows[0] >= 0)
    def _():
        items = [(q, m) for q in range(2) for m in range(4)]
        for t in range(len(items) + 2):
            if 0 <= t - 1 < len(items):
                q, m = items[t - 1]
                p6(tab, C.at[q, m], G.at[q, m])
            if 0 <= t - 2 < len(items):
                q, m = items[t - 2]
                p7(m == 0, tab, G.at[q, m], probe.at[:, m], pat.at[0, q], grad.at[q], total, m)
                if m == 3:
                    deposit(grid, grad.at[q], rows[q], cols[q])
            if t < len(items):
                q, m = items[t]
                if m == 0:
                    p4(amp.at[0, q], inten.at[0, q], fac.at[q])
                p5(far.at[0, q, m], fac.at[q], C.at[q, m])

    @pl.when(s == pl.num_programs(0) - 1)
    def _():
        for c in (0, 1):
            for t in range(10):
                ls = slice(t * H, t * H + H)
                l2 = slice(t * H - 1024, t * H - 1024 + H)
                if t < 8:
                    main_o[c, :, ls] = grid[c, t, :512]
                    down_o[c, :, ls] = grid[c, t, 512:].astype(bf)
                else:
                    right_o[c, :, l2] = grid[c, t, :512].astype(bf)
                    corner_o[c, :, l2] = grid[c, t, 512:].astype(bf)


def whole(*shape):
    return pl.BlockSpec(shape, lambda i, o: (0,) * len(shape), pipeline_mode=pl.Buffered(1))


def each(*shape):
    return pl.BlockSpec((1, *shape), lambda i, o: (i,) + (0,) * len(shape))


def like(shape, dtype):
    return jax.ShapeDtypeStruct(shape, dtype)


def forward(off, spec, right, lower, corner, probe, tab, sources):
    return pl.pallas_call(
        forward_kernel,
        out_shape=[like((sources, 2, 4, 2, 2, 128, 256), f32), like((sources, 2, 2, 256, 256), f32), like((sources, 2, 2, 128, 256), f32)],
        grid_spec=pltpu.PrefetchScalarGridSpec(
            num_scalar_prefetch=1, grid=(sources,),
            in_specs=[whole(2, 512, 1024), whole(2, 512, 256), whole(2, 256, 1024), whole(2, 256, 256), whole(2, 4, 256, 256), whole(8, 256, 256)],
            out_specs=[each(2, 4, 2, 2, 128, 256), each(2, 2, 256, 256), each(2, 2, 128, 256)],
            scratch_shapes=[pltpu.VMEM((2, 10, 768, 128), f32), pltpu.VMEM((2, 4, 2, 256, 256), bf), pltpu.VMEM((2, 4, 2, 256, 256), bf)]),
        compiler_params=pltpu.CompilerParams(vmem_limit_bytes=VMEM_LIMIT),
        cost_estimate=pl.CostEstimate(flops=32 * 2**29, bytes_accessed=100 * 2**20, transcendentals=0),
    )(off, spec, right, lower, corner, probe, tab)


def backward(off, probe, tab, amp, far, pat, inten, sources):
    return pl.pallas_call(
        backward_kernel,
        out_shape=[like((2, 512, 1024), f32), like((2, 256, 1024), bf), like((2, 512, 256), bf), like((2, 256, 256), bf), like((2, 4, 256, 256), f32)],
        grid_spec=pltpu.PrefetchScalarGridSpec(
            num_scalar_prefetch=1, grid=(sources,),
            in_specs=[whole(2, 4, 256, 256), whole(8, 256, 256), each(2, 256, 256), each(2, 4, 2, 2, 128, 256), each(2, 2, 256, 256), each(2, 2, 128, 256)],
            out_specs=[whole(2, 512, 1024), whole(2, 256, 1024), whole(2, 512, 256), whole(2, 256, 256), whole(2, 4, 256, 256)],
            scratch_shapes=[pltpu.VMEM((2, 10, 768, 128), f32), pltpu.VMEM((2, 2, 128, 256), f32), pltpu.VMEM((2, 4, 2, 256, 256), bf),
                            pltpu.VMEM((2, 4, 2, 256, 256), bf), pltpu.VMEM((2, 2, 256, 256), f32)]),
        compiler_params=pltpu.CompilerParams(vmem_limit_bytes=VMEM_LIMIT),
        cost_estimate=pl.CostEstimate(flops=32 * 2**29, bytes_accessed=100 * 2**20, transcendentals=0),
    )(off, probe, tab, amp, far, pat, inten)


def spread(axis, size, reach):
    lax.fori_loop(1, size, lambda d, c: (reach(d), c)[1], 0)


def beyond(axis, d, size):
    place = {"ty": lax.axis_index("ty"), "tx": lax.axis_index("tx")}
    place[axis] = lax.rem(place[axis] + d, size)
    return (place["ty"], place["tx"])


def gather_kernel(n_ty, own, out, send, recv):
    me = lax.axis_index("ty")
    barrier = pltpu.get_barrier_semaphore()
    spread("ty", n_ty, lambda d: pl.semaphore_signal(barrier, inc=1, device_id=beyond("ty", d, n_ty), device_id_type=MESH))
    pl.semaphore_wait(barrier, n_ty - 1)

    def copy(d):
        return pltpu.make_async_remote_copy(
            src_ref=own, dst_ref=out.at[me], send_sem=send.at[d], recv_sem=recv.at[d],
            device_id=beyond("ty", d, n_ty), device_id_type=MESH)

    spread("ty", n_ty, lambda d: copy(d).start())
    out[me] = own[...]
    spread("ty", n_ty, lambda d: copy(d).wait())


def gather_offsets(offsets, n_ty):
    own = jnp.zeros((8, 128), jnp.int32).at[0, : 2 * POS].set(offsets)
    out = pl.pallas_call(
        functools.partial(gather_kernel, n_ty),
        out_shape=like((n_ty, 8, 128), jnp.int32),
        in_specs=[pl.BlockSpec(memory_space=pltpu.VMEM)],
        out_specs=pl.BlockSpec(memory_space=pltpu.VMEM),
        scratch_shapes=[pltpu.SemaphoreType.DMA((n_ty,)), pltpu.SemaphoreType.DMA((n_ty,))],
        compiler_params=pltpu.CompilerParams(collective_id=0, has_side_effects=True),
    )(own)
    return out[:, 0, : 2 * POS].reshape(-1)


def finish_kernel(n_ty, n_tx, scale, total, down, right, corner, probe_o, down_o, right_o, corner_o,
                  cast, rax, ray, sx, sy, rbx, rby, gx, gy, hx, hy, send_ty, recv_ty, send_tx, recv_tx, send_h, recv_h):
    ty, tx = lax.axis_index("ty"), lax.axis_index("tx")
    nx, ny = 1024 // n_tx, 1024 // n_ty
    barrier = pltpu.get_barrier_semaphore()

    def greet(device):
        pl.semaphore_signal(barrier, inc=1, device_id=device, device_id_type=MESH)

    spread("ty", n_ty, lambda d: greet(beyond("ty", d, n_ty)))
    spread("tx", n_tx, lambda d: greet(beyond("tx", d, n_tx)))
    greet((lax.rem(ty + n_ty - 1, n_ty), lax.rem(tx + n_tx - 1, n_tx)))
    cast[...] = total[...].astype(bf)
    pl.semaphore_wait(barrier, n_ty + n_tx - 1)

    def over_ty(stage, d, src, dst):
        return pltpu.make_async_remote_copy(
            src_ref=src, dst_ref=dst, send_sem=send_ty.at[stage, d], recv_sem=recv_ty.at[stage, d],
            device_id=beyond("ty", d, n_ty), device_id_type=MESH)

    def over_tx(stage, d, src, dst):
        return pltpu.make_async_remote_copy(
            src_ref=src, dst_ref=dst, send_sem=send_tx.at[stage, d], recv_sem=recv_tx.at[stage, d],
            device_id=beyond("tx", d, n_tx), device_id_type=MESH)

    def rows(k, n):
        return pl.ds(pl.multiple_of(k * n, 8), n)

    def halo(k, src, dst, device):
        return pltpu.make_async_remote_copy(
            src_ref=src, dst_ref=dst, send_sem=send_h.at[k], recv_sem=recv_h.at[k], device_id=device, device_id_type=MESH)

    below, beside = lax.rem(ty + 1, n_ty), lax.rem(tx + 1, n_tx)
    halos = [halo(0, down, down_o, (below, tx)), halo(1, right, right_o, (ty, beside)), halo(2, corner, corner_o, (below, beside))]

    def ax(d):
        peer = lax.rem(tx + d, n_tx)
        return over_tx(0, d, cast.at[0, rows(peer, nx)], rax.at[d])

    def ay(d):
        peer = lax.rem(ty + d, n_ty)
        return over_ty(0, d, cast.at[1, rows(peer, ny)], ray.at[d])

    spread("tx", n_tx, lambda d: ax(d).start())
    spread("ty", n_ty, lambda d: ay(d).start())
    for h in halos:
        h.start()
    spread("tx", n_tx, lambda d: ax(d).wait())
    sx[...] = lax.fori_loop(1, n_tx, lambda d, t: t + rax[d].astype(f32), total[0, rows(tx, nx)])

    def bx(d):
        peer = lax.rem(ty + d, n_ty)
        return over_ty(1, d, sx.at[rows(peer, 8)], rbx.at[d])

    spread("ty", n_ty, lambda d: bx(d).start())
    spread("ty", n_ty, lambda d: ay(d).wait())
    sy[...] = lax.fori_loop(1, n_ty, lambda d, t: t + ray[d].astype(f32), total[1, rows(ty, ny)])

    def by(d):
        peer = lax.rem(tx + d, n_tx)
        return over_tx(1, d, sy.at[rows(peer, 8)], rby.at[d])

    spread("tx", n_tx, lambda d: by(d).start())
    spread("ty", n_ty, lambda d: bx(d).wait())
    gx[rows(ty, 8)] = scale * lax.fori_loop(1, n_ty, lambda d, t: t + rbx[d], sx[rows(ty, 8)])

    def cx(d):
        return over_ty(2, d, gx.at[rows(ty, 8)], gx.at[rows(ty, 8)])

    spread("ty", n_ty, lambda d: cx(d).start())
    spread("tx", n_tx, lambda d: by(d).wait())
    gy[rows(tx, 8)] = scale * lax.fori_loop(1, n_tx, lambda d, t: t + rby[d], sy[rows(tx, 8)])

    def cy(d):
        return over_tx(2, d, gy.at[rows(tx, 8)], gy.at[rows(tx, 8)])

    spread("tx", n_tx, lambda d: cy(d).start())
    spread("ty", n_ty, lambda d: cx(d).wait())
    hx[...] = gx[...].astype(bf)

    def dx(d):
        return over_tx(3, d, hx, probe_o.at[0, rows(tx, nx)])

    spread("tx", n_tx, lambda d: dx(d).start())
    probe_o[0, rows(tx, nx)] = hx[...]
    spread("tx", n_tx, lambda d: cy(d).wait())
    hy[...] = gy[...].astype(bf)

    def dy(d):
        return over_ty(3, d, hy, probe_o.at[1, rows(ty, ny)])

    spread("ty", n_ty, lambda d: dy(d).start())
    probe_o[1, rows(ty, ny)] = hy[...]
    spread("tx", n_tx, lambda d: dx(d).wait())
    spread("ty", n_ty, lambda d: dy(d).wait())
    for h in halos:
        h.wait()


def finish(total, down, right, corner, scale, n_ty, n_tx):
    nx, ny = 1024 // n_tx, 1024 // n_ty
    vmem = pl.BlockSpec(memory_space=pltpu.VMEM)
    hbm = pl.BlockSpec(memory_space=pl.ANY)
    dma = pltpu.SemaphoreType.DMA
    return pl.pallas_call(
        functools.partial(finish_kernel, n_ty, n_tx, scale),
        out_shape=[like((2, 1024, N), bf), like(down.shape, bf), like(right.shape, bf), like(corner.shape, bf)],
        in_specs=[vmem, hbm, hbm, hbm],
        out_specs=[vmem, hbm, hbm, hbm],
        scratch_shapes=[
            pltpu.VMEM((2, 1024, N), bf), pltpu.VMEM((n_tx, nx, N), bf), pltpu.VMEM((n_ty, ny, N), bf),
            pltpu.VMEM((nx, N), f32), pltpu.VMEM((ny, N), f32), pltpu.VMEM((n_ty, 8, N), f32), pltpu.VMEM((n_tx, 8, N), f32),
            pltpu.VMEM((nx, N), f32), pltpu.VMEM((ny, N), f32), pltpu.VMEM((nx, N), bf), pltpu.VMEM((ny, N), bf),
            dma((4, n_ty)), dma((4, n_ty)), dma((4, n_tx)), dma((4, n_tx)), dma((3,)), dma((3,))],
        compiler_params=pltpu.CompilerParams(collective_id=1, has_side_effects=True, vmem_limit_bytes=VMEM_LIMIT),
    )(total.reshape(2, 1024, N), down, right, corner)


def shift(value, d_ty, d_tx, n_ty, n_tx):
    pairs = []
    for y in range(n_ty):
        for x in range(n_tx):
            if 0 <= y + d_ty < n_ty and 0 <= x + d_tx < n_tx:
                pairs.append((y * n_tx + x, (y + d_ty) * n_tx + x + d_tx))
    return lax.ppermute(value, ("ty", "tx"), pairs)


def on_device(specimen, probe, amplitude, offsets):
    n_ty, n_tx = lax.axis_size("ty"), lax.axis_size("tx")
    positions = offsets.shape[0] * n_ty * n_tx
    right = shift(specimen[:, :, :N].astype(bf), 0, -1, n_ty, n_tx)
    lower = shift(specimen[:, :N, :].astype(bf), -1, 0, n_ty, n_tx)
    corner = shift(specimen[:, :N, :N].astype(bf), -1, -1, n_ty, n_tx)
    own = offsets.reshape(-1)
    slots = prepare(own, amplitude, n_ty)
    arrived = lax.all_to_all(slots, "ty", split_axis=0, concat_axis=0, tiled=True)
    everyone = gather_offsets(own, n_ty)
    tables = make_tables()
    arranged = arrange(probe)
    far, pat, inten = forward(everyone, specimen, right, lower, corner, arranged, tables, n_ty)
    main, down, rt, cn, total = backward(everyone, arranged, tables, arrived, far, pat, inten, n_ty)
    scale = float(probe.shape[1] / np.sqrt(positions))
    probe_grad, down, rt, cn = finish(total, down, rt, cn, scale, n_ty, n_tx)
    main = main.at[:, :N, :].add(down.astype(f32)).at[:, :, :N].add(rt.astype(f32)).at[:, :N, :N].add(cn.astype(f32))
    return (main, restore(probe_grad.reshape(probe.shape)).astype(f32))


def solution(mesh):
    in_specs = (P(None, "ty", "tx"), P(), P(("ty", "tx"), None, None), P(("ty", "tx"), None))
    out_specs = (P(None, "ty", "tx"), P())
    return jax.shard_map(on_device, mesh=mesh, in_specs=in_specs, out_specs=out_specs, check_vma=False)
```

time: 438 us -> 299 us (0.68)
  Pallas kernels: 28.2 us -> 260 us
  waiting for transfers between devices: 142 us -> 0.01 us
  starting transfers between devices: 151 us -> 14.1 us
  blocking collectives: 81.2 us -> 0 us
  between operations: 14.8 us -> 0.75 us
    pallas_call x1 -> x4, Pallas kernels: 17.2 us -> 249 us  [the longest x1 81.7 us: finish(): pl.pallas_call(functools.partial(finish_kernel, n_ty, n_tx, scale), out_s...]
    psum x1 -> x0, waiting for transfers between devices: 142 us -> none  [on_device(): lax.psum(total, ('ty', 'tx')) * (probe.shape[1] / np.sqrt(positions))]
    ppermute x6 -> x3, starting transfers between devices: 142 us -> 5.44 us  [shift(): return lax.ppermute(value, ('ty', 'tx'), pairs)]
    unnamed x1 -> x0, blocking collectives: 81.2 us -> none
    scatter-add x3, other arithmetic: 1.02 us -> 6.64 us  [on_device(): main.at[:, :N, :].add(down.astype(f32)).at[:, :, :N].add(rt.astype(f32))]
  transfers between devices with their start and end apart: 8 -> 4, of which waited for: 1 -> 0; matrix products, arithmetic and copies ran while one was open for 2% -> 3% of each run, Pallas kernels for 0% -> 41%
where the time goes in v2:
time: 299 us; the launch traced here: 298 us
  Pallas kernels  260 us (87%)
  starting transfers between devices  14.1 us (5%)
  local copies, waits for them, and re-layouts  12.7 us (4%)
  other arithmetic  10.7 us (4%)
    pallas_call x1, Pallas kernels, finish(): pl.pallas_call(functools.partial(finish_kernel, n_ty, n_tx, scale), out_s...  81.7 us
    pallas_call x1, Pallas kernels, gather_offsets(): pl.pallas_call(functools.partial(gather_kernel, n_ty), out_shape=like((n_...  81.7 us
    pallas_call x1, Pallas kernels, backward(): pl.pallas_call(backward_kernel, out_shape=[like((2, 512, 1024), f32), lik...  45.4 us
    pallas_call x1, Pallas kernels, forward(): pl.pallas_call(forward_kernel, out_shape=[like((sources, 2, 4, 2, 2, 128,...  40.3 us
    pallas_call x1, Pallas kernels, prepare(): pl.pallas_call(prep_kernel, out_shape=jax.ShapeDtypeStruct((sources, 2, N...  11 us
    all_to_all x1, starting transfers between devices, on_device(): lax.all_to_all(slots, 'ty', split_axis=0, concat_axis=0, tiled=True)  8.65 us
    scatter-add x3, other arithmetic, on_device(): main.at[:, :N, :].add(down.astype(f32)).at[:, :, :N].add(rt.astype(f32))  6.64 us
  transfers between devices with their start and end apart: 4, of which 0 were waited for; matrix products, arithmetic and copies ran while one was open for 3% of the time, Pallas kernels for 41%

profile of v2, /device:TPU:1, one launch (start us, length us, event | category | flops | bytes accessed | tf_op | source)
XLA Modules:
  0.0 298.4 jit_solution(13089849056943172226)
XLA Ops:
  0.6 0.8 copy.12
  1.4 0.6 reshape.150.off
  2.0 11.0 %shard_map.78 = bf16[16,2,256,256]{3,2,1,0:T(8,128)(2,1)} custom-call(s32[24]{0:T(128)} %reshape.150.off, f32[12,256,256]{2,1,0:T(8,128)} %amp.1, bf16[256,256]{1,0:T(8,128)(2,1)} %constant.109.clone.perm), custom_call_target="tpu_custom_call" | custom-call | tf_op jit(solution)/shard_map/pallas_call | solution.py:95
  13.0 8.6 %all-to-all-start = ((bf16[16,2,256,256]{3,2,1,0:T(8,128)(2,1)}), bf16[16,2,256,256]{3,2,1,0:T(8,128)(2,1)}, u32[]{:S(2)}, u32[]{:S(2)}) async-start(bf16[16,2,256,256]{3,2,1,0:T(8,128)(2,1)} %shard_map.78), calls=%async_computation | async-start | bytes 8388608 | tf_op jit(solution)/shard_map/all_to_all | solution.py:525
  21.7 2.5 convert.8
  24.3 1.3 collective-permute-start.1
  25.6 0.9 slice.115
  26.4 2.9 collective-permute-start
  29.3 1.3 collective-permute-start.2
  30.7 0.6 scatter.4.own
  31.3 81.7 %shard_map.77 = s32[16,8,128]{2,1,0:T(8,128)} custom-call(s32[8,128]{1,0:T(8,128)} %scatter.4.own), custom_call_target="tpu_custom_call" | custom-call | tf_op jit(solution)/shard_map/pallas_call | solution.py:379
  113.0 0.9 slice_reduce_fusion
  113.9 0.7 reshape_squeeze.3.off
  114.6 2.5 reshape.148
  117.1 1.6 copy.13
  118.7 40.3 %shard_map.79 = (f32[16,2,4,2,2,128,256]{6,5,4,3,2,1,0:T(8,128)}, f32[16,2,2,256,256]{4,3,2,1,0:T(8,128)}, f32[16,2,2,128,256]{4,3,2,1,0:T(8,128)}) custom-call(s32[384]{0:T(512)} %reshape_squeeze.3.off, f32[2,512,1024]{2,1,0:T(8,128)} %spec.1, bf16[2,512,256]{2,1,0:T(8,128)(2,1)} %collective-permute-done.right, ...), custom_call_target="tpu_custom_call" | custom-call | flops 17179869184 | bytes 104857600 | tf_op jit(solution)/shard_map/pallas_call | solution.py:323
  159.0 45.4 %shard_map.80 = (f32[2,512,1024]{2,1,0:T(8,128)}, bf16[2,256,1024]{2,1,0:T(8,128)(2,1)}, bf16[2,512,256]{2,1,0:T(8,128)(2,1)}, bf16[2,256,256]{2,1,0:T(8,128)(2,1)}, f32[2,4,256,256]{3,2,1,0:T(8,128)}) custom-call(s32[384]{0:T(512)} %reshape_squeeze.3.off, f32[2,4,256,256]{3,2,1,0:T(8,128)} %bitcast.11, bf16[8,256,256]{2,1,0:T(8,128)(2,1)} %constant.110.clone.tab, ...), custom_call_target="tpu_custom_call" | custom-call | flops 17179869184 | bytes 104857600 | tf_op jit(solution)/shard_map/pallas_call | solution.py:337
  204.4 81.7 %shard_map.81 = (bf16[2,1024,256]{2,1,0:T(8,128)(2,1)}, bf16[2,256,1024]{2,1,0:T(8,128)(2,1)}, bf16[2,512,256]{2,1,0:T(8,128)(2,1)}, bf16[2,256,256]{2,1,0:T(8,128)(2,1)}) custom-call(f32[2,1024,256]{2,1,0:T(8,128)} %bitcast.12, bf16[2,256,1024]{2,1,0:T(8,128)(2,1)} %get-tuple-element.67.down, bf16[2,512,256]{2,1,0:T(8,128)(2,1)} %get-tuple-element.68.right, ...), custom_call_target="tpu_custom_call" | custom-call | tf_op jit(solution)/shard_map/pallas_call | solution.py:494
  286.1 1.5 convert_bitcast_fusion
  287.6 1.6 copy.15
  289.3 2.4 reshape.152
  291.7 3.4 %add_dynamic-update-slice_fusion = f32[2,512,1024]{2,1,0:T(8,128)} fusion(f32[2,512,1024]{2,1,0:T(8,128)} %get-tuple-element.65, bf16[2,256,1024]{2,1,0:T(8,128)(2,1)S(1)} %copy-done), kind=kLoop, calls=%fused_computation.1 | loop fusion | flops 1048576 | bytes 5242880 | tf_op jit(solution)/shard_map/scatter-add | solution.py:533
  295.1 2.4 constant_dynamic-update-slice_fusion
  297.5 0.9 fusion
  (13 shorter events, 0.2 us)
Async XLA Ops:
  13.0 146.0 %all-to-all-start = ((bf16[16,2,256,256]{3,2,1,0:T(8,128)(2,1)}), bf16[16,2,256,256]{3,2,1,0:T(8,128)(2,1)}, u32[]{:S(2)}, u32[]{:S(2)}) async-start(bf16[16,2,256,256]{3,2,1,0:T(8,128)(2,1)} %shard_map.78), calls=%async_computation | async-start | bytes 8388608 | tf_op jit(solution)/shard_map/all_to_all | solution.py:525
  24.3 94.4 %collective-permute-start.1 = (bf16[2,256,1024]{2,1,0:T(8,128)(2,1)S(1)}, bf16[2,256,1024]{2,1,0:T(8,128)(2,1)}, u32[]{:S(2)}, u32[]{:S(2)}) collective-permute-start(bf16[2,256,1024]{2,1,0:T(8,128)(2,1)S(1)} %slice.116), channel_id=1, source_target_pairs={{8,0},{9,1},{10,2},{11,3},{12,4},{13,5},{14,6},{15,7},{16,8},{17,9... | collective-permute-start | bytes 3145736 | tf_op jit(solution)/shard_map/ppermute | solution.py:514
  26.4 92.2 %collective-permute-start = (bf16[2,512,256]{2,1,0:T(8,128)(2,1)}, bf16[2,512,256]{2,1,0:T(8,128)(2,1)}, u32[]{:S(2)}, u32[]{:S(2)}) collective-permute-start(bf16[2,512,256]{2,1,0:T(8,128)(2,1)} %slice.115), channel_id=1, source_target_pairs={{1,0},{2,1},{3,2},{4,3},{5,4},{6,5},{7,6},{9,8},{10,9},{11,10},{12... | collective-permute-start | bytes 1572872 | tf_op jit(solution)/shard_map/ppermute | solution.py:514
  29.3 89.3 %collective-permute-start.2 = (bf16[2,256,256]{2,1,0:T(8,128)(2,1)S(1)}, bf16[2,256,256]{2,1,0:T(8,128)(2,1)}, u32[]{:S(2)}, u32[]{:S(2)}) collective-permute-start(bf16[2,256,256]{2,1,0:T(8,128)(2,1)S(1)} %slice.117), channel_id=1, source_target_pairs={{9,0},{10,1},{11,2},{12,3},{13,4},{14,5},{15,6},{17,8},{18,9},{19,... | collective-permute-start | bytes 786440 | tf_op jit(solution)/shard_map/ppermute | solution.py:514
  287.6 4.1 %copy-start = (bf16[2,256,1024]{2,1,0:T(8,128)(2,1)S(1)}, bf16[2,256,1024]{2,1,0:T(8,128)(2,1)}, u32[]{:S(2)}) copy-start(bf16[2,256,1024]{2,1,0:T(8,128)(2,1)} %get-tuple-element.70) | copy-start | bytes 3145732
  291.7 3.4 %copy-start.1 = (bf16[2,512,256]{2,1,0:T(8,128)(2,1)S(1)}, bf16[2,512,256]{2,1,0:T(8,128)(2,1)}, u32[]{:S(2)}) copy-start(bf16[2,512,256]{2,1,0:T(8,128)(2,1)} %get-tuple-element.71) | copy-start | bytes 1572868
  291.7 5.8 %copy-start.2 = (bf16[2,256,256]{2,1,0:T(8,128)(2,1)S(1)}, bf16[2,256,256]{2,1,0:T(8,128)(2,1)}, u32[]{:S(2)}) copy-start(bf16[2,256,256]{2,1,0:T(8,128)(2,1)} %get-tuple-element.72) | copy-start | bytes 786436

commit v3 on v2

--- a/solution.py
+++ b/solution.py
@@ -17,6 +17,8 @@
 TILE_C = 1024
 POS = 12
 VMEM_LIMIT = 60 * 2**20
+ROWS = 2048
+PIECES = 4
 MESH = pl.DeviceIdType.MESH
 S = 2
 B = 16 // S
@@ -72,35 +74,29 @@
     return np.eye(N)[order].astype(ml_dtypes.bfloat16)
 
 
-def slot_of(off, i):
-    tile = off[2 * i] // TILE_R
-    rank = jnp.int32(0)
-    for j in range(POS):
-        same = (off[2 * j] // TILE_R == tile) & (j < i)
-        rank = rank + same.astype(jnp.int32)
-    return tile, rank
-
-
-def prep_kernel(off, amp, perm, out):
-    a = amp[0].astype(bf)
-    a = dot(perm[...], a).astype(bf)
-    out[0, 0] = lax.dot_general(a, perm[...], (((1,), (1,)), ((), ())), preferred_element_type=f32).astype(bf)
+def prep_kernel(off, amp, perm, out, buf, sem):
+    copies = []
+    for i in range(POS):
+        a = dot(perm[...], amp[i].astype(bf)).astype(bf)
+        buf[i] = lax.dot_general(a, perm[...], (((1,), (1,)), ((), ())), preferred_element_type=f32).astype(bf)
+        tile = off[2 * i] // TILE_R
+        rank = jnp.int32(0)
+        for j in range(i):
+            rank = rank + (off[2 * j] // TILE_R == tile).astype(jnp.int32)
+        copies.append(pltpu.make_async_copy(buf.at[i], out.at[tile, rank], sem.at[i]))
+        copies[i].start()
+    for copy in copies:
+        copy.wait()
 
 
 def prepare(off, amplitude, sources):
-    def place(i, off):
-        tile, rank = slot_of(off, i)
-        return (tile, rank, 0, 0)
-
     return pl.pallas_call(
         prep_kernel,
         out_shape=jax.ShapeDtypeStruct((sources, 2, N, N), bf),
-        grid_spec=pltpu.PrefetchScalarGridSpec(
-            num_scalar_prefetch=1,
-            grid=(POS,),
-            in_specs=[pl.BlockSpec((1, N, N), lambda i, o: (i, 0, 0)), pl.BlockSpec((N, N), lambda i, o: (0, 0))],
-            out_specs=pl.BlockSpec((1, 1, N, N), place),
-        ),
+        in_specs=[pl.BlockSpec(memory_space=pltpu.SMEM), pl.BlockSpec(memory_space=pltpu.VMEM), pl.BlockSpec(memory_space=pltpu.VMEM)],
+        out_specs=pl.BlockSpec(memory_space=pl.ANY),
+        scratch_shapes=[pltpu.VMEM((POS, N, N), bf), pltpu.SemaphoreType.DMA((POS,))],
+        compiler_params=pltpu.CompilerParams(vmem_limit_bytes=VMEM_LIMIT),
     )(off, amplitude, parity_matrix())
 
 
@@ -265,7 +261,7 @@
                 p1(probe.at[:, m], pat.at[0, q], A.at[q, m])
 
 
-def backward_kernel(off, probe, tab, amp, far, pat, inten, main_o, down_o, right_o, corner_o, total, grid, fac, C, G, grad):
+def backward_kernel(off, probe, tab, amp, far, pat, inten, main_o, down_o, right_o, corner_o, total_o, grid, total, fac, C, G, grad):
     s = pl.program_id(0)
 
     @pl.when(s == 0)
@@ -305,6 +301,11 @@
                 else:
                     right_o[c, :, l2] = grid[c, t, :512].astype(bf)
                     corner_o[c, :, l2] = grid[c, t, 512:].astype(bf)
+            for m in range(4):
+                for i in range(32):
+                    for t in range(2):
+                        ds = pl.ds(128 * (i % 2) + row0(i // 2), 8, stride=S)
+                        total_o[c, m, t, ds] = total[c, m, 8 * i:8 * i + 8, t * H:t * H + H]
 
 
 def whole(*shape):
@@ -336,12 +337,12 @@
 def backward(off, probe, tab, amp, far, pat, inten, sources):
     return pl.pallas_call(
         backward_kernel,
-        out_shape=[like((2, 512, 1024), f32), like((2, 256, 1024), bf), like((2, 512, 256), bf), like((2, 256, 256), bf), like((2, 4, 256, 256), f32)],
+        out_shape=[like((2, 512, 1024), f32), like((2, 256, 1024), bf), like((2, 512, 256), bf), like((2, 256, 256), bf), like((2, 4, 2, 256, 128), f32)],
         grid_spec=pltpu.PrefetchScalarGridSpec(
             num_scalar_prefetch=1, grid=(sources,),
             in_specs=[whole(2, 4, 256, 256), whole(8, 256, 256), each(2, 256, 256), each(2, 4, 2, 2, 128, 256), each(2, 2, 256, 256), each(2, 2, 128, 256)],
-            out_specs=[whole(2, 512, 1024), whole(2, 256, 1024), whole(2, 512, 256), whole(2, 256, 256), whole(2, 4, 256, 256)],
-            scratch_shapes=[pltpu.VMEM((2, 10, 768, 128), f32), pltpu.VMEM((2, 2, 128, 256), f32), pltpu.VMEM((2, 4, 2, 256, 256), bf),
+            out_specs=[whole(2, 512, 1024), whole(2, 256, 1024), whole(2, 512, 256), whole(2, 256, 256), whole(2, 4, 2, 256, 128)],
+            scratch_shapes=[pltpu.VMEM((2, 10, 768, 128), f32), pltpu.VMEM((2, 4, 256, 256), f32), pltpu.VMEM((2, 2, 128, 256), f32), pltpu.VMEM((2, 4, 2, 256, 256), bf),
                             pltpu.VMEM((2, 4, 2, 256, 256), bf), pltpu.VMEM((2, 2, 256, 256), f32)]),
         compiler_params=pltpu.CompilerParams(vmem_limit_bytes=VMEM_LIMIT),
         cost_estimate=pl.CostEstimate(flops=32 * 2**29, bytes_accessed=100 * 2**20, transcendentals=0),
@@ -390,7 +391,7 @@
 def finish_kernel(n_ty, n_tx, scale, total, down, right, corner, probe_o, down_o, right_o, corner_o,
                   cast, rax, ray, sx, sy, rbx, rby, gx, gy, hx, hy, send_ty, recv_ty, send_tx, recv_tx, send_h, recv_h):
     ty, tx = lax.axis_index("ty"), lax.axis_index("tx")
-    nx, ny = 1024 // n_tx, 1024 // n_ty
+    nx, ny, sub = ROWS // n_tx, ROWS // n_ty, ROWS // n_tx // n_ty
     barrier = pltpu.get_barrier_semaphore()
 
     def greet(device):
@@ -413,14 +414,16 @@
             device_id=beyond("tx", d, n_tx), device_id_type=MESH)
 
     def rows(k, n):
-        return pl.ds(pl.multiple_of(k * n, 8), n)
+        return pl.ds(pl.multiple_of(k * n, 16), n)
 
     def halo(k, src, dst, device):
         return pltpu.make_async_remote_copy(
             src_ref=src, dst_ref=dst, send_sem=send_h.at[k], recv_sem=recv_h.at[k], device_id=device, device_id_type=MESH)
 
     below, beside = lax.rem(ty + 1, n_ty), lax.rem(tx + 1, n_tx)
-    halos = [halo(0, down, down_o, (below, tx)), halo(1, right, right_o, (ty, beside)), halo(2, corner, corner_o, (below, beside))]
+    part = N // PIECES
+    pieces = [halo(k, down.at[:, k * part:k * part + part], down_o.at[:, k * part:k * part + part], (below, tx)) for k in range(PIECES)]
+    halos = pieces + [halo(PIECES, right, right_o, (ty, beside)), halo(PIECES + 1, corner, corner_o, (below, beside))]
 
     def ax(d):
         peer = lax.rem(tx + d, n_tx)
@@ -432,14 +435,13 @@
 
     spread("tx", n_tx, lambda d: ax(d).start())
     spread("ty", n_ty, lambda d: ay(d).start())
-    for h in halos:
-        h.start()
+    halos[0].start()
     spread("tx", n_tx, lambda d: ax(d).wait())
     sx[...] = lax.fori_loop(1, n_tx, lambda d, t: t + rax[d].astype(f32), total[0, rows(tx, nx)])
 
     def bx(d):
         peer = lax.rem(ty + d, n_ty)
-        return over_ty(1, d, sx.at[rows(peer, 8)], rbx.at[d])
+        return over_ty(1, d, sx.at[rows(peer, sub)], rbx.at[d])
 
     spread("ty", n_ty, lambda d: bx(d).start())
     spread("ty", n_ty, lambda d: ay(d).wait())
@@ -447,23 +449,25 @@
 
     def by(d):
         peer = lax.rem(tx + d, n_tx)
-        return over_tx(1, d, sy.at[rows(peer, 8)], rby.at[d])
+        return over_tx(1, d, sy.at[rows(peer, sub)], rby.at[d])
 
     spread("tx", n_tx, lambda d: by(d).start())
+    halos[1].start()
     spread("ty", n_ty, lambda d: bx(d).wait())
-    gx[rows(ty, 8)] = scale * lax.fori_loop(1, n_ty, lambda d, t: t + rbx[d], sx[rows(ty, 8)])
+    gx[rows(ty, sub)] = scale * lax.fori_loop(1, n_ty, lambda d, t: t + rbx[d], sx[rows(ty, sub)])
 
     def cx(d):
-        return over_ty(2, d, gx.at[rows(ty, 8)], gx.at[rows(ty, 8)])
+        return over_ty(2, d, gx.at[rows(ty, sub)], gx.at[rows(ty, sub)])
 
     spread("ty", n_ty, lambda d: cx(d).start())
     spread("tx", n_tx, lambda d: by(d).wait())
-    gy[rows(tx, 8)] = scale * lax.fori_loop(1, n_tx, lambda d, t: t + rby[d], sy[rows(tx, 8)])
+    gy[rows(tx, sub)] = scale * lax.fori_loop(1, n_tx, lambda d, t: t + rby[d], sy[rows(tx, sub)])
 
     def cy(d):
-        return over_tx(2, d, gy.at[rows(tx, 8)], gy.at[rows(tx, 8)])
+        return over_tx(2, d, gy.at[rows(tx, sub)], gy.at[rows(tx, sub)])
 
     spread("tx", n_tx, lambda d: cy(d).start())
+    halos[2].start()
     spread("ty", n_ty, lambda d: cx(d).wait())
     hx[...] = gx[...].astype(bf)
 
@@ -479,6 +483,8 @@
         return over_ty(3, d, hy, probe_o.at[1, rows(ty, ny)])
 
     spread("ty", n_ty, lambda d: dy(d).start())
+    for h in halos[3:]:
+        h.start()
     probe_o[1, rows(ty, ny)] = hy[...]
     spread("tx", n_tx, lambda d: dx(d).wait())
     spread("ty", n_ty, lambda d: dy(d).wait())
@@ -487,22 +493,22 @@
 
 
 def finish(total, down, right, corner, scale, n_ty, n_tx):
-    nx, ny = 1024 // n_tx, 1024 // n_ty
+    nx, ny, sub = ROWS // n_tx, ROWS // n_ty, ROWS // n_tx // n_ty
     vmem = pl.BlockSpec(memory_space=pltpu.VMEM)
     hbm = pl.BlockSpec(memory_space=pl.ANY)
     dma = pltpu.SemaphoreType.DMA
     return pl.pallas_call(
         functools.partial(finish_kernel, n_ty, n_tx, scale),
-        out_shape=[like((2, 1024, N), bf), like(down.shape, bf), like(right.shape, bf), like(corner.shape, bf)],
+        out_shape=[like((2, ROWS, H), bf), like(down.shape, bf), like(right.shape, bf), like(corner.shape, bf)],
         in_specs=[vmem, hbm, hbm, hbm],
         out_specs=[vmem, hbm, hbm, hbm],
         scratch_shapes=[
-            pltpu.VMEM((2, 1024, N), bf), pltpu.VMEM((n_tx, nx, N), bf), pltpu.VMEM((n_ty, ny, N), bf),
-            pltpu.VMEM((nx, N), f32), pltpu.VMEM((ny, N), f32), pltpu.VMEM((n_ty, 8, N), f32), pltpu.VMEM((n_tx, 8, N), f32),
-            pltpu.VMEM((nx, N), f32), pltpu.VMEM((ny, N), f32), pltpu.VMEM((nx, N), bf), pltpu.VMEM((ny, N), bf),
-            dma((4, n_ty)), dma((4, n_ty)), dma((4, n_tx)), dma((4, n_tx)), dma((3,)), dma((3,))],
+            pltpu.VMEM((2, ROWS, H), bf), pltpu.VMEM((n_tx, nx, H), bf), pltpu.VMEM((n_ty, ny, H), bf),
+            pltpu.VMEM((nx, H), f32), pltpu.VMEM((ny, H), f32), pltpu.VMEM((n_ty, sub, H), f32), pltpu.VMEM((n_tx, sub, H), f32),
+            pltpu.VMEM((nx, H), f32), pltpu.VMEM((ny, H), f32), pltpu.VMEM((nx, H), bf), pltpu.VMEM((ny, H), bf),
+            dma((4, n_ty)), dma((4, n_ty)), dma((4, n_tx)), dma((4, n_tx)), dma((PIECES + 2,)), dma((PIECES + 2,))],
         compiler_params=pltpu.CompilerParams(collective_id=1, has_side_effects=True, vmem_limit_bytes=VMEM_LIMIT),
-    )(total.reshape(2, 1024, N), down, right, corner)
+    )(total.reshape(2, ROWS, H), down, right, corner)
 
 
 def shift(value, d_ty, d_tx, n_ty, n_tx):
@@ -517,21 +523,30 @@
 def on_device(specimen, probe, amplitude, offsets):
     n_ty, n_tx = lax.axis_size("ty"), lax.axis_size("tx")
     positions = offsets.shape[0] * n_ty * n_tx
-    right = shift(specimen[:, :, :N].astype(bf), 0, -1, n_ty, n_tx)
-    lower = shift(specimen[:, :N, :].astype(bf), -1, 0, n_ty, n_tx)
-    corner = shift(specimen[:, :N, :N].astype(bf), -1, -1, n_ty, n_tx)
     own = offsets.reshape(-1)
+    half = (specimen[:, :, :N].astype(bf), specimen[:, :N, :].astype(bf))
+    everyone = gather_offsets(own, n_ty)
+    everyone, (side, top) = lax.optimization_barrier((everyone, half))
+    lower = shift(top, -1, 0, n_ty, n_tx)
+    right = shift(side, 0, -1, n_ty, n_tx)
+    corner = shift(top[:, :, :N], -1, -1, n_ty, n_tx)
     slots = prepare(own, amplitude, n_ty)
+    slots, everyone = lax.optimization_barrier((slots, everyone))
     arrived = lax.all_to_all(slots, "ty", split_axis=0, concat_axis=0, tiled=True)
-    everyone = gather_offsets(own, n_ty)
     tables = make_tables()
     arranged = arrange(probe)
     far, pat, inten = forward(everyone, specimen, right, lower, corner, arranged, tables, n_ty)
     main, down, rt, cn, total = backward(everyone, arranged, tables, arrived, far, pat, inten, n_ty)
     scale = float(probe.shape[1] / np.sqrt(positions))
     probe_grad, down, rt, cn = finish(total, down, rt, cn, scale, n_ty, n_tx)
-    main = main.at[:, :N, :].add(down.astype(f32)).at[:, :, :N].add(rt.astype(f32)).at[:, :N, :N].add(cn.astype(f32))
-    return (main, restore(probe_grad.reshape(probe.shape)).astype(f32))
+
+    def spot(piece):
+        rows, cols = TILE_R - piece.shape[1], TILE_C - piece.shape[2]
+        return jnp.pad(piece.astype(f32), ((0, 0), (0, rows), (0, cols)))
+
+    object_grad = main + spot(down) + spot(rt) + spot(cn)
+    probe_grad = jnp.swapaxes(probe_grad.reshape(2, 4, 2, N, H), 2, 3).reshape(probe.shape).astype(f32)
+    return (object_grad, probe_grad)
 
 
 def solution(mesh):

time: 299 us -> 289 us (0.967); the launches traced: 298 us -> 285 us
  Pallas kernels: 260 us -> 183 us
  waiting for transfers between devices: 0.01 us -> 70 us
  local copies, waits for them, and re-layouts: 12.7 us -> 8.68 us
    ppermute x3, waiting for transfers between devices: 0.01 us -> 70 us  [shift(): return lax.ppermute(value, ('ty', 'tx'), pairs)]
    pallas_call x1, Pallas kernels: 81.7 us -> 11.9 us  [gather_offsets(): pl.pallas_call(functools.partial(gather_kernel, n_ty), out_shape=like((n_...]
    pallas_call x1, Pallas kernels: 81.7 us -> 57.6 us  [finish(): pl.pallas_call(functools.partial(finish_kernel, n_ty, n_tx, scale), out_s...]
    pallas_call x1, Pallas kernels: 45.4 us -> 60 us  [backward(): pl.pallas_call(backward_kernel, out_shape=[like((2, 512, 1024), f32), lik...]
    pallas_call x1, Pallas kernels: 40.3 us -> 49.5 us  [forward(): pl.pallas_call(forward_kernel, out_shape=[like((sources, 2, 4, 2, 2, 128,...]
    pallas_call x1, Pallas kernels: 11 us -> 3.75 us  [prepare(): pl.pallas_call(prep_kernel, out_shape=jax.ShapeDtypeStruct((sources, 2, N...]
    scatter-add x3 -> x0, other arithmetic: 6.64 us -> none  [on_device(): main.at[:, :N, :].add(down.astype(f32)).at[:, :, :N].add(rt.astype(f32))]
    add x0 -> x1, other arithmetic: none -> 5.65 us  [on_device(): object_grad = main + spot(down) + spot(rt) + spot(cn)]
  transfers between devices with their start and end apart: 4 -> 4, of which waited for: 0 -> 2; matrix products, arithmetic and copies ran while one was open for 3% -> 1% of each run, Pallas kernels for 41% -> 17%
where the time goes in v3:
time: 289 us; the launch traced here: 285 us
  Pallas kernels  183 us (63%)
  waiting for transfers between devices  70 us (24%)
  starting transfers between devices  11.8 us (4%)
  other arithmetic  10.9 us (4%)
  local copies, waits for them, and re-layouts  8.68 us (3%)
    ppermute x3, waiting for transfers between devices, shift(): return lax.ppermute(value, ('ty', 'tx'), pairs)  70 us
    pallas_call x1, Pallas kernels, backward(): pl.pallas_call(backward_kernel, out_shape=[like((2, 512, 1024), f32), lik...  60 us
    pallas_call x1, Pallas kernels, finish(): pl.pallas_call(functools.partial(finish_kernel, n_ty, n_tx, scale), out_s...  57.6 us
    pallas_call x1, Pallas kernels, forward(): pl.pallas_call(forward_kernel, out_shape=[like((sources, 2, 4, 2, 2, 128,...  49.5 us
    pallas_call x1, Pallas kernels, gather_offsets(): pl.pallas_call(functools.partial(gather_kernel, n_ty), out_shape=like((n_...  11.9 us
    ppermute x3, starting transfers between devices, shift(): return lax.ppermute(value, ('ty', 'tx'), pairs)  6.76 us
  transfers between devices with their start and end apart: 4, of which 2 were waited for; matrix products, arithmetic and copies ran while one was open for 1% of the time, Pallas kernels for 17%

profile of v3, /device:TPU:1, one launch (start us, length us, event | category | flops | bytes accessed | tf_op | source)
XLA Modules:
  0.0 284.8 jit_solution(12050438162728524137)
XLA Ops:
  0.6 0.8 copy.12
  1.4 0.1 reshape.55
  1.5 0.6 reshape.54.off
  2.1 2.5 convert.13
  4.6 0.9 slice.34
  5.5 0.1 slice.35
  5.6 0.6 scatter.4.own
  6.2 11.9 %shard_map.78 = s32[16,8,128]{2,1,0:T(8,128)} custom-call(s32[8,128]{1,0:T(8,128)} %scatter.4.own), custom_call_target="tpu_custom_call" | custom-call | tf_op jit(solution)/shard_map/pallas_call | solution.py:380
  18.0 0.9 slice_reduce_fusion
  18.9 0.7 reshape_squeeze.3.off
  19.6 3.7 %shard_map.77 = bf16[16,2,256,256]{3,2,1,0:T(8,128)(2,1)} custom-call(s32[24]{0:T(128)} %reshape.54.off, f32[12,256,256]{2,1,0:T(8,128)} %amp.1, bf16[256,256]{1,0:T(8,128)(2,1)} %constant.35.clone.perm), custom_call_target="tpu_custom_call" | custom-call | tf_op jit(solution)/shard_map/pallas_call | solution.py:93
  23.3 5.0 %all-to-all-start = ((bf16[16,2,256,256]{3,2,1,0:T(8,128)(2,1)}), bf16[16,2,256,256]{3,2,1,0:T(8,128)(2,1)}, u32[]{:S(2)}, u32[]{:S(2)}) async-start(bf16[16,2,256,256]{3,2,1,0:T(8,128)(2,1)} %shard_map.77), calls=%async_computation | async-start | bytes 8388608 | tf_op jit(solution)/shard_map/all_to_all | solution.py:535
  28.3 1.3 collective-permute-start.1
  29.6 4.0 %collective-permute-start = (bf16[2,512,256]{2,1,0:T(8,128)(2,1)}, bf16[2,512,256]{2,1,0:T(8,128)(2,1)}, u32[]{:S(2)}, u32[]{:S(2)}) collective-permute-start(bf16[2,512,256]{2,1,0:T(8,128)(2,1)} %slice.34), channel_id=1, source_target_pairs={{1,0},{2,1},{3,2},{4,3},{5,4},{6,5},{7,6},{9,8},{10,9},{11,10},{12... | collective-permute-start | bytes 1572872 | tf_op jit(solution)/shard_map/ppermute | solution.py:520
  33.7 1.5 collective-permute-start.2
  35.2 2.5 reshape.56
  37.7 1.6 copy.14
  39.3 7.9 %collective-permute-done.2.corner = bf16[2,256,256]{2,1,0:T(8,128)(2,1)} collective-permute-done((bf16[2,256,256]{2,1,0:T(8,128)(2,1)S(1)}, bf16[2,256,256]{2,1,0:T(8,128)(2,1)}, u32[]{:S(2)}, u32[]{:S(2)}) %collective-permute-start.2) | collective-permute-done | bytes 262176 | tf_op jit(solution)/shard_map/ppermute | solution.py:520
  47.1 62.2 %collective-permute-done.1.lower = bf16[2,256,1024]{2,1,0:T(8,128)(2,1)} collective-permute-done((bf16[2,256,1024]{2,1,0:T(8,128)(2,1)S(1)}, bf16[2,256,1024]{2,1,0:T(8,128)(2,1)}, u32[]{:S(2)}, u32[]{:S(2)}) %collective-permute-start.1) | collective-permute-done | bytes 1048608 | tf_op jit(solution)/shard_map/ppermute | solution.py:520
  109.3 49.5 %shard_map.79 = (f32[16,2,4,2,2,128,256]{6,5,4,3,2,1,0:T(8,128)}, f32[16,2,2,256,256]{4,3,2,1,0:T(8,128)}, f32[16,2,2,128,256]{4,3,2,1,0:T(8,128)}) custom-call(s32[384]{0:T(512)} %reshape_squeeze.3.off, f32[2,512,1024]{2,1,0:T(8,128)} %spec.1, bf16[2,512,256]{2,1,0:T(8,128)(2,1)} %collective-permute-done.right, ...), custom_call_target="tpu_custom_call" | custom-call | flops 17179869184 | bytes 104857600 | tf_op jit(solution)/shard_map/pallas_call | solution.py:324
  158.8 60.0 %shard_map.80 = (f32[2,512,1024]{2,1,0:T(8,128)}, bf16[2,256,1024]{2,1,0:T(8,128)(2,1)}, bf16[2,512,256]{2,1,0:T(8,128)(2,1)}, bf16[2,256,256]{2,1,0:T(8,128)(2,1)}, f32[2,4,2,256,128]{4,3,2,1,0:T(8,128)}) custom-call(s32[384]{0:T(512)} %reshape_squeeze.3.off, f32[2,4,256,256]{3,2,1,0:T(8,128)} %bitcast.15, bf16[8,256,256]{2,1,0:T(8,128)(2,1)} %constant.36.clone.tab, ...), custom_call_target="tpu_custom_call" | custom-call | flops 17179869184 | bytes 104857600 | tf_op jit(solution)/shard_map/pallas_call | solution.py:338
  218.8 57.6 %shard_map.81 = (bf16[2,2048,128]{2,1,0:T(8,128)(2,1)}, bf16[2,256,1024]{2,1,0:T(8,128)(2,1)}, bf16[2,512,256]{2,1,0:T(8,128)(2,1)}, bf16[2,256,256]{2,1,0:T(8,128)(2,1)}) custom-call(f32[2,2048,128]{2,1,0:T(8,128)} %bitcast.16, bf16[2,256,1024]{2,1,0:T(8,128)(2,1)} %get-tuple-element.41.down, bf16[2,512,256]{2,1,0:T(8,128)(2,1)} %get-tuple-element.42.right, ...), custom_call_target="tpu_custom_call" | custom-call | tf_op jit(solution)/shard_map/pallas_call | solution.py:500
  276.4 2.7 copy_bitcast_fusion
  279.1 5.7 %convert_add_fusion = f32[2,512,1024]{2,1,0:T(8,128)} fusion(f32[2,512,1024]{2,1,0:T(8,128)} %get-tuple-element.39, bf16[2,256,256]{2,1,0:T(8,128)(2,1)} %get-tuple-element.46, bf16[2,512,256]{2,1,0:T(8,128)(2,1)} %get-tuple-element.45, bf16[2,256,1024]{2,1,0:T(8,128)(2,1)} %get-tuple-element.44), kind=kLoop, calls=%fused_computation | loop fusion | flops 6291456 | bytes 10223616 | tf_op jit(solution)/shard_map/add | solution.py:547
  (3 shorter events, 0.0 us)
Async XLA Ops:
  23.3 135.5 %all-to-all-start = ((bf16[16,2,256,256]{3,2,1,0:T(8,128)(2,1)}), bf16[16,2,256,256]{3,2,1,0:T(8,128)(2,1)}, u32[]{:S(2)}, u32[]{:S(2)}) async-start(bf16[16,2,256,256]{3,2,1,0:T(8,128)(2,1)} %shard_map.77), calls=%async_computation | async-start | bytes 8388608 | tf_op jit(solution)/shard_map/all_to_all | solution.py:535
  28.3 81.0 %collective-permute-start.1 = (bf16[2,256,1024]{2,1,0:T(8,128)(2,1)S(1)}, bf16[2,256,1024]{2,1,0:T(8,128)(2,1)}, u32[]{:S(2)}, u32[]{:S(2)}) collective-permute-start(bf16[2,256,1024]{2,1,0:T(8,128)(2,1)S(1)} %slice.35), channel_id=1, source_target_pairs={{8,0},{9,1},{10,2},{11,3},{12,4},{13,5},{14,6},{15,7},{16,8},{17,9... | collective-permute-start | bytes 3145736 | tf_op jit(solution)/shard_map/ppermute | solution.py:520
  29.6 17.5 %collective-permute-start = (bf16[2,512,256]{2,1,0:T(8,128)(2,1)}, bf16[2,512,256]{2,1,0:T(8,128)(2,1)}, u32[]{:S(2)}, u32[]{:S(2)}) collective-permute-start(bf16[2,512,256]{2,1,0:T(8,128)(2,1)} %slice.34), channel_id=1, source_target_pairs={{1,0},{2,1},{3,2},{4,3},{5,4},{6,5},{7,6},{9,8},{10,9},{11,10},{12... | collective-permute-start | bytes 1572872 | tf_op jit(solution)/shard_map/ppermute | solution.py:520
  33.7 13.4 %collective-permute-start.2 = (bf16[2,256,256]{2,1,0:T(8,128)(2,1)S(1)}, bf16[2,256,256]{2,1,0:T(8,128)(2,1)}, u32[]{:S(2)}, u32[]{:S(2)}) collective-permute-start(bf16[2,256,256]{2,1,0:T(8,128)(2,1)S(1)} %slice.33), channel_id=1, source_target_pairs={{9,0},{10,1},{11,2},{12,3},{13,4},{14,5},{15,6},{17,8},{18,9},{19,... | collective-permute-start | bytes 786440 | tf_op jit(solution)/shard_map/ppermute | solution.py:520

commit v4 on v3

--- a/solution.py
+++ b/solution.py
@@ -49,18 +49,6 @@
         out.append(mix(np.block([r, -i]), np.block([i, r])))
     return np.stack(out).astype(ml_dtypes.bfloat16)
 
-def arrange(x):
-    lead = x.shape[:-2]
-    x = x.reshape(*lead, 2, B, 8, S, x.shape[-1])
-    k = len(lead)
-    return jnp.transpose(x, (*range(k), k + 1, k + 3, k, k + 2, k + 4)).reshape(*lead, 256, x.shape[-1])
-
-def restore(x):
-    lead = x.shape[:-2]
-    x = x.reshape(*lead, B, S, 2, 8, x.shape[-1])
-    k = len(lead)
-    return jnp.transpose(x, (*range(k), k + 2, k, k + 3, k + 1, k + 4)).reshape(*lead, 256, x.shape[-1])
-
 def dot(a, b):
     return jnp.dot(a, b, preferred_element_type=f32)
 
@@ -359,33 +347,78 @@
     return (place["ty"], place["tx"])
 
 
-def gather_kernel(n_ty, own, out, send, recv):
-    me = lax.axis_index("ty")
+def gather_kernel(n_ty, n_tx, own, spec, probe, out, lower_o, right_o, corner_o, probe_o,
+                  top, side, half_top, half_side, split, send, recv, send_h, recv_h, sem):
+    ty, tx = lax.axis_index("ty"), lax.axis_index("tx")
+    above, left = lax.rem(ty + n_ty - 1, n_ty), lax.rem(tx + n_tx - 1, n_tx)
     barrier = pltpu.get_barrier_semaphore()
-    spread("ty", n_ty, lambda d: pl.semaphore_signal(barrier, inc=1, device_id=beyond("ty", d, n_ty), device_id_type=MESH))
-    pl.semaphore_wait(barrier, n_ty - 1)
+
+    def greet(device):
+        pl.semaphore_signal(barrier, inc=1, device_id=device, device_id_type=MESH)
+
+    spread("ty", n_ty, lambda d: greet(beyond("ty", d, n_ty)))
+    greet((ty, lax.rem(tx + 1, n_tx)))
+    greet((lax.rem(ty + 1, n_ty), lax.rem(tx + 1, n_tx)))
+    load_side = pltpu.make_async_copy(spec.at[:, :, 0:N], side, sem.at[0])
+    load_top = pltpu.make_async_copy(spec.at[:, 0:N], top, sem.at[1])
+    load_top.start()
+    load_side.start()
+    pl.semaphore_wait(barrier, n_ty + 1)
 
     def copy(d):
         return pltpu.make_async_remote_copy(
-            src_ref=own, dst_ref=out.at[me], send_sem=send.at[d], recv_sem=recv.at[d],
+            src_ref=own, dst_ref=out.at[ty], send_sem=send.at[d], recv_sem=recv.at[d],
             device_id=beyond("ty", d, n_ty), device_id_type=MESH)
 
+    def halo(k, src, dst, device):
+        return pltpu.make_async_remote_copy(
+            src_ref=src, dst_ref=dst, send_sem=send_h.at[k], recv_sem=recv_h.at[k], device_id=device, device_id_type=MESH)
+
     spread("ty", n_ty, lambda d: copy(d).start())
-    out[me] = own[...]
+    out[ty] = own[...]
+    load_top.wait()
+    half_top[...] = top[...].astype(bf)
+    lower = halo(0, half_top, lower_o, (above, tx))
+    lower.start()
+    corner = halo(1, half_top.at[:, :, 0:N], corner_o, (above, left))
+    corner.start()
+    load_side.wait()
+    half_side[...] = side[...].astype(bf)
+    right = halo(2, half_side, right_o, (ty, left))
+    right.start()
+    for c in (0, 1):
+        for t in (0, 1):
+            split[c, :, t] = probe[c, :, :, t * H:t * H + H]
+    for c in (0, 1):
+        for m in range(4):
+            for t in (0, 1):
+                for i in range(32):
+                    ds = pl.ds(128 * (i % 2) + row0(i // 2), 8, stride=S)
+                    probe_o[c, m, 8 * i:8 * i + 8, t * H:t * H + H] = split[c, m, t, ds]
     spread("ty", n_ty, lambda d: copy(d).wait())
-
-
-def gather_offsets(offsets, n_ty):
-    own = jnp.zeros((8, 128), jnp.int32).at[0, : 2 * POS].set(offsets)
-    out = pl.pallas_call(
-        functools.partial(gather_kernel, n_ty),
-        out_shape=like((n_ty, 8, 128), jnp.int32),
-        in_specs=[pl.BlockSpec(memory_space=pltpu.VMEM)],
-        out_specs=pl.BlockSpec(memory_space=pltpu.VMEM),
-        scratch_shapes=[pltpu.SemaphoreType.DMA((n_ty,)), pltpu.SemaphoreType.DMA((n_ty,))],
-        compiler_params=pltpu.CompilerParams(collective_id=0, has_side_effects=True),
-    )(own)
-    return out[:, 0, : 2 * POS].reshape(-1)
+    right.wait()
+    corner.wait()
+    lower.wait()
+
+
+def gather(offsets, specimen, probe, n_ty, n_tx):
+    own = jnp.pad(offsets.reshape(1, 2 * POS), ((0, 7), (0, 128 - 2 * POS)))
+    vmem = pl.BlockSpec(memory_space=pltpu.VMEM)
+    hbm = pl.BlockSpec(memory_space=pl.ANY)
+    dma = pltpu.SemaphoreType.DMA
+    out, lower, right, corner, arranged = pl.pallas_call(
+        functools.partial(gather_kernel, n_ty, n_tx),
+        out_shape=[like((n_ty, 8, 128), jnp.int32), like((2, N, TILE_C), bf), like((2, TILE_R, N), bf), like((2, N, N), bf),
+                   like(probe.shape, f32)],
+        in_specs=[vmem, hbm, vmem],
+        out_specs=[vmem, hbm, hbm, hbm, vmem],
+        scratch_shapes=[
+            pltpu.VMEM((2, N, TILE_C), f32), pltpu.VMEM((2, TILE_R, N), f32),
+            pltpu.VMEM((2, N, TILE_C), bf), pltpu.VMEM((2, TILE_R, N), bf), pltpu.VMEM((2, 4, 2, N, H), f32),
+            dma((n_ty,)), dma((n_ty,)), dma((3,)), dma((3,)), dma((2,))],
+        compiler_params=pltpu.CompilerParams(collective_id=0, has_side_effects=True, vmem_limit_bytes=VMEM_LIMIT),
+    )(own, specimen, probe)
+    return out[:, 0, : 2 * POS].reshape(-1), lower, right, corner, arranged
 
 
 def finish_kernel(n_ty, n_tx, scale, total, down, right, corner, probe_o, down_o, right_o, corner_o,
@@ -511,30 +544,15 @@
     )(total.reshape(2, ROWS, H), down, right, corner)
 
 
-def shift(value, d_ty, d_tx, n_ty, n_tx):
-    pairs = []
-    for y in range(n_ty):
-        for x in range(n_tx):
-            if 0 <= y + d_ty < n_ty and 0 <= x + d_tx < n_tx:
-                pairs.append((y * n_tx + x, (y + d_ty) * n_tx + x + d_tx))
-    return lax.ppermute(value, ("ty", "tx"), pairs)
-
-
 def on_device(specimen, probe, amplitude, offsets):
     n_ty, n_tx = lax.axis_size("ty"), lax.axis_size("tx")
     positions = offsets.shape[0] * n_ty * n_tx
     own = offsets.reshape(-1)
-    half = (specimen[:, :, :N].astype(bf), specimen[:, :N, :].astype(bf))
-    everyone = gather_offsets(own, n_ty)
-    everyone, (side, top) = lax.optimization_barrier((everyone, half))
-    lower = shift(top, -1, 0, n_ty, n_tx)
-    right = shift(side, 0, -1, n_ty, n_tx)
-    corner = shift(top[:, :, :N], -1, -1, n_ty, n_tx)
+    everyone, lower, right, corner, arranged = gather(own, specimen, probe, n_ty, n_tx)
     slots = prepare(own, amplitude, n_ty)
     slots, everyone = lax.optimization_barrier((slots, everyone))
     arrived = lax.all_to_all(slots, "ty", split_axis=0, concat_axis=0, tiled=True)
     tables = make_tables()
-    arranged = arrange(probe)
     far, pat, inten = forward(everyone, specimen, right, lower, corner, arranged, tables, n_ty)
     main, down, rt, cn, total = backward(everyone, arranged, tables, arrived, far, pat, inten, n_ty)
     scale = float(probe.shape[1] / np.sqrt(positions))

time: 289 us -> 237 us (0.82)
  waiting for transfers between devices: 70 us -> 21.7 us
  Pallas kernels: 183 us -> 195 us
  starting transfers between devices: 11.8 us -> 4.57 us
  local copies, waits for them, and re-layouts: 8.68 us -> 3.58 us
    ppermute x3 -> x0, waiting for transfers between devices: 70 us -> none  [shift(): return lax.ppermute(value, ('ty', 'tx'), pairs)]
    pallas_call x1, Pallas kernels: 11.9 us -> 40.1 us  [gather(): pl.pallas_call(functools.partial(gather_kernel, n_ty, n_tx), out_shape=[l...]
    pallas_call x1, Pallas kernels: 60 us -> 36.3 us  [backward(): pl.pallas_call(backward_kernel, out_shape=[like((2, 512, 1024), f32), lik...]
    pallas_call x1, Pallas kernels: 57.6 us -> 80.9 us  [finish(): pl.pallas_call(functools.partial(finish_kernel, n_ty, n_tx, scale), out_s...]
    all_to_all x1, waiting for transfers between devices: 0.01 us -> 21.7 us  [on_device(): lax.all_to_all(slots, 'ty', split_axis=0, concat_axis=0, tiled=True)]
    pallas_call x1, Pallas kernels: 49.5 us -> 33.4 us  [forward(): pl.pallas_call(forward_kernel, out_shape=[like((sources, 2, 4, 2, 2, 128,...]
    ppermute x3 -> x0, starting transfers between devices: 6.76 us -> none  [shift(): return lax.ppermute(value, ('ty', 'tx'), pairs)]
    reshape x2 -> x0, local copies, waits for them, and re-layouts: 4.1 us -> none  [arrange(): x = x.reshape(*lead, 2, B, 8, S, x.shape[-1])]
  transfers between devices with their start and end apart: 4 -> 1, of which waited for: 2 -> 1; matrix products, arithmetic and copies ran while one was open for 1% -> 0% of each run, Pallas kernels for 17% -> 14%
where the time goes in v4:
time: 237 us; the launch traced here: 233 us
  Pallas kernels  195 us (82%)
  waiting for transfers between devices  21.7 us (9%)
  other arithmetic  8.38 us (4%)
  starting transfers between devices  4.57 us (2%)
  local copies, waits for them, and re-layouts  3.58 us (2%)
    pallas_call x1, Pallas kernels, finish(): pl.pallas_call(functools.partial(finish_kernel, n_ty, n_tx, scale), out_s...  80.9 us
    pallas_call x1, Pallas kernels, gather(): pl.pallas_call(functools.partial(gather_kernel, n_ty, n_tx), out_shape=[l...  40.1 us
    pallas_call x1, Pallas kernels, backward(): pl.pallas_call(backward_kernel, out_shape=[like((2, 512, 1024), f32), lik...  36.3 us
    pallas_call x1, Pallas kernels, forward(): pl.pallas_call(forward_kernel, out_shape=[like((sources, 2, 4, 2, 2, 128,...  33.4 us
    all_to_all x1, waiting for transfers between devices, on_device(): lax.all_to_all(slots, 'ty', split_axis=0, concat_axis=0, tiled=True)  21.7 us
    add x1, other arithmetic, on_device(): object_grad = main + spot(down) + spot(rt) + spot(cn)  5.65 us
  transfers between devices with their start and end apart: 1, of which 1 were waited for; matrix products, arithmetic and copies ran while one was open for 0% of the time, Pallas kernels for 14%

profile of v4, /device:TPU:1, one launch (start us, length us, event | category | flops | bytes accessed | tf_op | source)
XLA Modules:
  0.0 233.4 jit_solution(9736267329699346559)
XLA Ops:
  0.6 0.8 copy.11
  1.4 0.1 reshape_reshape.3
  1.5 0.6 reshape.16.off
  2.1 0.6 pad.25.own
  2.7 40.1 %shard_map.78 = (s32[16,8,128]{2,1,0:T(8,128)}, bf16[2,256,1024]{2,1,0:T(8,128)(2,1)}, bf16[2,512,256]{2,1,0:T(8,128)(2,1)}, bf16[2,256,256]{2,1,0:T(8,128)(2,1)}, f32[2,4,256,256]{3,2,1,0:T(8,128)}) custom-call(s32[8,128]{1,0:T(8,128)} %pad.25.own, f32[2,512,1024]{2,1,0:T(8,128)} %spec.3, f32[2,4,256,256]{3,2,1,0:T(8,128)} %probe.1), custom_call_target="tpu_custom_call" | custom-call | tf_op jit(solution)/shard_map/pallas_call | solution.py:409
  42.8 0.9 slice_reduce_fusion
  43.7 0.7 reshape_squeeze.3.off
  44.4 3.8 %shard_map.77 = bf16[16,2,256,256]{3,2,1,0:T(8,128)(2,1)} custom-call(s32[24]{0:T(128)} %reshape.16.off, f32[12,256,256]{2,1,0:T(8,128)} %amp.1, bf16[256,256]{1,0:T(8,128)(2,1)} %constant.9.clone.perm), custom_call_target="tpu_custom_call" | custom-call | tf_op jit(solution)/shard_map/pallas_call | solution.py:81
  48.1 4.6 %all-to-all-start = ((bf16[16,2,256,256]{3,2,1,0:T(8,128)(2,1)}), bf16[16,2,256,256]{3,2,1,0:T(8,128)(2,1)}, u32[]{:S(2)}, u32[]{:S(2)}) async-start(bf16[16,2,256,256]{3,2,1,0:T(8,128)(2,1)} %shard_map.77), calls=%async_computation | async-start | bytes 8388608 | tf_op jit(solution)/shard_map/all_to_all | solution.py:554
  52.7 33.4 %shard_map.79 = (f32[16,2,4,2,2,128,256]{6,5,4,3,2,1,0:T(8,128)}, f32[16,2,2,256,256]{4,3,2,1,0:T(8,128)}, f32[16,2,2,128,256]{4,3,2,1,0:T(8,128)}) custom-call(s32[384]{0:T(512)} %reshape_squeeze.3.off, f32[2,512,1024]{2,1,0:T(8,128)} %spec.3, bf16[2,512,256]{2,1,0:T(8,128)(2,1)} %get-tuple-element.25.right, bf16[2,256,1024]{2,1,0:T(8,128)(2,1)} %get-tuple-element.26.lower, ...), custom_call_target="tpu_custom_call" | custom-call | flops 17179869184 | bytes 104857600 | tf_op jit(solution)/shard_map/pallas_call | solution.py:312
  86.1 21.7 %all-to-all-done.amp = bf16[16,2,256,256]{3,2,1,0:T(8,128)(2,1)} async-done(((bf16[16,2,256,256]{3,2,1,0:T(8,128)(2,1)}), bf16[16,2,256,256]{3,2,1,0:T(8,128)(2,1)}, u32[]{:S(2)}, u32[]{:S(2)}) %all-to-all-start) | async-done | bytes 4194336 | tf_op jit(solution)/shard_map/all_to_all | solution.py:554
  107.8 36.3 %shard_map.80 = (f32[2,512,1024]{2,1,0:T(8,128)}, bf16[2,256,1024]{2,1,0:T(8,128)(2,1)}, bf16[2,512,256]{2,1,0:T(8,128)(2,1)}, bf16[2,256,256]{2,1,0:T(8,128)(2,1)}, f32[2,4,2,256,128]{4,3,2,1,0:T(8,128)}) custom-call(s32[384]{0:T(512)} %reshape_squeeze.3.off, f32[2,4,256,256]{3,2,1,0:T(8,128)} %get-tuple-element.23.probe, ...), custom_call_target="tpu_custom_call" | custom-call | flops 17179869184 | bytes 104857600 | tf_op jit(solution)/shard_map/pallas_call | solution.py:326
  144.1 80.9 %shard_map.81 = (bf16[2,2048,128]{2,1,0:T(8,128)(2,1)}, bf16[2,256,1024]{2,1,0:T(8,128)(2,1)}, bf16[2,512,256]{2,1,0:T(8,128)(2,1)}, bf16[2,256,256]{2,1,0:T(8,128)(2,1)}) custom-call(f32[2,2048,128]{2,1,0:T(8,128)} %bitcast.9, bf16[2,256,1024]{2,1,0:T(8,128)(2,1)} %get-tuple-element.33.down, bf16[2,512,256]{2,1,0:T(8,128)(2,1)} %get-tuple-element.34.right, ...), custom_call_target="tpu_custom_call" | custom-call | tf_op jit(solution)/shard_map/pallas_call | solution.py:533
  225.0 2.7 %copy_bitcast_fusion = f32[2,4,256,256]{3,2,1,0:T(8,128)} fusion(bf16[2,4,2,256,128]{4,3,2,1,0:T(8,128)(2,1)} %bitcast.10), kind=kLoop, calls=%fused_computation.1 | loop fusion | flops 524288 | bytes 3145728 | tf_op jit(solution)/shard_map/convert_element_type | solution.py:566
  227.8 5.7 %convert_add_fusion = f32[2,512,1024]{2,1,0:T(8,128)} fusion(f32[2,512,1024]{2,1,0:T(8,128)} %get-tuple-element.31, bf16[2,256,256]{2,1,0:T(8,128)(2,1)} %get-tuple-element.38, bf16[2,512,256]{2,1,0:T(8,128)(2,1)} %get-tuple-element.37, bf16[2,256,1024]{2,1,0:T(8,128)(2,1)} %get-tuple-element.36), kind=kLoop, calls=%fused_computation | loop fusion | flops 6291456 | bytes 10223616 | tf_op jit(solution)/shard_map/add | solution.py:565
Async XLA Ops:
  48.1 59.7 %all-to-all-start = ((bf16[16,2,256,256]{3,2,1,0:T(8,128)(2,1)}), bf16[16,2,256,256]{3,2,1,0:T(8,128)(2,1)}, u32[]{:S(2)}, u32[]{:S(2)}) async-start(bf16[16,2,256,256]{3,2,1,0:T(8,128)(2,1)} %shard_map.77), calls=%async_computation | async-start | bytes 8388608 | tf_op jit(solution)/shard_map/all_to_all | solution.py:554

commit v5 on v4

--- a/solution.py
+++ b/solution.py
@@ -62,45 +62,55 @@
     return np.eye(N)[order].astype(ml_dtypes.bfloat16)
 
 
-def prep_kernel(off, amp, perm, out, buf, sem):
+def prep_kernel(sources, off, amp, perm, out, places, buf, sem):
+    ty = lax.axis_index("ty")
     copies = []
     for i in range(POS):
         a = dot(perm[...], amp[i].astype(bf)).astype(bf)
         buf[i] = lax.dot_general(a, perm[...], (((1,), (1,)), ((), ())), preferred_element_type=f32).astype(bf)
-        tile = off[2 * i] // TILE_R
+        tile = off[ty, 0, 2 * i] // TILE_R
         rank = jnp.int32(0)
         for j in range(i):
-            rank = rank + (off[2 * j] // TILE_R == tile).astype(jnp.int32)
+            rank = rank + (off[ty, 0, 2 * j] // TILE_R == tile).astype(jnp.int32)
         copies.append(pltpu.make_async_copy(buf.at[i], out.at[tile, rank], sem.at[i]))
         copies[i].start()
+
+    def one(s, carry):
+        rows, cols = [jnp.int32(-1)] * 2, [jnp.int32(0)] * 2
+        seen = jnp.int32(0)
+        for i in range(POS):
+            r, c = off[s, 0, 2 * i], off[s, 0, 2 * i + 1]
+            mine = r // TILE_R == ty
+            for q in range(2):
+                take = mine & (seen == q)
+                rows[q] = jnp.where(take, r % TILE_R, rows[q])
+                cols[q] = jnp.where(take, c % TILE_C, cols[q])
+            seen = seen + mine.astype(jnp.int32)
+        for q in range(2):
+            places[s * 4 + 2 * q] = rows[q]
+            places[s * 4 + 2 * q + 1] = cols[q]
+        return carry
+
+    lax.fori_loop(0, sources, one, 0)
     for copy in copies:
         copy.wait()
 
 
-def prepare(off, amplitude, sources):
+def prepare(everyone, amplitude, sources):
+    vmem = pl.BlockSpec(memory_space=pltpu.VMEM)
+    smem = pl.BlockSpec(memory_space=pltpu.SMEM)
     return pl.pallas_call(
-        prep_kernel,
-        out_shape=jax.ShapeDtypeStruct((sources, 2, N, N), bf),
-        in_specs=[pl.BlockSpec(memory_space=pltpu.SMEM), pl.BlockSpec(memory_space=pltpu.VMEM), pl.BlockSpec(memory_space=pltpu.VMEM)],
-        out_specs=pl.BlockSpec(memory_space=pl.ANY),
+        functools.partial(prep_kernel, sources),
+        out_shape=[jax.ShapeDtypeStruct((sources, 2, N, N), bf), jax.ShapeDtypeStruct((4 * sources,), jnp.int32)],
+        in_specs=[smem, vmem, vmem],
+        out_specs=[pl.BlockSpec(memory_space=pl.ANY), smem],
         scratch_shapes=[pltpu.VMEM((POS, N, N), bf), pltpu.SemaphoreType.DMA((POS,))],
         compiler_params=pltpu.CompilerParams(vmem_limit_bytes=VMEM_LIMIT),
-    )(off, amplitude, parity_matrix())
-
-
-def find(off, source, tile):
-    rows, cols = [jnp.int32(-1)] * 2, [jnp.int32(0)] * 2
-    seen = jnp.int32(0)
-    for i in range(POS):
-        base = (source * POS + i) * 2
-        r, c = off[base], off[base + 1]
-        mine = r // TILE_R == tile
-        for q in range(2):
-            take = mine & (seen == q)
-            rows[q] = jnp.where(take, r % TILE_R, rows[q])
-            cols[q] = jnp.where(take, c % TILE_C, cols[q])
-        seen = seen + mine.astype(jnp.int32)
-    return rows, cols
+    )(everyone, amplitude, parity_matrix())
+
+
+def find(places, source):
+    return [places[4 * source], places[4 * source + 2]], [places[4 * source + 1], places[4 * source + 3]]
 
 
 def p1(probe, pat, A):
@@ -230,7 +240,7 @@
                 ext[c, t, :512] = (spec[c, :, ls] if t < 8 else right[c, :, l2]).astype(bf).astype(f32)
                 ext[c, t, 512:] = (lower[c, :, ls] if t < 8 else corner[c, :, l2]).astype(f32)
 
-    rows, cols = find(off, s, lax.axis_index("ty"))
+    rows, cols = find(off, s)
 
     @pl.when(rows[0] >= 0)
     def _():
@@ -257,7 +267,7 @@
         grid[...] = jnp.zeros_like(grid)
         total[...] = jnp.zeros_like(total)
 
-    rows, cols = find(off, s, lax.axis_index("ty"))
+    rows, cols = find(off, s)
 
     @pl.when(rows[0] >= 0)
     def _():
@@ -358,12 +368,11 @@
 
     spread("ty", n_ty, lambda d: greet(beyond("ty", d, n_ty)))
     greet((ty, lax.rem(tx + 1, n_tx)))
-    greet((lax.rem(ty + 1, n_ty), lax.rem(tx + 1, n_tx)))
     load_side = pltpu.make_async_copy(spec.at[:, :, 0:N], side, sem.at[0])
     load_top = pltpu.make_async_copy(spec.at[:, 0:N], top, sem.at[1])
     load_top.start()
     load_side.start()
-    pl.semaphore_wait(barrier, n_ty + 1)
+    pl.semaphore_wait(barrier, n_ty)
 
     def copy(d):
         return pltpu.make_async_remote_copy(
@@ -377,15 +386,19 @@
     spread("ty", n_ty, lambda d: copy(d).start())
     out[ty] = own[...]
     load_top.wait()
-    half_top[...] = top[...].astype(bf)
-    lower = halo(0, half_top, lower_o, (above, tx))
-    lower.start()
-    corner = halo(1, half_top.at[:, :, 0:N], corner_o, (above, left))
-    corner.start()
+    half_top[:, :, 0:N] = top[:, :, 0:N].astype(bf)
+    first = halo(0, half_top.at[:, :, 0:N], lower_o.at[:, :, 0:N], (above, tx))
+    first.start()
+    half_top[:, :, N:TILE_C] = top[:, :, N:TILE_C].astype(bf)
+    rest = halo(1, half_top.at[:, :, N:TILE_C], lower_o.at[:, :, N:TILE_C], (above, tx))
+    rest.start()
     load_side.wait()
     half_side[...] = side[...].astype(bf)
     right = halo(2, half_side, right_o, (ty, left))
     right.start()
+    first.wait()
+    corner = halo(3, lower_o.at[:, :, 0:N], corner_o, (ty, left))
+    corner.start()
     for c in (0, 1):
         for t in (0, 1):
             split[c, :, t] = probe[c, :, :, t * H:t * H + H]
@@ -398,7 +411,7 @@
     spread("ty", n_ty, lambda d: copy(d).wait())
     right.wait()
     corner.wait()
-    lower.wait()
+    rest.wait()
 
 
 def gather(offsets, specimen, probe, n_ty, n_tx):
@@ -415,14 +428,14 @@
         scratch_shapes=[
             pltpu.VMEM((2, N, TILE_C), f32), pltpu.VMEM((2, TILE_R, N), f32),
             pltpu.VMEM((2, N, TILE_C), bf), pltpu.VMEM((2, TILE_R, N), bf), pltpu.VMEM((2, 4, 2, N, H), f32),
-            dma((n_ty,)), dma((n_ty,)), dma((3,)), dma((3,)), dma((2,))],
+            dma((n_ty,)), dma((n_ty,)), dma((4,)), dma((4,)), dma((2,))],
         compiler_params=pltpu.CompilerParams(collective_id=0, has_side_effects=True, vmem_limit_bytes=VMEM_LIMIT),
     )(own, specimen, probe)
-    return out[:, 0, : 2 * POS].reshape(-1), lower, right, corner, arranged
-
-
-def finish_kernel(n_ty, n_tx, scale, total, down, right, corner, probe_o, down_o, right_o, corner_o,
-                  cast, rax, ray, sx, sy, rbx, rby, gx, gy, hx, hy, send_ty, recv_ty, send_tx, recv_tx, send_h, recv_h):
+    return out, lower, right, corner, arranged
+
+
+def finish_kernel(n_ty, n_tx, scale, total, down, right, corner, probe_o, down_o, right_o,
+                  cast, rax, ray, sx, sy, rbx, rby, gx, gy, hx, hy, arrived, edge, send_ty, recv_ty, send_tx, recv_tx, send_h, recv_h, sem):
     ty, tx = lax.axis_index("ty"), lax.axis_index("tx")
     nx, ny, sub = ROWS // n_tx, ROWS // n_ty, ROWS // n_tx // n_ty
     barrier = pltpu.get_barrier_semaphore()
@@ -432,9 +445,11 @@
 
     spread("ty", n_ty, lambda d: greet(beyond("ty", d, n_ty)))
     spread("tx", n_tx, lambda d: greet(beyond("tx", d, n_tx)))
-    greet((lax.rem(ty + n_ty - 1, n_ty), lax.rem(tx + n_tx - 1, n_tx)))
+    load = pltpu.make_async_copy(down.at[:, :, 0:N], edge, sem)
+    load.start()
     cast[...] = total[...].astype(bf)
-    pl.semaphore_wait(barrier, n_ty + n_tx - 1)
+    load.wait()
+    pl.semaphore_wait(barrier, n_ty + n_tx - 2)
 
     def over_ty(stage, d, src, dst):
         return pltpu.make_async_remote_copy(
@@ -454,9 +469,11 @@
             src_ref=src, dst_ref=dst, send_sem=send_h.at[k], recv_sem=recv_h.at[k], device_id=device, device_id_type=MESH)
 
     below, beside = lax.rem(ty + 1, n_ty), lax.rem(tx + 1, n_tx)
-    part = N // PIECES
-    pieces = [halo(k, down.at[:, k * part:k * part + part], down_o.at[:, k * part:k * part + part], (below, tx)) for k in range(PIECES)]
-    halos = pieces + [halo(PIECES, right, right_o, (ty, beside)), halo(PIECES + 1, corner, corner_o, (below, beside))]
+    cross = halo(0, corner, arrived, (ty, beside))
+    side = halo(1, right, right_o, (ty, beside))
+    pieces = [halo(2 + k, edge if k == 0 else down.at[:, :, k * N:k * N + N], down_o.at[:, :, k * N:k * N + N], (below, tx)) for k in range(PIECES)]
+    cross.start()
+    side.start()
 
     def ax(d):
         peer = lax.rem(tx + d, n_tx)
@@ -468,7 +485,7 @@
 
     spread("tx", n_tx, lambda d: ax(d).start())
     spread("ty", n_ty, lambda d: ay(d).start())
-    halos[0].start()
+    pieces[1].start()
     spread("tx", n_tx, lambda d: ax(d).wait())
     sx[...] = lax.fori_loop(1, n_tx, lambda d, t: t + rax[d].astype(f32), total[0, rows(tx, nx)])
 
@@ -485,7 +502,7 @@
         return over_tx(1, d, sy.at[rows(peer, sub)], rby.at[d])
 
     spread("tx", n_tx, lambda d: by(d).start())
-    halos[1].start()
+    pieces[2].start()
     spread("ty", n_ty, lambda d: bx(d).wait())
     gx[rows(ty, sub)] = scale * lax.fori_loop(1, n_ty, lambda d, t: t + rbx[d], sx[rows(ty, sub)])
 
@@ -500,7 +517,9 @@
         return over_tx(2, d, gy.at[rows(tx, sub)], gy.at[rows(tx, sub)])
 
     spread("tx", n_tx, lambda d: cy(d).start())
-    halos[2].start()
+    cross.wait()
+    edge[...] = (edge[...].astype(f32) + arrived[...].astype(f32)).astype(bf)
+    pieces[0].start()
     spread("ty", n_ty, lambda d: cx(d).wait())
     hx[...] = gx[...].astype(bf)
 
@@ -516,12 +535,11 @@
         return over_ty(3, d, hy, probe_o.at[1, rows(ty, ny)])
 
     spread("ty", n_ty, lambda d: dy(d).start())
-    for h in halos[3:]:
-        h.start()
+    pieces[3].start()
     probe_o[1, rows(ty, ny)] = hy[...]
     spread("tx", n_tx, lambda d: dx(d).wait())
     spread("ty", n_ty, lambda d: dy(d).wait())
-    for h in halos:
+    for h in (side, *pieces):
         h.wait()
 
 
@@ -532,38 +550,65 @@
     dma = pltpu.SemaphoreType.DMA
     return pl.pallas_call(
         functools.partial(finish_kernel, n_ty, n_tx, scale),
-        out_shape=[like((2, ROWS, H), bf), like(down.shape, bf), like(right.shape, bf), like(corner.shape, bf)],
+        out_shape=[like((2, ROWS, H), bf), like(down.shape, bf), like(right.shape, bf)],
         in_specs=[vmem, hbm, hbm, hbm],
-        out_specs=[vmem, hbm, hbm, hbm],
+        out_specs=[vmem, hbm, hbm],
         scratch_shapes=[
             pltpu.VMEM((2, ROWS, H), bf), pltpu.VMEM((n_tx, nx, H), bf), pltpu.VMEM((n_ty, ny, H), bf),
             pltpu.VMEM((nx, H), f32), pltpu.VMEM((ny, H), f32), pltpu.VMEM((n_ty, sub, H), f32), pltpu.VMEM((n_tx, sub, H), f32),
             pltpu.VMEM((nx, H), f32), pltpu.VMEM((ny, H), f32), pltpu.VMEM((nx, H), bf), pltpu.VMEM((ny, H), bf),
-            dma((4, n_ty)), dma((4, n_ty)), dma((4, n_tx)), dma((4, n_tx)), dma((PIECES + 2,)), dma((PIECES + 2,))],
+            pltpu.VMEM((2, N, N), bf), pltpu.VMEM((2, N, N), bf),
+            dma((4, n_ty)), dma((4, n_ty)), dma((4, n_tx)), dma((4, n_tx)), dma((PIECES + 2,)), dma((PIECES + 2,)), dma],
         compiler_params=pltpu.CompilerParams(collective_id=1, has_side_effects=True, vmem_limit_bytes=VMEM_LIMIT),
     )(total.reshape(2, ROWS, H), down, right, corner)
+
+
+def close_kernel(main, down, right, probe, object_o, probe_o):
+    b = pl.program_id(1)
+
+    @pl.when(b == 0)
+    def _():
+        object_o[0, :, 0:N] = main[0, :, 0:N] + (down[0, :, 0:N].astype(f32) + right[0].astype(f32))
+        object_o[0, :, N:TILE_C] = main[0, :, N:TILE_C] + down[0, :, N:TILE_C].astype(f32)
+
+    @pl.when(b == 1)
+    def _():
+        object_o[0, :, 0:N] = main[0, :, 0:N] + right[0].astype(f32)
+        object_o[0, :, N:TILE_C] = main[0, :, N:TILE_C]
+
+    for m in (0, 1):
+        for t in (0, 1):
+            at = (2 * m + t) * N
+            probe_o[0, m, :, t * H:t * H + H] = probe[0, at:at + N].astype(f32)
+
+
+def close(main, down, right, probe):
+    def spec(*shape):
+        return pl.BlockSpec((1, *shape), lambda c, b: (c, b) + (0,) * (len(shape) - 1))
+
+    return pl.pallas_call(
+        close_kernel,
+        out_shape=[like(main.shape, f32), like((2, 4, N, N), f32)],
+        grid=(2, TILE_R // N),
+        in_specs=[spec(N, TILE_C), pl.BlockSpec((1, N, TILE_C), lambda c, b: (c, 0, 0)), spec(N, N), spec(ROWS // 2, H)],
+        out_specs=[spec(N, TILE_C), spec(2, N, N)],
+        compiler_params=pltpu.CompilerParams(vmem_limit_bytes=VMEM_LIMIT),
+    )(main, down, right, probe)
 
 
 def on_device(specimen, probe, amplitude, offsets):
     n_ty, n_tx = lax.axis_size("ty"), lax.axis_size("tx")
     positions = offsets.shape[0] * n_ty * n_tx
-    own = offsets.reshape(-1)
-    everyone, lower, right, corner, arranged = gather(own, specimen, probe, n_ty, n_tx)
-    slots = prepare(own, amplitude, n_ty)
-    slots, everyone = lax.optimization_barrier((slots, everyone))
+    everyone, lower, right, corner, arranged = gather(offsets.reshape(-1), specimen, probe, n_ty, n_tx)
+    slots, places = prepare(everyone, amplitude, n_ty)
+    slots, places = lax.optimization_barrier((slots, places))
     arrived = lax.all_to_all(slots, "ty", split_axis=0, concat_axis=0, tiled=True)
     tables = make_tables()
-    far, pat, inten = forward(everyone, specimen, right, lower, corner, arranged, tables, n_ty)
-    main, down, rt, cn, total = backward(everyone, arranged, tables, arrived, far, pat, inten, n_ty)
+    far, pat, inten = forward(places, specimen, right, lower, corner, arranged, tables, n_ty)
+    main, down, rt, cn, total = backward(places, arranged, tables, arrived, far, pat, inten, n_ty)
     scale = float(probe.shape[1] / np.sqrt(positions))
-    probe_grad, down, rt, cn = finish(total, down, rt, cn, scale, n_ty, n_tx)
-
-    def spot(piece):
-        rows, cols = TILE_R - piece.shape[1], TILE_C - piece.shape[2]
-        return jnp.pad(piece.astype(f32), ((0, 0), (0, rows), (0, cols)))
-
-    object_grad = main + spot(down) + spot(rt) + spot(cn)
-    probe_grad = jnp.swapaxes(probe_grad.reshape(2, 4, 2, N, H), 2, 3).reshape(probe.shape).astype(f32)
+    probe_grad, down, rt = finish(total, down, rt, cn, scale, n_ty, n_tx)
+    object_grad, probe_grad = close(main, down, rt, probe_grad)
     return (object_grad, probe_grad)
 
 

time: 237 us -> 228 us (0.962)
  other arithmetic: 8.38 us -> 0 us
    pallas_call x1, Pallas kernels: 80.9 us -> 71 us  [finish(): pl.pallas_call(functools.partial(finish_kernel, n_ty, n_tx, scale), out_s...]
    pallas_call x1 -> x2, Pallas kernels: 3.75 us -> 12.2 us  [the longest x1 6.09 us: close(): pl.pallas_call(close_kernel, out_shape=[like(main.shape, f32), like((2, 4...]
    pallas_call x1, Pallas kernels: 40.1 us -> 34.3 us  [gather(): pl.pallas_call(functools.partial(gather_kernel, n_ty, n_tx), out_shape=[l...]
    add x1 -> x0, other arithmetic: 5.65 us -> none  [on_device(): object_grad = main + spot(down) + spot(rt) + spot(cn)]
    pallas_call x1, Pallas kernels: 36.3 us -> 40.2 us  [backward(): pl.pallas_call(backward_kernel, out_shape=[like((2, 512, 1024), f32), lik...]
    convert_element_type x1 -> x0, other arithmetic: 2.73 us -> none  [on_device(): jnp.swapaxes(probe_grad.reshape(2, 4, 2, N, H), 2, 3).reshape(probe.shape)]
    pallas_call x1, Pallas kernels: 33.4 us -> 36.2 us  [forward(): pl.pallas_call(forward_kernel, out_shape=[like((sources, 2, 4, 2, 2, 128,...]
  transfers between devices with their start and end apart: 1 -> 1, of which waited for: 1 -> 1; matrix products, arithmetic and copies ran while one was open for 0% -> 0% of each run, Pallas kernels for 14% -> 16%
where the time goes in v5:
time: 228 us; the launch traced here: 226 us
  Pallas kernels  194 us (85%)
  waiting for transfers between devices  24 us (11%)
  starting transfers between devices  6.03 us (3%)
    pallas_call x1, Pallas kernels, finish(): pl.pallas_call(functools.partial(finish_kernel, n_ty, n_tx, scale), out_s...  71 us
    pallas_call x1, Pallas kernels, backward(): pl.pallas_call(backward_kernel, out_shape=[like((2, 512, 1024), f32), lik...  40.2 us
    pallas_call x1, Pallas kernels, forward(): pl.pallas_call(forward_kernel, out_shape=[like((sources, 2, 4, 2, 2, 128,...  36.2 us
    pallas_call x1, Pallas kernels, gather(): pl.pallas_call(functools.partial(gather_kernel, n_ty, n_tx), out_shape=[l...  34.3 us
    all_to_all x1, waiting for transfers between devices, on_device(): lax.all_to_all(slots, 'ty', split_axis=0, concat_axis=0, tiled=True)  24 us
    pallas_call x1, Pallas kernels, close(): pl.pallas_call(close_kernel, out_shape=[like(main.shape, f32), like((2, 4...  6.09 us
    pallas_call x1, Pallas kernels, prepare(): pl.pallas_call(functools.partial(prep_kernel, sources), out_shape=[jax.Sh...  6.08 us
    all_to_all x1, starting transfers between devices, on_device(): lax.all_to_all(slots, 'ty', split_axis=0, concat_axis=0, tiled=True)  6.03 us
  transfers between devices with their start and end apart: 1, of which 1 were waited for; matrix products, arithmetic and copies ran while one was open for 0% of the time, Pallas kernels for 16%

profile of v5, /device:TPU:1, one launch (start us, length us, event | category | flops | bytes accessed | tf_op | source)
XLA Modules:
  0.0 226.0 jit_solution(1943265531250549891)
XLA Ops:
  0.6 0.8 copy.9
  1.4 0.1 reshape_reshape.3
  1.5 0.6 pad.4.own
  2.1 34.3 %shard_map.77 = (s32[16,8,128]{2,1,0:T(8,128)}, bf16[2,256,1024]{2,1,0:T(8,128)(2,1)}, bf16[2,512,256]{2,1,0:T(8,128)(2,1)}, bf16[2,256,256]{2,1,0:T(8,128)(2,1)}, f32[2,4,256,256]{3,2,1,0:T(8,128)}) custom-call(s32[8,128]{1,0:T(8,128)} %pad.4.own, f32[2,512,1024]{2,1,0:T(8,128)} %spec.3, f32[2,4,256,256]{3,2,1,0:T(8,128)} %probe.1), custom_call_target="tpu_custom_call" | custom-call | tf_op jit(solution)/shard_map/pallas_call | solution.py:422
  36.4 6.1 %shard_map.78 = (bf16[16,2,256,256]{3,2,1,0:T(8,128)(2,1)}, s32[64]{0:T(128)}) custom-call(s32[16,8,128]{2,1,0:T(8,128)} %get-tuple-element.20.off, f32[12,256,256]{2,1,0:T(8,128)} %amp.1, bf16[256,256]{1,0:T(8,128)(2,1)} %constant.6.clone.perm), custom_call_target="tpu_custom_call" | custom-call | tf_op jit(solution)/shard_map/pallas_call | solution.py:102
  42.5 6.0 %all-to-all-start = ((bf16[16,2,256,256]{3,2,1,0:T(8,128)(2,1)}), bf16[16,2,256,256]{3,2,1,0:T(8,128)(2,1)}, u32[]{:S(2)}, u32[]{:S(2)}) async-start(bf16[16,2,256,256]{3,2,1,0:T(8,128)(2,1)} %get-tuple-element.23), calls=%async_computation | async-start | bytes 8388608 | tf_op jit(solution)/shard_map/all_to_all | solution.py:605
  48.5 36.2 %shard_map.79 = (f32[16,2,4,2,2,128,256]{6,5,4,3,2,1,0:T(8,128)}, f32[16,2,2,256,256]{4,3,2,1,0:T(8,128)}, f32[16,2,2,128,256]{4,3,2,1,0:T(8,128)}) custom-call(s32[64]{0:T(128)} %get-tuple-element.21.off, f32[2,512,1024]{2,1,0:T(8,128)} %spec.3, bf16[2,512,256]{2,1,0:T(8,128)(2,1)} %get-tuple-element.24.right, ...), custom_call_target="tpu_custom_call" | custom-call | flops 17179869184 | bytes 104857600 | tf_op jit(solution)/shard_map/pallas_call | solution.py:322
  84.7 24.0 %all-to-all-done.amp = bf16[16,2,256,256]{3,2,1,0:T(8,128)(2,1)} async-done(((bf16[16,2,256,256]{3,2,1,0:T(8,128)(2,1)}), bf16[16,2,256,256]{3,2,1,0:T(8,128)(2,1)}, u32[]{:S(2)}, u32[]{:S(2)}) %all-to-all-start) | async-done | bytes 4194336 | tf_op jit(solution)/shard_map/all_to_all | solution.py:605
  108.6 40.2 %shard_map.80 = (f32[2,512,1024]{2,1,0:T(8,128)}, bf16[2,256,1024]{2,1,0:T(8,128)(2,1)}, bf16[2,512,256]{2,1,0:T(8,128)(2,1)}, bf16[2,256,256]{2,1,0:T(8,128)(2,1)}, f32[2,4,2,256,128]{4,3,2,1,0:T(8,128)}) custom-call(s32[64]{0:T(128)} %get-tuple-element.21.off, f32[2,4,256,256]{3,2,1,0:T(8,128)} %get-tuple-element.22.probe, ...), custom_call_target="tpu_custom_call" | custom-call | flops 17179869184 | bytes 104857600 | tf_op jit(solution)/shard_map/pallas_call | solution.py:336
  148.9 71.0 %shard_map.81 = (bf16[2,2048,128]{2,1,0:T(8,128)(2,1)}, bf16[2,256,1024]{2,1,0:T(8,128)(2,1)}, bf16[2,512,256]{2,1,0:T(8,128)(2,1)}) custom-call(f32[2,2048,128]{2,1,0:T(8,128)} %bitcast.1, bf16[2,256,1024]{2,1,0:T(8,128)(2,1)} %get-tuple-element.32.down, bf16[2,512,256]{2,1,0:T(8,128)(2,1)} %get-tuple-element.33.right, ...), custom_call_target="tpu_custom_call" | custom-call | tf_op jit(solution)/shard_map/pallas_call | solution.py:551
  219.9 6.1 %shard_map.82 = (f32[2,512,1024]{2,1,0:T(8,128)}, f32[2,4,256,256]{3,2,1,0:T(8,128)}) custom-call(f32[2,512,1024]{2,1,0:T(8,128)} %get-tuple-element.30.main, bf16[2,256,1024]{2,1,0:T(8,128)(2,1)} %get-tuple-element.35.down, bf16[2,512,256]{2,1,0:T(8,128)(2,1)} %get-tuple-element.36.right, bf16[2,2048,128]{2,1,0:T(8,128)(2,1)} %get-tuple-element.37.probe), custom_call_target="tpu_custom_call" | custom-call | tf_op jit(solution)/shard_map/pallas_call | solution.py:589
Async XLA Ops:
  42.5 66.2 %all-to-all-start = ((bf16[16,2,256,256]{3,2,1,0:T(8,128)(2,1)}), bf16[16,2,256,256]{3,2,1,0:T(8,128)(2,1)}, u32[]{:S(2)}, u32[]{:S(2)}) async-start(bf16[16,2,256,256]{3,2,1,0:T(8,128)(2,1)} %get-tuple-element.23), calls=%async_computation | async-start | bytes 8388608 | tf_op jit(solution)/shard_map/all_to_all | solution.py:605

commit v6 on v5

--- a/solution.py
+++ b/solution.py
@@ -17,7 +17,8 @@
 TILE_C = 1024
 POS = 12
 VMEM_LIMIT = 60 * 2**20
-ROWS = 2048
+ROWS = 4096
+ROWS_X = 3072
 PIECES = 4
 MESH = pl.DeviceIdType.MESH
 S = 2
@@ -62,51 +63,47 @@
     return np.eye(N)[order].astype(ml_dtypes.bfloat16)
 
 
-def prep_kernel(sources, off, amp, perm, out, places, buf, sem):
+def prep_kernel(off, amp, out, sem):
     ty = lax.axis_index("ty")
     copies = []
     for i in range(POS):
-        a = dot(perm[...], amp[i].astype(bf)).astype(bf)
-        buf[i] = lax.dot_general(a, perm[...], (((1,), (1,)), ((), ())), preferred_element_type=f32).astype(bf)
         tile = off[ty, 0, 2 * i] // TILE_R
         rank = jnp.int32(0)
         for j in range(i):
             rank = rank + (off[ty, 0, 2 * j] // TILE_R == tile).astype(jnp.int32)
-        copies.append(pltpu.make_async_copy(buf.at[i], out.at[tile, rank], sem.at[i]))
+        copies.append(pltpu.make_async_copy(amp.at[i], out.at[tile, rank], sem.at[i]))
         copies[i].start()
-
-    def one(s, carry):
-        rows, cols = [jnp.int32(-1)] * 2, [jnp.int32(0)] * 2
-        seen = jnp.int32(0)
-        for i in range(POS):
-            r, c = off[s, 0, 2 * i], off[s, 0, 2 * i + 1]
-            mine = r // TILE_R == ty
-            for q in range(2):
-                take = mine & (seen == q)
-                rows[q] = jnp.where(take, r % TILE_R, rows[q])
-                cols[q] = jnp.where(take, c % TILE_C, cols[q])
-            seen = seen + mine.astype(jnp.int32)
-        for q in range(2):
-            places[s * 4 + 2 * q] = rows[q]
-            places[s * 4 + 2 * q + 1] = cols[q]
-        return carry
-
-    lax.fori_loop(0, sources, one, 0)
     for copy in copies:
         copy.wait()
 
 
 def prepare(everyone, amplitude, sources):
-    vmem = pl.BlockSpec(memory_space=pltpu.VMEM)
-    smem = pl.BlockSpec(memory_space=pltpu.SMEM)
+    hbm = pl.BlockSpec(memory_space=pl.ANY)
     return pl.pallas_call(
-        functools.partial(prep_kernel, sources),
-        out_shape=[jax.ShapeDtypeStruct((sources, 2, N, N), bf), jax.ShapeDtypeStruct((4 * sources,), jnp.int32)],
-        in_specs=[smem, vmem, vmem],
-        out_specs=[pl.BlockSpec(memory_space=pl.ANY), smem],
-        scratch_shapes=[pltpu.VMEM((POS, N, N), bf), pltpu.SemaphoreType.DMA((POS,))],
-        compiler_params=pltpu.CompilerParams(vmem_limit_bytes=VMEM_LIMIT),
-    )(everyone, amplitude, parity_matrix())
+        prep_kernel,
+        out_shape=jax.ShapeDtypeStruct((sources, 2, N, N), bf),
+        in_specs=[pl.BlockSpec(memory_space=pltpu.SMEM), hbm],
+        out_specs=hbm,
+        scratch_shapes=[pltpu.SemaphoreType.DMA((POS,))],
+    )(everyone, amplitude)
+
+
+def scan(off, source, places):
+    ty = lax.axis_index("ty")
+    rows, cols = [jnp.int32(-1)] * 2, [jnp.int32(0)] * 2
+    seen = jnp.int32(0)
+    for i in range(POS):
+        r, c = off[source, 0, 2 * i], off[source, 0, 2 * i + 1]
+        mine = r // TILE_R == ty
+        for q in range(2):
+            take = mine & (seen == q)
+            rows[q] = jnp.where(take, r % TILE_R, rows[q])
+            cols[q] = jnp.where(take, c % TILE_C, cols[q])
+        seen = seen + mine.astype(jnp.int32)
+    for q in range(2):
+        places[source * 4 + 2 * q] = rows[q]
+        places[source * 4 + 2 * q + 1] = cols[q]
+    return rows, cols
 
 
 def find(places, source):
@@ -228,7 +225,7 @@
                     grid[k, ct + t, ds] = grid[k, ct + t, ds] + y[16 * i + 8 * h:16 * i + 8 * h + 8]
 
 
-def forward_kernel(off, spec, right, lower, corner, probe, tab, far, pat, inten, ext, A, Bb):
+def forward_kernel(off, spec, right, lower, corner, probe, tab, far, pat, inten, places, ext, A, Bb):
     s = pl.program_id(0)
 
     @pl.when(s == 0)
@@ -240,7 +237,7 @@
                 ext[c, t, :512] = (spec[c, :, ls] if t < 8 else right[c, :, l2]).astype(bf).astype(f32)
                 ext[c, t, 512:] = (lower[c, :, ls] if t < 8 else corner[c, :, l2]).astype(f32)
 
-    rows, cols = find(off, s)
+    rows, cols = scan(off, s, places)
 
     @pl.when(rows[0] >= 0)
     def _():
@@ -321,11 +318,12 @@
 def forward(off, spec, right, lower, corner, probe, tab, sources):
     return pl.pallas_call(
         forward_kernel,
-        out_shape=[like((sources, 2, 4, 2, 2, 128, 256), f32), like((sources, 2, 2, 256, 256), f32), like((sources, 2, 2, 128, 256), f32)],
+        out_shape=[like((sources, 2, 4, 2, 2, 128, 256), f32), like((sources, 2, 2, 256, 256), f32), like((sources, 2, 2, 128, 256), f32),
+                   like((4 * sources,), jnp.int32)],
         grid_spec=pltpu.PrefetchScalarGridSpec(
             num_scalar_prefetch=1, grid=(sources,),
             in_specs=[whole(2, 512, 1024), whole(2, 512, 256), whole(2, 256, 1024), whole(2, 256, 256), whole(2, 4, 256, 256), whole(8, 256, 256)],
-            out_specs=[each(2, 4, 2, 2, 128, 256), each(2, 2, 256, 256), each(2, 2, 128, 256)],
+            out_specs=[each(2, 4, 2, 2, 128, 256), each(2, 2, 256, 256), each(2, 2, 128, 256), pl.BlockSpec(memory_space=pltpu.SMEM)],
             scratch_shapes=[pltpu.VMEM((2, 10, 768, 128), f32), pltpu.VMEM((2, 4, 2, 256, 256), bf), pltpu.VMEM((2, 4, 2, 256, 256), bf)]),
         compiler_params=pltpu.CompilerParams(vmem_limit_bytes=VMEM_LIMIT),
         cost_estimate=pl.CostEstimate(flops=32 * 2**29, bytes_accessed=100 * 2**20, transcendentals=0),
@@ -357,8 +355,8 @@
     return (place["ty"], place["tx"])
 
 
-def gather_kernel(n_ty, n_tx, own, spec, probe, out, lower_o, right_o, corner_o, probe_o,
-                  top, side, half_top, half_side, split, send, recv, send_h, recv_h, sem):
+def gather_kernel(n_ty, n_tx, own, spec, probe, amp, perm, out, lower_o, right_o, corner_o, probe_o, amp_o,
+                  top, side, half_top, half_side, split, raw, send, recv, send_h, recv_h, sem):
     ty, tx = lax.axis_index("ty"), lax.axis_index("tx")
     above, left = lax.rem(ty + n_ty - 1, n_ty), lax.rem(tx + n_tx - 1, n_tx)
     barrier = pltpu.get_barrier_semaphore()
@@ -372,6 +370,8 @@
     load_top = pltpu.make_async_copy(spec.at[:, 0:N], top, sem.at[1])
     load_top.start()
     load_side.start()
+    load_raw = pltpu.make_async_copy(amp, raw, sem.at[2])
+    load_raw.start()
     pl.semaphore_wait(barrier, n_ty)
 
     def copy(d):
@@ -408,36 +408,44 @@
                 for i in range(32):
                     ds = pl.ds(128 * (i % 2) + row0(i // 2), 8, stride=S)
                     probe_o[c, m, 8 * i:8 * i + 8, t * H:t * H + H] = split[c, m, t, ds]
+    load_raw.wait()
+
+    def reorder(i, carry):
+        a = dot(perm[...], raw[i].astype(bf)).astype(bf)
+        amp_o[i] = lax.dot_general(a, perm[...], (((1,), (1,)), ((), ())), preferred_element_type=f32).astype(bf)
+        return carry
+
+    lax.fori_loop(0, POS, reorder, 0)
     spread("ty", n_ty, lambda d: copy(d).wait())
     right.wait()
     corner.wait()
     rest.wait()
 
 
-def gather(offsets, specimen, probe, n_ty, n_tx):
+def gather(offsets, specimen, probe, amplitude, n_ty, n_tx):
     own = jnp.pad(offsets.reshape(1, 2 * POS), ((0, 7), (0, 128 - 2 * POS)))
     vmem = pl.BlockSpec(memory_space=pltpu.VMEM)
     hbm = pl.BlockSpec(memory_space=pl.ANY)
     dma = pltpu.SemaphoreType.DMA
-    out, lower, right, corner, arranged = pl.pallas_call(
+    return pl.pallas_call(
         functools.partial(gather_kernel, n_ty, n_tx),
         out_shape=[like((n_ty, 8, 128), jnp.int32), like((2, N, TILE_C), bf), like((2, TILE_R, N), bf), like((2, N, N), bf),
-                   like(probe.shape, f32)],
-        in_specs=[vmem, hbm, vmem],
-        out_specs=[vmem, hbm, hbm, hbm, vmem],
+                   like(probe.shape, f32), like(amplitude.shape, bf)],
+        in_specs=[vmem, hbm, vmem, hbm, vmem],
+        out_specs=[vmem, hbm, hbm, hbm, vmem, vmem],
         scratch_shapes=[
             pltpu.VMEM((2, N, TILE_C), f32), pltpu.VMEM((2, TILE_R, N), f32),
             pltpu.VMEM((2, N, TILE_C), bf), pltpu.VMEM((2, TILE_R, N), bf), pltpu.VMEM((2, 4, 2, N, H), f32),
-            dma((n_ty,)), dma((n_ty,)), dma((4,)), dma((4,)), dma((2,))],
+            pltpu.VMEM(amplitude.shape, f32), dma((n_ty,)), dma((n_ty,)), dma((4,)), dma((4,)), dma((3,))],
         compiler_params=pltpu.CompilerParams(collective_id=0, has_side_effects=True, vmem_limit_bytes=VMEM_LIMIT),
-    )(own, specimen, probe)
-    return out, lower, right, corner, arranged
+    )(own, specimen, probe, amplitude, parity_matrix())
 
 
 def finish_kernel(n_ty, n_tx, scale, total, down, right, corner, probe_o, down_o, right_o,
                   cast, rax, ray, sx, sy, rbx, rby, gx, gy, hx, hy, arrived, edge, send_ty, recv_ty, send_tx, recv_tx, send_h, recv_h, sem):
     ty, tx = lax.axis_index("ty"), lax.axis_index("tx")
-    nx, ny, sub = ROWS // n_tx, ROWS // n_ty, ROWS // n_tx // n_ty
+    nx, ny = ROWS_X // n_tx, (ROWS - ROWS_X) // n_ty
+    ux, uy = nx // n_ty, ny // n_tx
     barrier = pltpu.get_barrier_semaphore()
 
     def greet(device):
@@ -461,8 +469,8 @@
             src_ref=src, dst_ref=dst, send_sem=send_tx.at[stage, d], recv_sem=recv_tx.at[stage, d],
             device_id=beyond("tx", d, n_tx), device_id_type=MESH)
 
-    def rows(k, n):
-        return pl.ds(pl.multiple_of(k * n, 16), n)
+    def rows(k, n, first=0):
+        return pl.ds(pl.multiple_of(first + k * n, 8), n)
 
     def halo(k, src, dst, device):
         return pltpu.make_async_remote_copy(
@@ -477,44 +485,45 @@
 
     def ax(d):
         peer = lax.rem(tx + d, n_tx)
-        return over_tx(0, d, cast.at[0, rows(peer, nx)], rax.at[d])
+        return over_tx(0, d, cast.at[rows(peer, nx)], rax.at[d])
 
     def ay(d):
         peer = lax.rem(ty + d, n_ty)
-        return over_ty(0, d, cast.at[1, rows(peer, ny)], ray.at[d])
+        return over_ty(0, d, cast.at[rows(peer, ny, ROWS_X)], ray.at[d])
 
     spread("tx", n_tx, lambda d: ax(d).start())
     spread("ty", n_ty, lambda d: ay(d).start())
     pieces[1].start()
+    pieces[2].start()
     spread("tx", n_tx, lambda d: ax(d).wait())
-    sx[...] = lax.fori_loop(1, n_tx, lambda d, t: t + rax[d].astype(f32), total[0, rows(tx, nx)])
+    sx[...] = lax.fori_loop(1, n_tx, lambda d, t: t + rax[d].astype(f32), total[rows(tx, nx)])
 
     def bx(d):
         peer = lax.rem(ty + d, n_ty)
-        return over_ty(1, d, sx.at[rows(peer, sub)], rbx.at[d])
+        return over_ty(1, d, sx.at[rows(peer, ux)], rbx.at[d])
 
     spread("ty", n_ty, lambda d: bx(d).start())
     spread("ty", n_ty, lambda d: ay(d).wait())
-    sy[...] = lax.fori_loop(1, n_ty, lambda d, t: t + ray[d].astype(f32), total[1, rows(ty, ny)])
+    sy[...] = lax.fori_loop(1, n_ty, lambda d, t: t + ray[d].astype(f32), total[rows(ty, ny, ROWS_X)])
 
     def by(d):
         peer = lax.rem(tx + d, n_tx)
-        return over_tx(1, d, sy.at[rows(peer, sub)], rby.at[d])
+        return over_tx(1, d, sy.at[rows(peer, uy)], rby.at[d])
 
     spread("tx", n_tx, lambda d: by(d).start())
-    pieces[2].start()
+    pieces[3].start()
     spread("ty", n_ty, lambda d: bx(d).wait())
-    gx[rows(ty, sub)] = scale * lax.fori_loop(1, n_ty, lambda d, t: t + rbx[d], sx[rows(ty, sub)])
+    gx[rows(ty, ux)] = scale * lax.fori_loop(1, n_ty, lambda d, t: t + rbx[d], sx[rows(ty, ux)])
 
     def cx(d):
-        return over_ty(2, d, gx.at[rows(ty, sub)], gx.at[rows(ty, sub)])
+        return over_ty(2, d, gx.at[rows(ty, ux)], gx.at[rows(ty, ux)])
 
     spread("ty", n_ty, lambda d: cx(d).start())
     spread("tx", n_tx, lambda d: by(d).wait())
-    gy[rows(tx, sub)] = scale * lax.fori_loop(1, n_tx, lambda d, t: t + rby[d], sy[rows(tx, sub)])
+    gy[rows(tx, uy)] = scale * lax.fori_loop(1, n_tx, lambda d, t: t + rby[d], sy[rows(tx, uy)])
 
     def cy(d):
-        return over_tx(2, d, gy.at[rows(tx, sub)], gy.at[rows(tx, sub)])
+        return over_tx(2, d, gy.at[rows(tx, uy)], gy.at[rows(tx, uy)])
 
     spread("tx", n_tx, lambda d: cy(d).start())
     cross.wait()
@@ -524,19 +533,18 @@
     hx[...] = gx[...].astype(bf)
 
     def dx(d):
-        return over_tx(3, d, hx, probe_o.at[0, rows(tx, nx)])
+        return over_tx(3, d, hx, probe_o.at[rows(tx, nx)])
 
     spread("tx", n_tx, lambda d: dx(d).start())
-    probe_o[0, rows(tx, nx)] = hx[...]
+    probe_o[rows(tx, nx)] = hx[...]
     spread("tx", n_tx, lambda d: cy(d).wait())
     hy[...] = gy[...].astype(bf)
 
     def dy(d):
-        return over_ty(3, d, hy, probe_o.at[1, rows(ty, ny)])
+        return over_ty(3, d, hy, probe_o.at[rows(ty, ny, ROWS_X)])
 
     spread("ty", n_ty, lambda d: dy(d).start())
-    pieces[3].start()
-    probe_o[1, rows(ty, ny)] = hy[...]
+    probe_o[rows(ty, ny, ROWS_X)] = hy[...]
     spread("tx", n_tx, lambda d: dx(d).wait())
     spread("ty", n_ty, lambda d: dy(d).wait())
     for h in (side, *pieces):
@@ -544,23 +552,23 @@
 
 
 def finish(total, down, right, corner, scale, n_ty, n_tx):
-    nx, ny, sub = ROWS // n_tx, ROWS // n_ty, ROWS // n_tx // n_ty
+    nx, ny = ROWS_X // n_tx, (ROWS - ROWS_X) // n_ty
     vmem = pl.BlockSpec(memory_space=pltpu.VMEM)
     hbm = pl.BlockSpec(memory_space=pl.ANY)
     dma = pltpu.SemaphoreType.DMA
     return pl.pallas_call(
         functools.partial(finish_kernel, n_ty, n_tx, scale),
-        out_shape=[like((2, ROWS, H), bf), like(down.shape, bf), like(right.shape, bf)],
+        out_shape=[like((ROWS, H), bf), like(down.shape, bf), like(right.shape, bf)],
         in_specs=[vmem, hbm, hbm, hbm],
         out_specs=[vmem, hbm, hbm],
         scratch_shapes=[
-            pltpu.VMEM((2, ROWS, H), bf), pltpu.VMEM((n_tx, nx, H), bf), pltpu.VMEM((n_ty, ny, H), bf),
-            pltpu.VMEM((nx, H), f32), pltpu.VMEM((ny, H), f32), pltpu.VMEM((n_ty, sub, H), f32), pltpu.VMEM((n_tx, sub, H), f32),
+            pltpu.VMEM((ROWS, H), bf), pltpu.VMEM((n_tx, nx, H), bf), pltpu.VMEM((n_ty, ny, H), bf),
+            pltpu.VMEM((nx, H), f32), pltpu.VMEM((ny, H), f32), pltpu.VMEM((n_ty, nx // n_ty, H), f32), pltpu.VMEM((n_tx, ny // n_tx, H), f32),
             pltpu.VMEM((nx, H), f32), pltpu.VMEM((ny, H), f32), pltpu.VMEM((nx, H), bf), pltpu.VMEM((ny, H), bf),
             pltpu.VMEM((2, N, N), bf), pltpu.VMEM((2, N, N), bf),
             dma((4, n_ty)), dma((4, n_ty)), dma((4, n_tx)), dma((4, n_tx)), dma((PIECES + 2,)), dma((PIECES + 2,)), dma],
         compiler_params=pltpu.CompilerParams(collective_id=1, has_side_effects=True, vmem_limit_bytes=VMEM_LIMIT),
-    )(total.reshape(2, ROWS, H), down, right, corner)
+    )(total.reshape(ROWS, H), down, right, corner)
 
 
 def close_kernel(main, down, right, probe, object_o, probe_o):
@@ -590,21 +598,20 @@
         close_kernel,
         out_shape=[like(main.shape, f32), like((2, 4, N, N), f32)],
         grid=(2, TILE_R // N),
-        in_specs=[spec(N, TILE_C), pl.BlockSpec((1, N, TILE_C), lambda c, b: (c, 0, 0)), spec(N, N), spec(ROWS // 2, H)],
+        in_specs=[spec(N, TILE_C), pl.BlockSpec((1, N, TILE_C), lambda c, b: (c, 0, 0)), spec(N, N), spec(ROWS // 4, H)],
         out_specs=[spec(N, TILE_C), spec(2, N, N)],
         compiler_params=pltpu.CompilerParams(vmem_limit_bytes=VMEM_LIMIT),
-    )(main, down, right, probe)
+    )(main, down, right, probe.reshape(2, ROWS // 2, H))
 
 
 def on_device(specimen, probe, amplitude, offsets):
     n_ty, n_tx = lax.axis_size("ty"), lax.axis_size("tx")
     positions = offsets.shape[0] * n_ty * n_tx
-    everyone, lower, right, corner, arranged = gather(offsets.reshape(-1), specimen, probe, n_ty, n_tx)
-    slots, places = prepare(everyone, amplitude, n_ty)
-    slots, places = lax.optimization_barrier((slots, places))
+    everyone, lower, right, corner, arranged, sorted_amp = gather(offsets.reshape(-1), specimen, probe, amplitude, n_ty, n_tx)
+    slots = prepare(everyone, sorted_amp, n_ty)
     arrived = lax.all_to_all(slots, "ty", split_axis=0, concat_axis=0, tiled=True)
     tables = make_tables()
-    far, pat, inten = forward(places, specimen, right, lower, corner, arranged, tables, n_ty)
+    far, pat, inten, places = forward(everyone, specimen, right, lower, corner, arranged, tables, n_ty)
     main, down, rt, cn, total = backward(places, arranged, tables, arrived, far, pat, inten, n_ty)
     scale = float(probe.shape[1] / np.sqrt(positions))
     probe_grad, down, rt = finish(total, down, rt, cn, scale, n_ty, n_tx)

time: 228 us -> 270 us (1.18)
  Pallas kernels: 194 us -> 244 us
  waiting for transfers between devices: 24 us -> 17.5 us
    pallas_call x1, Pallas kernels: 6.08 us -> 50.6 us  [prepare(): pl.pallas_call(prep_kernel, out_shape=jax.ShapeDtypeStruct((sources, 2, N...]
    pallas_call x1, Pallas kernels: 71 us -> 62.5 us  [finish(): pl.pallas_call(functools.partial(finish_kernel, n_ty, n_tx, scale), out_s...]
    pallas_call x1, Pallas kernels: 40.2 us -> 47.7 us  [backward(): pl.pallas_call(backward_kernel, out_shape=[like((2, 512, 1024), f32), lik...]
    all_to_all x1, waiting for transfers between devices: 24 us -> 17.5 us  [on_device(): lax.all_to_all(slots, 'ty', split_axis=0, concat_axis=0, tiled=True)]
    pallas_call x1, Pallas kernels: 36.2 us -> 42.6 us  [forward(): pl.pallas_call(forward_kernel, out_shape=[like((sources, 2, 4, 2, 2, 128,...]
where the time goes in v6:
time: 270 us
  Pallas kernels  244 us (90%)
  waiting for transfers between devices  17.5 us (6%)
  starting transfers between devices  6.02 us (2%)
    pallas_call x1, Pallas kernels, finish(): pl.pallas_call(functools.partial(finish_kernel, n_ty, n_tx, scale), out_s...  62.5 us
    pallas_call x1, Pallas kernels, prepare(): pl.pallas_call(prep_kernel, out_shape=jax.ShapeDtypeStruct((sources, 2, N...  50.6 us
    pallas_call x1, Pallas kernels, backward(): pl.pallas_call(backward_kernel, out_shape=[like((2, 512, 1024), f32), lik...  47.7 us
    pallas_call x1, Pallas kernels, forward(): pl.pallas_call(forward_kernel, out_shape=[like((sources, 2, 4, 2, 2, 128,...  42.6 us
    pallas_call x1, Pallas kernels, gather(): pl.pallas_call(functools.partial(gather_kernel, n_ty, n_tx), out_shape=[l...  34.8 us
    all_to_all x1, waiting for transfers between devices, on_device(): lax.all_to_all(slots, 'ty', split_axis=0, concat_axis=0, tiled=True)  17.5 us
    pallas_call x1, Pallas kernels, close(): pl.pallas_call(close_kernel, out_shape=[like(main.shape, f32), like((2, 4...  6.09 us
    all_to_all x1, starting transfers between devices, on_device(): lax.all_to_all(slots, 'ty', split_axis=0, concat_axis=0, tiled=True)  6.02 us
  transfers between devices with their start and end apart: 1, of which 1 were waited for; matrix products, arithmetic and copies ran while one was open for 0% of the time, Pallas kernels for 16%

profile of v6, /device:TPU:1, one launch (start us, length us, event | category | flops | bytes accessed | tf_op | source)
XLA Modules:
  0.0 269.9 jit_solution(13546027483114133171)
XLA Ops:
  0.6 0.8 copy.9
  1.4 0.1 reshape_reshape.3
  1.5 0.6 pad.4.own
  2.1 34.8 %shard_map.77 = (s32[16,8,128]{2,1,0:T(8,128)}, bf16[2,256,1024]{2,1,0:T(8,128)(2,1)}, bf16[2,512,256]{2,1,0:T(8,128)(2,1)}, bf16[2,256,256]{2,1,0:T(8,128)(2,1)...) custom-call(s32[8,128]{1,0:T(8,128)} %pad.4.own, f32[2,512,1024]{2,1,0:T(8,128)} %spec.3, ...), custom_call_target="tpu_custom_call" | custom-call | tf_op jit(solution)/shard_map/pallas_call | solution.py:430
  36.9 50.6 %shard_map.79 = bf16[16,2,256,256]{3,2,1,0:T(8,128)(2,1)} custom-call(s32[16,8,128]{2,1,0:T(8,128)} %get-tuple-element.20.off, bf16[12,256,256]{2,1,0:T(8,128)(2,1)} %get-tuple-element.26.amp), custom_call_target="tpu_custom_call" | custom-call | tf_op jit(solution)/shard_map/pallas_call | solution.py:82
  87.5 6.0 %all-to-all-start = ((bf16[16,2,256,256]{3,2,1,0:T(8,128)(2,1)}), bf16[16,2,256,256]{3,2,1,0:T(8,128)(2,1)}, u32[]{:S(2)}, u32[]{:S(2)}) async-start(bf16[16,2,256,256]{3,2,1,0:T(8,128)(2,1)} %shard_map.79), calls=%async_computation | async-start | bytes 8388608 | tf_op jit(solution)/shard_map/all_to_all | solution.py:612
  93.6 42.6 %shard_map.78 = (f32[16,2,4,2,2,128,256]{6,5,4,3,2,1,0:T(8,128)}, f32[16,2,2,256,256]{4,3,2,1,0:T(8,128)}, f32[16,2,2,128,256]{4,3,2,1,0:T(8,128)}, s32[64]{0:T(128)}) custom-call(s32[16,8,128]{2,1,0:T(8,128)} %get-tuple-element.20.off, f32[2,512,1024]{2,1,0:T(8,128)} %spec.3, bf16[2,512,256]{2,1,0:T(8,128)(2,1)} %get-tuple-element.21.right, ...), custom_call_target="tpu_custom_call" | custom-call | flops 17179869184 | bytes 104857600 | tf_op jit(solution)/shard_map/pallas_call | solution.py:319
  136.2 17.5 %all-to-all-done.amp = bf16[16,2,256,256]{3,2,1,0:T(8,128)(2,1)} async-done(((bf16[16,2,256,256]{3,2,1,0:T(8,128)(2,1)}), bf16[16,2,256,256]{3,2,1,0:T(8,128)(2,1)}, u32[]{:S(2)}, u32[]{:S(2)}) %all-to-all-start) | async-done | bytes 4194336 | tf_op jit(solution)/shard_map/all_to_all | solution.py:612
  153.7 47.7 %shard_map.80 = (f32[2,512,1024]{2,1,0:T(8,128)}, bf16[2,256,1024]{2,1,0:T(8,128)(2,1)}, bf16[2,512,256]{2,1,0:T(8,128)(2,1)}, bf16[2,256,256]{2,1,0:T(8,128)(2,1)}, f32[2,4,2,256,128]{4,3,2,1,0:T(8,128)}) custom-call(s32[64]{0:T(128)} %get-tuple-element.25.off, f32[2,4,256,256]{3,2,1,0:T(8,128)} %get-tuple-element.24.probe, ...), custom_call_target="tpu_custom_call" | custom-call | flops 17179869184 | bytes 104857600 | tf_op jit(solution)/shard_map/pallas_call | solution.py:334
  201.3 62.5 %shard_map.81 = (bf16[4096,128]{1,0:T(8,128)(2,1)}, bf16[2,256,1024]{2,1,0:T(8,128)(2,1)}, bf16[2,512,256]{2,1,0:T(8,128)(2,1)}) custom-call(f32[4096,128]{1,0:T(8,128)} %bitcast.2, bf16[2,256,1024]{2,1,0:T(8,128)(2,1)} %get-tuple-element.32.down, bf16[2,512,256]{2,1,0:T(8,128)(2,1)} %get-tuple-element.33.right, bf16[2,256,256]{2,1,0:T(8,128)(2,1)} %get-tuple-element.34.corner), custom_call_target="tpu_custom_call" | custom-call | tf_op jit(solution)/shard_map/pallas_call | solution.py:559
  263.8 6.1 %shard_map.82 = (f32[2,512,1024]{2,1,0:T(8,128)}, f32[2,4,256,256]{3,2,1,0:T(8,128)}) custom-call(f32[2,512,1024]{2,1,0:T(8,128)} %get-tuple-element.30.main, bf16[2,256,1024]{2,1,0:T(8,128)(2,1)} %get-tuple-element.35.down, bf16[2,512,256]{2,1,0:T(8,128)(2,1)} %get-tuple-element.36.right, bf16[2,2048,128]{2,1,0:T(8,128)(2,1)} %bitcast.3), custom_call_target="tpu_custom_call" | custom-call | tf_op jit(solution)/shard_map/pallas_call | solution.py:597
Async XLA Ops:
  87.5 66.2 %all-to-all-start = ((bf16[16,2,256,256]{3,2,1,0:T(8,128)(2,1)}), bf16[16,2,256,256]{3,2,1,0:T(8,128)(2,1)}, u32[]{:S(2)}, u32[]{:S(2)}) async-start(bf16[16,2,256,256]{3,2,1,0:T(8,128)(2,1)} %shard_map.79), calls=%async_computation | async-start | bytes 8388608 | tf_op jit(solution)/shard_map/all_to_all | solution.py:612

commit v7 on v6

--- a/solution.py
+++ b/solution.py
@@ -82,9 +82,10 @@
     return pl.pallas_call(
         prep_kernel,
         out_shape=jax.ShapeDtypeStruct((sources, 2, N, N), bf),
-        in_specs=[pl.BlockSpec(memory_space=pltpu.SMEM), hbm],
+        in_specs=[pl.BlockSpec(memory_space=pltpu.SMEM), pl.BlockSpec(memory_space=pltpu.VMEM)],
         out_specs=hbm,
         scratch_shapes=[pltpu.SemaphoreType.DMA((POS,))],
+        compiler_params=pltpu.CompilerParams(vmem_limit_bytes=VMEM_LIMIT),
     )(everyone, amplitude)
 
 

time: 270 us -> 224 us (0.83)
  Pallas kernels: 244 us -> 197 us
    pallas_call x1, Pallas kernels: 50.6 us -> 2.99 us  [prepare(): pl.pallas_call(prep_kernel, out_shape=jax.ShapeDtypeStruct((sources, 2, N...]
  transfers between devices with their start and end apart: 1 -> 1, of which waited for: 1 -> 1; matrix products, arithmetic and copies ran while one was open for 0% -> 0% of each run, Pallas kernels for 16% -> 19%
where the time goes in v7:
time: 224 us
  Pallas kernels  197 us (88%)
  waiting for transfers between devices  18.4 us (8%)
  starting transfers between devices  6.02 us (3%)
    pallas_call x1, Pallas kernels, finish(): pl.pallas_call(functools.partial(finish_kernel, n_ty, n_tx, scale), out_s...  64 us
    pallas_call x1, Pallas kernels, backward(): pl.pallas_call(backward_kernel, out_shape=[like((2, 512, 1024), f32), lik...  47.4 us
    pallas_call x1, Pallas kernels, forward(): pl.pallas_call(forward_kernel, out_shape=[like((sources, 2, 4, 2, 2, 128,...  41.7 us
    pallas_call x1, Pallas kernels, gather(): pl.pallas_call(functools.partial(gather_kernel, n_ty, n_tx), out_shape=[l...  34.8 us
    all_to_all x1, waiting for transfers between devices, on_device(): lax.all_to_all(slots, 'ty', split_axis=0, concat_axis=0, tiled=True)  18.4 us
    pallas_call x1, Pallas kernels, close(): pl.pallas_call(close_kernel, out_shape=[like(main.shape, f32), like((2, 4...  6.09 us
    all_to_all x1, starting transfers between devices, on_device(): lax.all_to_all(slots, 'ty', split_axis=0, concat_axis=0, tiled=True)  6.02 us
  transfers between devices with their start and end apart: 1, of which 1 were waited for; matrix products, arithmetic and copies ran while one was open for 0% of the time, Pallas kernels for 19%

profile of v7, /device:TPU:1, one launch (start us, length us, event | category | flops | bytes accessed | tf_op | source)
XLA Modules:
  0.0 223.6 jit_solution(4320919587257248106)
XLA Ops:
  0.6 0.8 copy.9
  1.4 0.1 reshape_reshape.3
  1.5 0.6 pad.4.own
  2.1 34.8 %shard_map.77 = (s32[16,8,128]{2,1,0:T(8,128)}, bf16[2,256,1024]{2,1,0:T(8,128)(2,1)}, bf16[2,512,256]{2,1,0:T(8,128)(2,1)}, bf16[2,256,256]{2,1,0:T(8,128)(2,1)...) custom-call(s32[8,128]{1,0:T(8,128)} %pad.4.own, f32[2,512,1024]{2,1,0:T(8,128)} %spec.3, ...), custom_call_target="tpu_custom_call" | custom-call | tf_op jit(solution)/shard_map/pallas_call | solution.py:431
  36.9 3.0 %shard_map.79 = bf16[16,2,256,256]{3,2,1,0:T(8,128)(2,1)} custom-call(s32[16,8,128]{2,1,0:T(8,128)} %get-tuple-element.20.off, bf16[12,256,256]{2,1,0:T(8,128)(2,1)} %get-tuple-element.26.amp), custom_call_target="tpu_custom_call" | custom-call | tf_op jit(solution)/shard_map/pallas_call | solution.py:82
  39.9 6.0 %all-to-all-start = ((bf16[16,2,256,256]{3,2,1,0:T(8,128)(2,1)}), bf16[16,2,256,256]{3,2,1,0:T(8,128)(2,1)}, u32[]{:S(2)}, u32[]{:S(2)}) async-start(bf16[16,2,256,256]{3,2,1,0:T(8,128)(2,1)} %shard_map.79), calls=%async_computation | async-start | bytes 8388608 | tf_op jit(solution)/shard_map/all_to_all | solution.py:613
  45.9 41.7 %shard_map.78 = (f32[16,2,4,2,2,128,256]{6,5,4,3,2,1,0:T(8,128)}, f32[16,2,2,256,256]{4,3,2,1,0:T(8,128)}, f32[16,2,2,128,256]{4,3,2,1,0:T(8,128)}, s32[64]{0:T(128)}) custom-call(s32[16,8,128]{2,1,0:T(8,128)} %get-tuple-element.20.off, f32[2,512,1024]{2,1,0:T(8,128)} %spec.3, bf16[2,512,256]{2,1,0:T(8,128)(2,1)} %get-tuple-element.21.right, ...), custom_call_target="tpu_custom_call" | custom-call | flops 17179869184 | bytes 104857600 | tf_op jit(solution)/shard_map/pallas_call | solution.py:320
  87.6 18.4 %all-to-all-done.amp = bf16[16,2,256,256]{3,2,1,0:T(8,128)(2,1)} async-done(((bf16[16,2,256,256]{3,2,1,0:T(8,128)(2,1)}), bf16[16,2,256,256]{3,2,1,0:T(8,128)(2,1)}, u32[]{:S(2)}, u32[]{:S(2)}) %all-to-all-start) | async-done | bytes 4194336 | tf_op jit(solution)/shard_map/all_to_all | solution.py:613
  106.1 47.4 %shard_map.80 = (f32[2,512,1024]{2,1,0:T(8,128)}, bf16[2,256,1024]{2,1,0:T(8,128)(2,1)}, bf16[2,512,256]{2,1,0:T(8,128)(2,1)}, bf16[2,256,256]{2,1,0:T(8,128)(2,1)}, f32[2,4,2,256,128]{4,3,2,1,0:T(8,128)}) custom-call(s32[64]{0:T(128)} %get-tuple-element.25.off, f32[2,4,256,256]{3,2,1,0:T(8,128)} %get-tuple-element.24.probe, ...), custom_call_target="tpu_custom_call" | custom-call | flops 17179869184 | bytes 104857600 | tf_op jit(solution)/shard_map/pallas_call | solution.py:335
  153.5 64.0 %shard_map.81 = (bf16[4096,128]{1,0:T(8,128)(2,1)}, bf16[2,256,1024]{2,1,0:T(8,128)(2,1)}, bf16[2,512,256]{2,1,0:T(8,128)(2,1)}) custom-call(f32[4096,128]{1,0:T(8,128)} %bitcast.2, bf16[2,256,1024]{2,1,0:T(8,128)(2,1)} %get-tuple-element.32.down, bf16[2,512,256]{2,1,0:T(8,128)(2,1)} %get-tuple-element.33.right, bf16[2,256,256]{2,1,0:T(8,128)(2,1)} %get-tuple-element.34.corner), custom_call_target="tpu_custom_call" | custom-call | tf_op jit(solution)/shard_map/pallas_call | solution.py:560
  217.5 6.1 %shard_map.82 = (f32[2,512,1024]{2,1,0:T(8,128)}, f32[2,4,256,256]{3,2,1,0:T(8,128)}) custom-call(f32[2,512,1024]{2,1,0:T(8,128)} %get-tuple-element.30.main, bf16[2,256,1024]{2,1,0:T(8,128)(2,1)} %get-tuple-element.35.down, bf16[2,512,256]{2,1,0:T(8,128)(2,1)} %get-tuple-element.36.right, bf16[2,2048,128]{2,1,0:T(8,128)(2,1)} %bitcast.3), custom_call_target="tpu_custom_call" | custom-call | tf_op jit(solution)/shard_map/pallas_call | solution.py:598
Async XLA Ops:
  39.9 66.2 %all-to-all-start = ((bf16[16,2,256,256]{3,2,1,0:T(8,128)(2,1)}), bf16[16,2,256,256]{3,2,1,0:T(8,128)(2,1)}, u32[]{:S(2)}, u32[]{:S(2)}) async-start(bf16[16,2,256,256]{3,2,1,0:T(8,128)(2,1)} %shard_map.79), calls=%async_computation | async-start | bytes 8388608 | tf_op jit(solution)/shard_map/all_to_all | solution.py:613

commit v8 on v7

--- a/solution.py
+++ b/solution.py
@@ -18,7 +18,7 @@
 POS = 12
 VMEM_LIMIT = 60 * 2**20
 ROWS = 4096
-ROWS_X = 3072
+ROWS_X = 2048
 PIECES = 4
 MESH = pl.DeviceIdType.MESH
 S = 2
@@ -356,8 +356,8 @@
     return (place["ty"], place["tx"])
 
 
-def gather_kernel(n_ty, n_tx, own, spec, probe, amp, perm, out, lower_o, right_o, corner_o, probe_o, amp_o,
-                  top, side, half_top, half_side, split, raw, send, recv, send_h, recv_h, sem):
+def gather_kernel(n_ty, n_tx, own, spec, probe_in, amp, perm, out, lower_o, right_o, corner_o, probe_o, amp_o,
+                  top, side, half_top, half_side, probe, split, raw, send, recv, send_h, recv_h, sem):
     ty, tx = lax.axis_index("ty"), lax.axis_index("tx")
     above, left = lax.rem(ty + n_ty - 1, n_ty), lax.rem(tx + n_tx - 1, n_tx)
     barrier = pltpu.get_barrier_semaphore()
@@ -373,6 +373,8 @@
     load_side.start()
     load_raw = pltpu.make_async_copy(amp, raw, sem.at[2])
     load_raw.start()
+    load_probe = pltpu.make_async_copy(probe_in, probe, sem.at[3])
+    load_probe.start()
     pl.semaphore_wait(barrier, n_ty)
 
     def copy(d):
@@ -400,6 +402,7 @@
     first.wait()
     corner = halo(3, lower_o.at[:, :, 0:N], corner_o, (ty, left))
     corner.start()
+    load_probe.wait()
     for c in (0, 1):
         for t in (0, 1):
             split[c, :, t] = probe[c, :, :, t * H:t * H + H]
@@ -432,18 +435,18 @@
         functools.partial(gather_kernel, n_ty, n_tx),
         out_shape=[like((n_ty, 8, 128), jnp.int32), like((2, N, TILE_C), bf), like((2, TILE_R, N), bf), like((2, N, N), bf),
                    like(probe.shape, f32), like(amplitude.shape, bf)],
-        in_specs=[vmem, hbm, vmem, hbm, vmem],
+        in_specs=[vmem, hbm, hbm, hbm, vmem],
         out_specs=[vmem, hbm, hbm, hbm, vmem, vmem],
         scratch_shapes=[
             pltpu.VMEM((2, N, TILE_C), f32), pltpu.VMEM((2, TILE_R, N), f32),
-            pltpu.VMEM((2, N, TILE_C), bf), pltpu.VMEM((2, TILE_R, N), bf), pltpu.VMEM((2, 4, 2, N, H), f32),
-            pltpu.VMEM(amplitude.shape, f32), dma((n_ty,)), dma((n_ty,)), dma((4,)), dma((4,)), dma((3,))],
+            pltpu.VMEM((2, N, TILE_C), bf), pltpu.VMEM((2, TILE_R, N), bf), pltpu.VMEM(probe.shape, f32), pltpu.VMEM((2, 4, 2, N, H), f32),
+            pltpu.VMEM(amplitude.shape, f32), dma((n_ty,)), dma((n_ty,)), dma((4,)), dma((4,)), dma((4,))],
         compiler_params=pltpu.CompilerParams(collective_id=0, has_side_effects=True, vmem_limit_bytes=VMEM_LIMIT),
     )(own, specimen, probe, amplitude, parity_matrix())
 
 
-def finish_kernel(n_ty, n_tx, scale, total, down, right, corner, probe_o, down_o, right_o,
-                  cast, rax, ray, sx, sy, rbx, rby, gx, gy, hx, hy, arrived, edge, send_ty, recv_ty, send_tx, recv_tx, send_h, recv_h, sem):
+def finish_kernel(n_ty, n_tx, scale, total_in, down, right, corner, probe_o, down_o, right_o,
+                  total, cast, rax, ray, sx, sy, rbx, rby, gx, gy, arrived, edge, send_ty, recv_ty, send_tx, recv_tx, send_h, recv_h, sem):
     ty, tx = lax.axis_index("ty"), lax.axis_index("tx")
     nx, ny = ROWS_X // n_tx, (ROWS - ROWS_X) // n_ty
     ux, uy = nx // n_ty, ny // n_tx
@@ -454,8 +457,11 @@
 
     spread("ty", n_ty, lambda d: greet(beyond("ty", d, n_ty)))
     spread("tx", n_tx, lambda d: greet(beyond("tx", d, n_tx)))
-    load = pltpu.make_async_copy(down.at[:, :, 0:N], edge, sem)
+    load_total = pltpu.make_async_copy(total_in, total, sem.at[0])
+    load_total.start()
+    load = pltpu.make_async_copy(down.at[:, :, 0:N], edge, sem.at[1])
     load.start()
+    load_total.wait()
     cast[...] = total[...].astype(bf)
     load.wait()
     pl.semaphore_wait(barrier, n_ty + n_tx - 2)
@@ -471,7 +477,7 @@
             device_id=beyond("tx", d, n_tx), device_id_type=MESH)
 
     def rows(k, n, first=0):
-        return pl.ds(pl.multiple_of(first + k * n, 8), n)
+        return pl.ds(pl.multiple_of(first + k * n, 16), n)
 
     def halo(k, src, dst, device):
         return pltpu.make_async_remote_copy(
@@ -514,14 +520,14 @@
     spread("tx", n_tx, lambda d: by(d).start())
     pieces[3].start()
     spread("ty", n_ty, lambda d: bx(d).wait())
-    gx[rows(ty, ux)] = scale * lax.fori_loop(1, n_ty, lambda d, t: t + rbx[d], sx[rows(ty, ux)])
+    gx[rows(ty, ux)] = (scale * lax.fori_loop(1, n_ty, lambda d, t: t + rbx[d], sx[rows(ty, ux)])).astype(bf)
 
     def cx(d):
         return over_ty(2, d, gx.at[rows(ty, ux)], gx.at[rows(ty, ux)])
 
     spread("ty", n_ty, lambda d: cx(d).start())
     spread("tx", n_tx, lambda d: by(d).wait())
-    gy[rows(tx, uy)] = scale * lax.fori_loop(1, n_tx, lambda d, t: t + rby[d], sy[rows(tx, uy)])
+    gy[rows(tx, uy)] = (scale * lax.fori_loop(1, n_tx, lambda d, t: t + rby[d], sy[rows(tx, uy)])).astype(bf)
 
     def cy(d):
         return over_tx(2, d, gy.at[rows(tx, uy)], gy.at[rows(tx, uy)])
@@ -531,21 +537,19 @@
     edge[...] = (edge[...].astype(f32) + arrived[...].astype(f32)).astype(bf)
     pieces[0].start()
     spread("ty", n_ty, lambda d: cx(d).wait())
-    hx[...] = gx[...].astype(bf)
 
     def dx(d):
-        return over_tx(3, d, hx, probe_o.at[rows(tx, nx)])
+        return over_tx(3, d, gx, probe_o.at[rows(tx, nx)])
 
     spread("tx", n_tx, lambda d: dx(d).start())
-    probe_o[rows(tx, nx)] = hx[...]
+    probe_o[rows(tx, nx)] = gx[...]
     spread("tx", n_tx, lambda d: cy(d).wait())
-    hy[...] = gy[...].astype(bf)
 
     def dy(d):
-        return over_ty(3, d, hy, probe_o.at[rows(ty, ny, ROWS_X)])
+        return over_ty(3, d, gy, probe_o.at[rows(ty, ny, ROWS_X)])
 
     spread("ty", n_ty, lambda d: dy(d).start())
-    probe_o[rows(ty, ny, ROWS_X)] = hy[...]
+    probe_o[rows(ty, ny, ROWS_X)] = gy[...]
     spread("tx", n_tx, lambda d: dx(d).wait())
     spread("ty", n_ty, lambda d: dy(d).wait())
     for h in (side, *pieces):
@@ -560,14 +564,14 @@
     return pl.pallas_call(
         functools.partial(finish_kernel, n_ty, n_tx, scale),
         out_shape=[like((ROWS, H), bf), like(down.shape, bf), like(right.shape, bf)],
-        in_specs=[vmem, hbm, hbm, hbm],
+        in_specs=[hbm, hbm, hbm, hbm],
         out_specs=[vmem, hbm, hbm],
         scratch_shapes=[
-            pltpu.VMEM((ROWS, H), bf), pltpu.VMEM((n_tx, nx, H), bf), pltpu.VMEM((n_ty, ny, H), bf),
+            pltpu.VMEM((ROWS, H), f32), pltpu.VMEM((ROWS, H), bf), pltpu.VMEM((n_tx, nx, H), bf), pltpu.VMEM((n_ty, ny, H), bf),
             pltpu.VMEM((nx, H), f32), pltpu.VMEM((ny, H), f32), pltpu.VMEM((n_ty, nx // n_ty, H), f32), pltpu.VMEM((n_tx, ny // n_tx, H), f32),
-            pltpu.VMEM((nx, H), f32), pltpu.VMEM((ny, H), f32), pltpu.VMEM((nx, H), bf), pltpu.VMEM((ny, H), bf),
+            pltpu.VMEM((nx, H), bf), pltpu.VMEM((ny, H), bf),
             pltpu.VMEM((2, N, N), bf), pltpu.VMEM((2, N, N), bf),
-            dma((4, n_ty)), dma((4, n_ty)), dma((4, n_tx)), dma((4, n_tx)), dma((PIECES + 2,)), dma((PIECES + 2,)), dma],
+            dma((4, n_ty)), dma((4, n_ty)), dma((4, n_tx)), dma((4, n_tx)), dma((PIECES + 2,)), dma((PIECES + 2,)), dma((2,))],
         compiler_params=pltpu.CompilerParams(collective_id=1, has_side_effects=True, vmem_limit_bytes=VMEM_LIMIT),
     )(total.reshape(ROWS, H), down, right, corner)
 

time: 224 us -> 222 us (level)
  Pallas kernels: 197 us -> 189 us
  waiting for transfers between devices: 18.4 us -> 22.4 us
    pallas_call x1, Pallas kernels: 47.4 us -> 39.5 us  [backward(): pl.pallas_call(backward_kernel, out_shape=[like((2, 512, 1024), f32), lik...]
    pallas_call x1, Pallas kernels: 64 us -> 68.5 us  [finish(): pl.pallas_call(functools.partial(finish_kernel, n_ty, n_tx, scale), out_s...]
    pallas_call x1, Pallas kernels: 41.7 us -> 37.7 us  [forward(): pl.pallas_call(forward_kernel, out_shape=[like((sources, 2, 4, 2, 2, 128,...]
    all_to_all x1, waiting for transfers between devices: 18.4 us -> 22.4 us  [on_device(): lax.all_to_all(slots, 'ty', split_axis=0, concat_axis=0, tiled=True)]
  transfers between devices with their start and end apart: 1 -> 1, of which waited for: 1 -> 1; matrix products, arithmetic and copies ran while one was open for 0% -> 0% of each run, Pallas kernels for 19% -> 17%
where the time goes in v8:
time: 222 us; the launch traced here: 219 us
  Pallas kernels  189 us (85%)
  waiting for transfers between devices  22.4 us (10%)
  starting transfers between devices  6.02 us (3%)
    pallas_call x1, Pallas kernels, finish(): pl.pallas_call(functools.partial(finish_kernel, n_ty, n_tx, scale), out_s...  68.5 us
    pallas_call x1, Pallas kernels, backward(): pl.pallas_call(backward_kernel, out_shape=[like((2, 512, 1024), f32), lik...  39.5 us
    pallas_call x1, Pallas kernels, forward(): pl.pallas_call(forward_kernel, out_shape=[like((sources, 2, 4, 2, 2, 128,...  37.7 us
    pallas_call x1, Pallas kernels, gather(): pl.pallas_call(functools.partial(gather_kernel, n_ty, n_tx), out_shape=[l...  34.2 us
    all_to_all x1, waiting for transfers between devices, on_device(): lax.all_to_all(slots, 'ty', split_axis=0, concat_axis=0, tiled=True)  22.4 us
    pallas_call x1, Pallas kernels, close(): pl.pallas_call(close_kernel, out_shape=[like(main.shape, f32), like((2, 4...  6.09 us
    all_to_all x1, starting transfers between devices, on_device(): lax.all_to_all(slots, 'ty', split_axis=0, concat_axis=0, tiled=True)  6.02 us
  transfers between devices with their start and end apart: 1, of which 1 were waited for; matrix products, arithmetic and copies ran while one was open for 0% of the time, Pallas kernels for 17%

profile of v8, /device:TPU:1, one launch (start us, length us, event | category | flops | bytes accessed | tf_op | source)
XLA Modules:
  0.0 219.5 jit_solution(3318106395403208970)
XLA Ops:
  0.6 0.8 copy.9
  1.4 0.1 reshape_reshape.3
  1.5 0.6 pad.4.own
  2.1 34.2 %shard_map.77 = (s32[16,8,128]{2,1,0:T(8,128)}, bf16[2,256,1024]{2,1,0:T(8,128)(2,1)}, bf16[2,512,256]{2,1,0:T(8,128)(2,1)}, bf16[2,256,256]{2,1,0:T(8,128)(2,1)...) custom-call(s32[8,128]{1,0:T(8,128)} %pad.4.own, f32[2,512,1024]{2,1,0:T(8,128)} %spec.3, ...), custom_call_target="tpu_custom_call" | custom-call | tf_op jit(solution)/shard_map/pallas_call | solution.py:434
  36.2 3.0 %shard_map.79 = bf16[16,2,256,256]{3,2,1,0:T(8,128)(2,1)} custom-call(s32[16,8,128]{2,1,0:T(8,128)} %get-tuple-element.20.off, bf16[12,256,256]{2,1,0:T(8,128)(2,1)} %get-tuple-element.26.amp), custom_call_target="tpu_custom_call" | custom-call | tf_op jit(solution)/shard_map/pallas_call | solution.py:82
  39.2 6.0 %all-to-all-start = ((bf16[16,2,256,256]{3,2,1,0:T(8,128)(2,1)}), bf16[16,2,256,256]{3,2,1,0:T(8,128)(2,1)}, u32[]{:S(2)}, u32[]{:S(2)}) async-start(bf16[16,2,256,256]{3,2,1,0:T(8,128)(2,1)} %shard_map.79), calls=%async_computation | async-start | bytes 8388608 | tf_op jit(solution)/shard_map/all_to_all | solution.py:617
  45.3 37.7 %shard_map.78 = (f32[16,2,4,2,2,128,256]{6,5,4,3,2,1,0:T(8,128)}, f32[16,2,2,256,256]{4,3,2,1,0:T(8,128)}, f32[16,2,2,128,256]{4,3,2,1,0:T(8,128)}, s32[64]{0:T(128)}) custom-call(s32[16,8,128]{2,1,0:T(8,128)} %get-tuple-element.20.off, f32[2,512,1024]{2,1,0:T(8,128)} %spec.3, bf16[2,512,256]{2,1,0:T(8,128)(2,1)} %get-tuple-element.21.right, ...), custom_call_target="tpu_custom_call" | custom-call | flops 17179869184 | bytes 104857600 | tf_op jit(solution)/shard_map/pallas_call | solution.py:320
  83.0 22.4 %all-to-all-done.amp = bf16[16,2,256,256]{3,2,1,0:T(8,128)(2,1)} async-done(((bf16[16,2,256,256]{3,2,1,0:T(8,128)(2,1)}), bf16[16,2,256,256]{3,2,1,0:T(8,128)(2,1)}, u32[]{:S(2)}, u32[]{:S(2)}) %all-to-all-start) | async-done | bytes 4194336 | tf_op jit(solution)/shard_map/all_to_all | solution.py:617
  105.4 39.5 %shard_map.80 = (f32[2,512,1024]{2,1,0:T(8,128)}, bf16[2,256,1024]{2,1,0:T(8,128)(2,1)}, bf16[2,512,256]{2,1,0:T(8,128)(2,1)}, bf16[2,256,256]{2,1,0:T(8,128)(2,1)}, f32[2,4,2,256,128]{4,3,2,1,0:T(8,128)}) custom-call(s32[64]{0:T(128)} %get-tuple-element.25.off, f32[2,4,256,256]{3,2,1,0:T(8,128)} %get-tuple-element.24.probe, ...), custom_call_target="tpu_custom_call" | custom-call | flops 17179869184 | bytes 104857600 | tf_op jit(solution)/shard_map/pallas_call | solution.py:335
  144.9 68.5 %shard_map.81 = (bf16[4096,128]{1,0:T(8,128)(2,1)}, bf16[2,256,1024]{2,1,0:T(8,128)(2,1)}, bf16[2,512,256]{2,1,0:T(8,128)(2,1)}) custom-call(f32[4096,128]{1,0:T(8,128)} %bitcast.2, bf16[2,256,1024]{2,1,0:T(8,128)(2,1)} %get-tuple-element.32.down, bf16[2,512,256]{2,1,0:T(8,128)(2,1)} %get-tuple-element.33.right, bf16[2,256,256]{2,1,0:T(8,128)(2,1)} %get-tuple-element.34.corner), custom_call_target="tpu_custom_call" | custom-call | tf_op jit(solution)/shard_map/pallas_call | solution.py:564
  213.4 6.1 %shard_map.82 = (f32[2,512,1024]{2,1,0:T(8,128)}, f32[2,4,256,256]{3,2,1,0:T(8,128)}) custom-call(f32[2,512,1024]{2,1,0:T(8,128)} %get-tuple-element.30.main, bf16[2,256,1024]{2,1,0:T(8,128)(2,1)} %get-tuple-element.35.down, bf16[2,512,256]{2,1,0:T(8,128)(2,1)} %get-tuple-element.36.right, bf16[2,2048,128]{2,1,0:T(8,128)(2,1)} %bitcast.3), custom_call_target="tpu_custom_call" | custom-call | tf_op jit(solution)/shard_map/pallas_call | solution.py:602
Async XLA Ops:
  39.2 66.2 %all-to-all-start = ((bf16[16,2,256,256]{3,2,1,0:T(8,128)(2,1)}), bf16[16,2,256,256]{3,2,1,0:T(8,128)(2,1)}, u32[]{:S(2)}, u32[]{:S(2)}) async-start(bf16[16,2,256,256]{3,2,1,0:T(8,128)(2,1)} %shard_map.79), calls=%async_computation | async-start | bytes 8388608 | tf_op jit(solution)/shard_map/all_to_all | solution.py:617
